TPU v7x, 256 devices: a whole 4x4x8 slice. The times are simulated.
256 devices in a mesh: seq: 32 (over y, x, core), head: 8 (over z).
Axes of the slice: x: 4, y: 4, z: 8, core: 2. Of those that a mesh axis runs over, the one named last changes fastest.
Arguments:
- queries: bfloat16 [16384, 4096], P('seq', 'head'), may hold values from -6 to 6
- keys: bfloat16 [16384, 4096], P('seq', 'head'), may hold values from -6 to 6
- values: bfloat16 [16384, 4096], P('seq', 'head'), may hold values from -6 to 6
- log_decay: float32 [32, 16384], P('head', 'seq'), may hold values from -1 to 0
- out_weight: bfloat16 [4096, 3072], P('head'), may hold values from -0.09375 to 0.09375
- grad_out: bfloat16 [16384, 3072], P('seq', 'head'), may hold values from -0.0625 to 0.0625
Outputs:
- grad_q: float32 [16384, 4096], P('seq', 'head')
- grad_k: float32 [16384, 4096], P('seq', 'head')
- grad_v: float32 [16384, 4096], P('seq', 'head')
All inputs are finite; a program needn't handle non-finite values.
Results may differ from a plain program's by a relative error of at most 0.003.
Values may be sent and summed in bfloat16 or wider, within the bound.
No kernel may reach another device: no remote copies, remote signals or barrier semaphores. Data moves between devices by JAX's collectives and lax.ppermute only.
A program may use at most 128 MiB of HBM per device.

v0:
```python
import jax
import jax.numpy as jnp
from jax import lax
from jax.sharding import PartitionSpec as P

DH = 128


def local_terms(queries, keys, values, grad_attn, log_decay):
    head_size = queries.shape[-1]
    running = jnp.cumsum(log_decay, axis=1)
    location_numbers = jnp.arange(running.shape[1])
    causal = location_numbers[:, None] >= location_numbers[None, :]
    decay_mask = (
        jnp.exp(jnp.where(causal[None], running[:, :, None] - running[:, None, :], -jnp.inf))
        / head_size
    )
    scores = (
        jnp.einsum("thd,shd->hts", queries, keys, preferred_element_type=jnp.float32) * decay_mask
    ).astype(jnp.bfloat16)
    grad_scores = (
        jnp.einsum("the,she->hts", grad_attn, values, preferred_element_type=jnp.float32)
        * decay_mask
    ).astype(jnp.bfloat16)
    query_gradient_local = jnp.einsum(
        "hts,shd->thd", grad_scores, keys, preferred_element_type=jnp.float32
    )
    dk_local = jnp.einsum("hts,thd->shd", grad_scores, queries, preferred_element_type=jnp.float32)
    dv_local = jnp.einsum("hts,the->she", scores, grad_attn, preferred_element_type=jnp.float32)
    to_end = jnp.exp(running[:, -1:] - running)
    from_start = jnp.exp(running)
    key_state = jnp.einsum(
        "thd,the->hde",
        keys.astype(jnp.float32) * to_end.T[:, :, None],
        values.astype(jnp.float32),
        precision=lax.Precision.HIGHEST,
    )
    grad_state = jnp.einsum(
        "thd,the->hde",
        queries.astype(jnp.float32) * from_start.T[:, :, None],
        grad_attn.astype(jnp.float32),
        precision=lax.Precision.HIGHEST,
    )
    return (
        (query_gradient_local, dk_local, dv_local, to_end, from_start),
        key_state,
        grad_state,
        running[:, -1],
    )


def finish(queries, keys, values, grad_attn, parts, state_in, state_out):
    query_gradient_local, dk_local, dv_local, to_end, from_start = parts
    head_size = state_in.shape[-1]
    start_w = (from_start.T / head_size)[:, :, None]
    end_w = (to_end.T / head_size)[:, :, None]
    high = lax.Precision.HIGHEST
    grad_q = query_gradient_local + start_w * jnp.einsum(
        "the,hde->thd", grad_attn.astype(jnp.float32), state_in, precision=high
    )
    grad_k = dk_local + end_w * jnp.einsum(
        "the,hde->thd", values.astype(jnp.float32), state_out, precision=high
    )
    grad_v = dv_local + end_w * jnp.einsum(
        "thd,hde->the", keys.astype(jnp.float32), state_out, precision=high
    )
    return (grad_q, grad_k, grad_v)


def local(queries, keys, values, log_decay, out_weight, grad_out):
    tok_rows = queries.shape[0]
    head_count = log_decay.shape[0]
    cotangent = lax.all_gather(grad_out, "head", axis=1, tiled=True)
    grad_attn = lax.dot_general(
        cotangent, out_weight, (((1,), (1,)), ((), ())), preferred_element_type=jnp.float32
    ).astype(jnp.bfloat16)

    def heads_view(array):
        return array.reshape(tok_rows, head_count, DH)

    inputs = (heads_view(queries), heads_view(keys), heads_view(values), heads_view(grad_attn))
    parts, key_state, grad_state, total = local_terms(*inputs, log_decay)
    all_keys, all_grads, all_totals = (
        lax.all_gather(key_state[None], "seq", axis=0, tiled=True),
        lax.all_gather(grad_state[None], "seq", axis=0, tiled=True),
        lax.all_gather(total[None], "seq", axis=0, tiled=True),
    )
    device = lax.axis_index("seq")
    order = jnp.arange(all_totals.shape[0])
    upto = jnp.cumsum(all_totals, axis=0)
    before = jnp.concatenate([jnp.zeros_like(upto[:1]), upto[:-1]], axis=0)
    mine_before = before[device]
    mine_upto = upto[device]
    fwd_weight = jnp.exp(jnp.where((order < device)[:, None], mine_before[None] - upto, -jnp.inf))
    bwd_weight = jnp.exp(jnp.where((order > device)[:, None], before - mine_upto[None], -jnp.inf))
    state_in = jnp.einsum("mh,mhde->hde", fwd_weight, all_keys, precision=lax.Precision.HIGHEST)
    state_out = jnp.einsum("mh,mhde->hde", bwd_weight, all_grads, precision=lax.Precision.HIGHEST)
    grad_q, grad_k, grad_v = finish(*inputs, parts, state_in, state_out)
    width = head_count * DH
    return (
        grad_q.reshape(tok_rows, width),
        grad_k.reshape(tok_rows, width),
        grad_v.reshape(tok_rows, width),
    )


def solution(mesh):
    return jax.shard_map(
        local,
        mesh=mesh,
        in_specs=(
            P("seq", "head"),
            P("seq", "head"),
            P("seq", "head"),
            P("head", "seq"),
            P("head", None),
            P("seq", "head"),
        ),
        out_specs=(P("seq", "head"), P("seq", "head"), P("seq", "head")),
        check_vma=False,
    )
```

profile of v0, /device:TPU:1, one launch (start us, length us, event | category | flops | bytes accessed | tf_op | source)
XLA Modules:
  0.0 199.2 jit_solution(3255864303995326208)
XLA Ops:
  7.2 0.7 all-gather.7.cloned.1.call-update
  8.0 0.9 reshape.87
  8.8 1.2 reduce-window.6
  10.0 0.2 slice_reduce_fusion
  10.2 0.2 reduce-window.9
  10.5 0.1 copy.72
  10.6 2.1 %copy.74 = bf16[512,512]{0,1:T(8,128)(2,1)} copy(bf16[512,512]{1,0:T(8,128)(2,1)} %param.7) | data formatting | bytes 1048576 | tf_op jit(solution)/shard_map/reshape | solution.py:79
  12.8 2.6 %fusion.13 = f32[4,128,128]{2,1,0:T(8,128)} fusion(bf16[512,4,128]{0,2,1:T(8,128)(2,1)} %bitcast.107, f32[512,4]{0,1:T(4,128)S(1)} %get-tuple-element.13, bf16[512,512]{1,0:T(8,128)(2,1)} %param.8), kind=kOutput, calls=%fused_computation.23 | convolution fusion | flops 403177472 | bytes 1318912 | tf_op jit(solution)/shard_map/thd,the->hde/dot_general | solution.py:32
  15.4 2.1 %copy.75 = bf16[512,512]{0,1:T(8,128)(2,1)} copy(bf16[512,512]{1,0:T(8,128)(2,1)} %param.6) | data formatting | bytes 1048576 | tf_op jit(solution)/shard_map/reshape | solution.py:79
  17.5 40.3 %all-gather.7.cloned.1.call-done = bf16[512,3072]{1,0:T(8,128)(2,1)} async-done(((bf16[512,384]{1,0:T(8,128)(2,1)}), bf16[512,3072]{1,0:T(8,128)(2,1)}) %all-gather.7.cloned.1.call-update) | async-done | bytes 3145744 | tf_op jit(solution)/shard_map/all_gather | solution.py:73
  57.8 3.8 %convolution_convert_fusion = bf16[512,512]{0,1:T(8,128)(2,1)S(1)} fusion(bf16[512,3072]{1,0:T(8,128)(2,1)} %all-gather.7.cloned.1.call-done, bf16[512,3072]{1,0:T(8,128)(2,1)S(1)} %copy-done), kind=kOutput, calls=%fused_computation.19 | convolution fusion | flops 1610874880 | bytes 6815744 | tf_op jit(solution)/shard_map/dot_general | solution.py:74
  61.6 0.8 copy-done.6
  62.4 1.4 fusion.10
  63.8 0.6 dynamic-slice
  65.0 0.1 bitcast_dynamic-update-slice_fusion
  65.1 64.8 %all-reduce.1 = f32[128]{0:T(128)S(1)} all-reduce(f32[128]{0:T(128)S(1)} %bitcast_dynamic-update-slice_fusion), channel_id=2, replica_groups=mesh['seq'=32,'head'=8] {'seq'}, use_global_device_ids=true, to_apply=%add.1 | all-reduce | flops 128 | bytes 1024
  129.9 0.1 reshape.94
  130.3 0.1 iota_compare_fusion
  130.3 0.1 exponential_bitcast_fusion
  130.4 2.7 %multiply_convert_fusion.1 = bf16[4,512,512]{2,1,0:T(8,128)(2,1)S(1)} fusion(bf16[512,4,128]{0,2,1:T(8,128)(2,1)} %bitcast.115, f32[4,512]{1,0:T(4,128)S(1)} %bitcast.122, pred[512,512]{1,0:T(8,128)(4,1)S(1)} %iota_compare_fusion, bf16[512,512]{1,0:T(8,128)(2,1)} %param.8), kind=kOutput, calls=%fused_computation.4 | convolution fusion | flops 273678336 | bytes 3416064 | tf_op jit(solution)/shard_map/the,she->hts/dot_general | solution.py:22
  133.2 1.4 convolution_bitcast_fusion
  134.6 1.8 convolution_bitcast_fusion.1
  136.4 4.1 %fusion.3 = f32[512,4,128]{0,2,1:T(8,128)} fusion(bf16[512,4,128]{0,2,1:T(8,128)(2,1)} %bitcast.116, bf16[512,4,128]{0,2,1:T(8,128)(2,1)} %bitcast.104, bf16[512,4,128]{0,2,1:T(8,128)(2,1)} %bitcast.108, f32[4,512]{1,0:T(4,128)S(1)} %bitcast.123, pred[512,512]{1,0:T(8,128)(4,1)S(1)} %iota_compare_fusion), kind=kOutput, calls=%fused_computation.9 | convolution fusion | flops 542113792 | bytes 2891776 | tf_op jit(solution)/shard_map/hts,the->she/dot_general | solution.py:29
  140.5 12.4 %fusion = f32[4,1,128,128]{3,1,2,0:T(1,128)S(1)} fusion(f32[32,4,1,1]{0,2,3,1:T(1,128)S(1)} %copy.60, f32[32,4,128,128]{3,2,1,0:T(8,128)} %bitcast.102), kind=kOutput, calls=%fused_computation.1 | convolution fusion | flops 25165824 | bytes 8651264 | tf_op jit(solution)/shard_map/mh,mhde->hde/dot_general | solution.py:96
  153.0 1.6 fusion.9
  154.6 2.5 %copy.56 = f32[512,512]{1,0:T(8,128)} copy(f32[512,512]{0,1:T(8,128)} %bitcast.111) | data formatting | bytes 2097152
  157.1 21.8 %all-gather.11.cloned.1.call-done = f32[128,128,128]{2,1,0:T(8,128)} async-done(((f32[4,128,128]{2,1,0:T(8,128)}), f32[128,128,128]{2,1,0:T(8,128)}) %all-gather.11.cloned.1.call-update) | async-done | bytes 8388624 | tf_op jit(solution)/shard_map/all_gather | solution.py:85
  178.8 4.1 %multiply_reduce_fusion = f32[4,128,128]{2,1,0:T(8,128)S(1)} fusion(f32[4,32,128,128]{3,2,0,1:T(8,128)} %bitcast.103, f32[4,32]{0,1:T(8,128)S(1)} %exponential_bitcast_fusion), kind=kLoop, calls=%fused_computation | loop fusion | flops 4128768 | bytes 8651264 | tf_op jit(solution)/shard_map/mh,mhde->hde/dot_general | solution.py:97
  183.0 1.7 fusion.5
  184.7 2.5 %copy.58 = f32[512,512]{1,0:T(8,128)} copy(f32[512,512]{0,1:T(8,128)} %bitcast.113) | data formatting | bytes 2097152
  187.2 3.0 %fusion.7 = f32[512,4,128]{0,2,1:T(8,128)} fusion(f32[512,4,128]{0,2,1:T(8,128)} %convolution_bitcast_fusion, f32[4,128,128]{2,1,0:T(8,128)S(1)} %multiply_reduce_fusion, f32[512,4]{0,1:T(4,128)S(1)} %get-tuple-element.12, bf16[512,512]{1,0:T(8,128)(2,1)} %param.8), kind=kOutput, calls=%fused_computation.15 | convolution fusion | flops 403177472 | bytes 2891776 | tf_op jit(solution)/shard_map/the,hde->thd/dot_general | solution.py:61
  190.1 2.5 %copy.57 = f32[512,512]{1,0:T(8,128)} copy(f32[512,512]{0,1:T(8,128)} %bitcast.112) | data formatting | bytes 2097152
  (38 shorter events, 0.7 us)
Async XLA Ops:
  7.2 50.6 %copy-start = (bf16[512,3072]{1,0:T(8,128)(2,1)S(1)}, bf16[512,3072]{1,0:T(8,128)(2,1)}, u32[]{:S(2)}) copy-start(bf16[512,3072]{1,0:T(8,128)(2,1)} %param.10) | copy-start | bytes 9437188
  7.2 50.6 %all-gather.7.cloned.1.call-start = ((), (), s32[]{:S(2)}) async-start(), calls=%async_computation | async-start | bytes 3538944 | tf_op jit(solution)/shard_map/all_gather | solution.py:73
  7.9 132.6 %all-gather.9.cloned.1.call-start = ((), (), s32[]{:S(2)}) async-start(), calls=%async_computation.1 | async-start | bytes 8650752 | tf_op jit(solution)/shard_map/all_gather | solution.py:84
  15.4 163.5 %all-gather.11.cloned.1.call-start = ((), (), s32[]{:S(2)}) async-start(), calls=%async_computation.2 | async-start | bytes 8650752 | tf_op jit(solution)/shard_map/all_gather | solution.py:85
  17.5 46.3 %copy-start.9 = (u32[256]{0:T(256)S(1)}, u32[256]{0:T(256)}, u32[]{:S(2)}) copy-start(u32[256]{0:T(256)} %constant.31) | copy-start | bytes 3076
  57.8 4.6 %copy-start.1 = (bf16[512,512]{0,1:T(8,128)(2,1)S(1)}, bf16[512,512]{0,1:T(8,128)(2,1)}, u32[]{:S(2)}) copy-start(bf16[512,512]{0,1:T(8,128)(2,1)} %copy.75) | copy-start | bytes 1572868
  61.6 0.8 copy-start.6
  130.2 3.0 %copy-start.2 = (bf16[512,512]{0,1:T(8,128)(2,1)S(1)}, bf16[512,512]{0,1:T(8,128)(2,1)}, u32[]{:S(2)}) copy-start(bf16[512,512]{0,1:T(8,128)(2,1)} %copy.75) | copy-start | bytes 1572868
  130.4 4.2 %copy-start.3 = (bf16[512,512]{0,1:T(8,128)(2,1)S(1)}, bf16[512,512]{0,1:T(8,128)(2,1)}, u32[]{:S(2)}) copy-start(bf16[512,512]{0,1:T(8,128)(2,1)} %copy.74) | copy-start | bytes 1572868
  140.5 12.4 %copy-start.5 = (f32[512,4,128]{0,2,1:T(8,128)S(1)}, f32[512,4,128]{0,2,1:T(8,128)}, u32[]{:S(2)}) copy-start(f32[512,4,128]{0,2,1:T(8,128)} %convolution_bitcast_fusion.1) | copy-start | bytes 3145732
  140.5 12.4 %copy-start.7 = (bf16[512,512]{0,1:T(8,128)(2,1)S(1)}, bf16[512,512]{0,1:T(8,128)(2,1)}, u32[]{:S(2)}) copy-start(bf16[512,512]{0,1:T(8,128)(2,1)} %copy-done.6) | copy-start | bytes 1572868
  178.8 4.2 %copy-start.4 = (bf16[512,512]{0,1:T(8,128)(2,1)S(1)}, bf16[512,512]{0,1:T(8,128)(2,1)}, u32[]{:S(2)}) copy-start(bf16[512,512]{0,1:T(8,128)(2,1)} %copy.74) | copy-start | bytes 1572868
  178.8 4.2 %copy-start.8 = (f32[512,4,128]{0,2,1:T(8,128)S(1)}, f32[512,4,128]{0,2,1:T(8,128)}, u32[]{:S(2)}) copy-start(f32[512,4,128]{0,2,1:T(8,128)} %fusion.3) | copy-start | bytes 3145732
Sparse Core Ops, SparseCore 0:
  9.8 47.9 all-gather.6
  60.3 58.4 all-gather.8
  121.4 57.4 all-gather.10
where the time goes:
time: 200 us; the launch traced here: 199 us
  blocking collectives  64.8 us (32%)
  waiting for transfers between devices  62.8 us (31%)
  matrix products  36.4 us (18%)
  local copies, waits for them, and re-layouts  14.6 us (7%)
  between operations  14.6 us (7%)
  other arithmetic  5.98 us (3%)
    unnamed x1, blocking collectives  64.8 us
    all_gather x1, waiting for transfers between devices, local(): cotangent = lax.all_gather(grad_out, 'head', axis=1, tiled=True)  40.3 us
    all_gather x1, waiting for transfers between devices, local(): lax.all_gather(grad_state[None], 'seq', axis=0, tiled=True)  21.8 us
    dot_general x1, matrix products, local(): jnp.einsum('mh,mhde->hde', fwd_weight, all_keys, precision=lax.Precision....  12.4 us
    unnamed x28, local copies, waits for them, and re-layouts  9.21 us
    dot_general x1, matrix products, local_terms(): jnp.einsum('hts,the->she', scores, grad_attn, preferred_element_type=jnp....  4.14 us
    dot_general x1, other arithmetic, local(): jnp.einsum('mh,mhde->hde', bwd_weight, all_grads, precision=lax.Precision...  4.14 us
    reshape x2, local copies, waits for them, and re-layouts, heads_view(): return array.reshape(tok_rows, head_count, DH)  4.11 us
  transfers between devices with their start and end apart: 3, of which 2 were waited for; matrix products, arithmetic and copies ran while one was open for 21% of the time, Pallas kernels for 0%

commit v1 on v0

v1 whole, which is shorter than its diff:
```python
import functools

import jax
import jax.numpy as jnp
from jax import lax
from jax.experimental import pallas as pl
from jax.experimental.pallas import tpu as pltpu
from jax.sharding import PartitionSpec as P

DH = 128
NT = (((1,), (1,)), ((), ()))
NN = (((1,), (0,)), ((), ()))
TN = (((0,), (0,)), ((), ()))
VMEM = pl.BlockSpec(memory_space=pltpu.VMEM)
ANY = pl.BlockSpec(memory_space=pl.ANY)
SMEM = pl.BlockSpec(memory_space=pltpu.SMEM)


def dot(a, b, dims):
    return lax.dot_general(a, b, dims, preferred_element_type=jnp.float32)


def pieces(x, n):
    out = []
    for _ in range(n):
        p = x.astype(jnp.bfloat16)
        out.append(p)
        x = x - p.astype(jnp.float32)
    return out


def call(kernel, outs, *args, specs=None, limit=24, scratch=(), aliases=None):
    return pl.pallas_call(
        kernel,
        out_shape=outs,
        in_specs=specs or [VMEM] * len(args),
        out_specs=tuple(VMEM for _ in outs),
        scratch_shapes=scratch,
        input_output_aliases=aliases or {},
        compiler_params=pltpu.CompilerParams(vmem_limit_bytes=limit * 2**20),
    )(*args)


def f32(*shape):
    return jax.ShapeDtypeStruct(shape, jnp.float32)


def bf16(*shape):
    return jax.ShapeDtypeStruct(shape, jnp.bfloat16)


def running(ld):
    n = ld.shape[1]
    s = lax.broadcasted_iota(jnp.int32, (n, n), 0)
    t = lax.broadcasted_iota(jnp.int32, (n, n), 1)
    upto = jnp.where(s <= t, 1.0, 0.0).astype(jnp.bfloat16)
    parts = pieces(ld, 3)
    return sum(dot(p, upto, NN) for p in parts), sum(dot(p, jnp.ones((n, DH), jnp.bfloat16), NN) for p in parts)


def running_columns(ld):
    n = ld.shape[1]
    s = lax.broadcasted_iota(jnp.int32, (n, n), 0)
    t = lax.broadcasted_iota(jnp.int32, (n, n), 1)
    since = jnp.where(s >= t, 1.0, 0.0).astype(jnp.bfloat16)
    return sum(dot(since, p, NT) for p in pieces(ld, 3))


def open_kernel(heads, k_hbm, v_hbm, ld_ref, tie_ref, state_ref, tied_ref, k_ref, v_ref, sems):
    copies = [pltpu.make_async_copy(src, dst, sems.at[i]) for i, (src, dst) in enumerate(((k_hbm, k_ref), (v_hbm, v_ref)))]
    for copy in copies:
        copy.start()
    tied_ref[...] = tie_ref[...]
    n = k_ref.shape[0]
    row, total = running(ld_ref[...])
    state_ref[pl.ds(heads * DH, heads), :] = total
    state_ref[pl.ds(heads * DH + heads, 8 - heads), :] = jnp.zeros((8 - heads, DH), jnp.float32)
    for copy in copies:
        copy.wait()
    for h in range(heads):
        cols = slice(h * DH, (h + 1) * DH)
        kt = k_ref[:, cols].T.astype(jnp.float32) * jnp.exp(row[h : h + 1, n - 1 : n] - row[h : h + 1, :])
        hi, lo = pieces(kt, 2)
        v = v_ref[:, cols]
        state_ref[pl.ds(h * DH, DH), :] = dot(hi, v, NN) + dot(lo, v, NN)


def local_kernel(heads, first, q_ref, k_ref, v_ref, ga_ref, row_ref, col_ref, dq_ref, dk_ref, dv_ref, start_ref, end_ref, tie_ref):
    n = q_ref.shape[0]
    step = n // 2
    s = lax.broadcasted_iota(jnp.int32, (step, step), 0)
    t = lax.broadcasted_iota(jnp.int32, (step, step), 1)
    keep = s <= t
    for i in range(heads):
        h = first + i
        cols, to = slice(h * DH, (h + 1) * DH), slice(i * DH, (i + 1) * DH)
        col = col_ref[:, h : h + 1]
        start_ref[:, to] = jnp.broadcast_to(jnp.exp(col) * (1.0 / DH), (n, DH))
        end_ref[:, to] = jnp.broadcast_to(jnp.exp(row_ref[h : h + 1, n - 1 : n] - col) * (1.0 / DH), (n, DH))
        for sb in range(2):
            srows = slice(sb * step, (sb + 1) * step)
            k, v = k_ref[srows, cols], v_ref[srows, cols]
            col = col_ref[srows, h : h + 1]
            dk = dv = None
            for tb in range(sb, 2):
                trows = slice(tb * step, (tb + 1) * step)
                q, ga = q_ref[trows, cols], ga_ref[trows, cols]
                gap = row_ref[h : h + 1, trows] - col
                if tb == sb:
                    gap = jnp.where(keep, gap, -jnp.inf)
                weight = jnp.exp(gap) * (1.0 / DH)
                scores = (dot(k, q, NT) * weight).astype(jnp.bfloat16)
                grads = (dot(v, ga, NT) * weight).astype(jnp.bfloat16)
                dv_part = dot(scores, ga, NN)
                dk_part = dot(grads, q, NN)
                dv = dv_part if dv is None else dv + dv_part
                dk = dk_part if dk is None else dk + dk_part
                dq = dot(grads, k, TN)
                if sb == 0:
                    dq_ref[trows, to] = dq
                else:
                    dq_ref[trows, to] += dq
            dk_ref[srows, to] = dk
            dv_ref[srows, to] = dv
    tie_ref[...] = jnp.zeros(tie_ref.shape, jnp.float32)


def first_kernel(
    place_ref, w_hbm, c_hbm, q_hbm, ld_ref, a1, b1, a2, b2,
    acc_ref, w_ref, qw_ref, row_ref, col_ref, near_ref, c_ref, q_ref, sems,
):
    z, side = place_ref[0], 1 - 2 * place_ref[1]
    rows, width = c_ref.shape
    heads = ld_ref.shape[0]
    targets = [near_ref.at[i] for i in range(5)] + [w_ref.at[i] for i in range(3)]
    copies = [pltpu.make_async_copy(c_hbm, c_ref, sems.at[8]), pltpu.make_async_copy(q_hbm, q_ref, sems.at[9])]
    for i, (offset, target) in enumerate(zip((0, -1, 1, -2, 2, -3, 3, 4), targets)):
        at = lax.rem(z + offset * side + 8, 8) * width
        copies.append(pltpu.make_async_copy(w_hbm.at[:, pl.ds(pl.multiple_of(at, 128), width)], target, sems.at[i]))
    for copy in copies:
        copy.start()
    row, _ = running(ld_ref[...])
    row_ref[...] = row
    col_ref[...] = running_columns(ld_ref[...])
    copies[1].wait()
    for h in range(heads):
        qt = q_ref[:, h * DH : (h + 1) * DH].T.astype(jnp.float32) * jnp.exp(row[h : h + 1, :])
        hi, lo = pieces(qt, 2)
        qw_ref[h, :DH, :] = hi
        qw_ref[h, DH:, :] = lo
    copies[0].wait()
    for copy in copies[2:]:
        copy.wait()
    half = rows // 2
    for part in range(2):
        at = pl.ds(part * half, half)
        acc = dot(c_ref[at, :], near_ref[0], NT)
        for i, ref in enumerate((a1, b1, a2, b2)):
            acc += dot(ref[at, :], near_ref[i + 1], NT)
        acc_ref[at, :] = acc


def second_kernel(acc_ref, a3, b3, w_ref, out_ref):
    half = acc_ref.shape[0] // 2
    for part in range(2):
        at = pl.ds(part * half, half)
        out_ref[at, :] = acc_ref[at, :] + dot(a3[at, :], w_ref[0], NT) + dot(b3[at, :], w_ref[1], NT)


def late_kernel(heads, acc_ref, a4, w_ref, qw_ref, ga_ref, state_ref):
    half = acc_ref.shape[0] // 2
    for part in range(2):
        at = pl.ds(part * half, half)
        ga_ref[at, :] = (acc_ref[at, :] + dot(a4[at, :], w_ref[2], NT)).astype(jnp.bfloat16)
    for h in range(heads):
        both = dot(qw_ref[h], ga_ref[:, h * DH : (h + 1) * DH], NN)
        state_ref[pl.ds(h * DH, DH), :] = both[:DH] + both[DH:]


def one_row(tile, i):
    return jnp.sum(jnp.where(lax.broadcasted_iota(jnp.int32, tile.shape, 0) == i, tile, 0.0), axis=0, keepdims=True)


def tail_of(totals):
    parts = [[p.astype(jnp.float32) for p in pieces(t, 3)] for t in totals]
    at = lax.broadcasted_iota(jnp.int32, (16, DH), 0)
    out = jnp.zeros((16, DH), jnp.float32)
    for j, three in enumerate(parts):
        for i, part in enumerate(three):
            out = jnp.where(at == 3 * j + i, part, out)
    return out.astype(jnp.bfloat16)


def total_in(tail, j):
    tail = tail.astype(jnp.float32)
    return one_row(tail, 3 * j) + one_row(tail, 3 * j + 1) + one_row(tail, 3 * j + 2)


def chip_key_kernel(heads, place_ref, key_ref, key_other, tie_ref, sent_ref, chip_ref, tied_ref):
    tied_ref[...] = tie_ref[...]
    core = place_ref[1]
    pair = heads // 2
    first = core == 0
    totals = []
    for j in range(pair):
        h = core * pair + j
        mine = one_row(key_ref[heads * DH :, :], h)
        others = one_row(key_other[heads * DH :, :], h)
        totals.append(mine + others)
        at = pl.ds(pl.multiple_of(h * DH, DH), DH)
        key = jnp.where(first, jnp.exp(others), 1.0) * key_ref[at, :] + jnp.where(first, 1.0, jnp.exp(mine)) * key_other[at, :]
        chip_ref[pl.ds(j * DH, DH), :] = key
        sent_ref[pl.ds(j * DH, DH), :] = key.astype(jnp.bfloat16)
    sent_ref[pl.ds(pair * DH, 16), :] = tail_of(totals)


def chip_grad_kernel(heads, place_ref, key_ref, key_other, grad_ref, grad_other, sent_ref, chip_ref):
    core = place_ref[1]
    pair = heads // 2
    first = core == 0
    for j in range(pair):
        h = core * pair + j
        mine = jnp.exp(one_row(key_ref[heads * DH :, :], h))
        others = jnp.exp(one_row(key_other[heads * DH :, :], h))
        at = pl.ds(pl.multiple_of(h * DH, DH), DH)
        grad = jnp.where(first, 1.0, others) * grad_ref[at, :] + jnp.where(first, mine, 1.0) * grad_other[at, :]
        chip_ref[pl.ds(j * DH, DH), :] = grad
        sent_ref[pl.ds(j * DH, DH), :] = grad.astype(jnp.bfloat16)


def flag(condition):
    return jnp.where(condition, 1.0, 0.0)


def chip_places(x):
    return [lax.rem(x - d + 4, 4) for d in range(4)]


def between(totals, place, low, high):
    return sum(t * flag((low < p) & (p < high)) for t, p in zip(totals, place))


def row_key_kernel(pair, place_ref, sent_ref, chip_ref, r1, r2, r3, tie_ref, in_ref, whole_ref, table_ref, tied_ref):
    tied_ref[...] = tie_ref[...]
    x = place_ref[2]
    n = pair * DH
    refs = (sent_ref, r1, r2, r3)
    place = chip_places(x)
    tails = [ref[pl.ds(n, 16), :] for ref in refs]
    for j in range(pair):
        totals = [total_in(tail, j) for tail in tails]
        at = pl.ds(j * DH, DH)
        inside = 0.0
        whole = jnp.exp(between(totals, place, x, 4)) * chip_ref[at, :]
        for d in range(1, 4):
            state = refs[d][at, :].astype(jnp.float32)
            whole += jnp.exp(between(totals, place, place[d], 4)) * state
            inside += jnp.exp(between(totals, place, place[d], x)) * flag(place[d] < x) * state
        in_ref[at, :] = inside
        whole_ref[at, :] = whole
        lines = totals + [
            jnp.exp(between(totals, place, -1, x)), jnp.exp(between(totals, place, x, 4)), sum(totals), jnp.zeros_like(totals[0])
        ]
        for i, line in enumerate(lines):
            table_ref[pl.ds(8 * j + i, 1), :] = line


def row_grad_kernel(pair, place_ref, chip_ref, r1, r2, r3, whole_key, table_ref, tie_ref, in_ref, s1, s2, s3, tied_ref):
    x, y = place_ref[2], place_ref[3]
    n = pair * DH
    refs = (chip_ref, r1, r2, r3)
    place = chip_places(x)
    row_totals = []
    for j in range(pair):
        totals = [table_ref[pl.ds(8 * j + d, 1), :] for d in range(4)]
        row_totals.append(table_ref[pl.ds(8 * j + 6, 1), :])
        at = pl.ds(j * DH, DH)
        inside = 0.0
        whole = jnp.exp(between(totals, place, -1, x)) * chip_ref[at, :]
        for d in range(1, 4):
            state = refs[d][at, :].astype(jnp.float32)
            whole += jnp.exp(between(totals, place, -1, place[d])) * state
            inside += jnp.exp(between(totals, place, x, place[d])) * flag(place[d] > x) * state
        in_ref[at, :] = inside
        for dy, ref in ((1, s1), (2, s2), (3, s3)):
            ref[at, :] = jnp.where(y + dy < 4, whole_key[at, :], whole).astype(jnp.bfloat16)
    tail = tail_of(row_totals)
    for ref in (s1, s2, s3):
        ref[pl.ds(n, 16), :] = tail
    tied_ref[...] = tie_ref[...]


def enter_kernel(pair, place_ref, key_in, grad_in, table_ref, r1, r2, r3, tie_ref, enter_ref, tied_ref):
    tied_ref[...] = tie_ref[...]
    y = place_ref[3]
    n = pair * DH
    refs = (r1, r2, r3)
    place = [lax.rem(y - d + 4, 4) for d in (1, 2, 3)]
    tails = [ref[pl.ds(n, 16), :] for ref in refs]
    for j in range(pair):
        totals = [total_in(tail, j) for tail in tails]
        at = pl.ds(j * DH, DH)
        key, grad = key_in[at, :], grad_in[at, :]
        into, out = table_ref[pl.ds(8 * j + 4, 1), :], table_ref[pl.ds(8 * j + 5, 1), :]
        for d in range(3):
            p = place[d]
            gap = sum(t * flag(((p < q) & (q < y)) | ((y < q) & (q < p))) for t, q in zip(totals, place))
            weight = jnp.exp(gap)
            state = refs[d][at, :].astype(jnp.float32)
            key += into * weight * flag(p < y) * state
            grad += out * weight * flag(p > y) * state
        enter_ref[at, :] = key
        enter_ref[pl.ds((pair + j) * DH, DH), :] = grad


def close_kernel(heads, place_ref, enter_ref, enter_other, key_other, grad_other, ga_ref, k_ref, v_ref, *refs):
    halves, outs, room, sems = (refs[:5], refs[5:10]), refs[10:13], refs[13], refs[14]
    core = place_ref[1]
    pair = heads // 2
    first = core == 0
    copies = []

    def fold(x):
        return x[:, :DH] + x[:, DH:]

    for h in range(heads):
        start_w, end_w, dq, dk, dv = halves[h // pair]
        i = h % pair
        at, low = pl.ds(i * DH, DH), pl.ds((pair + i) * DH, DH)
        cols, mine = slice(h * DH, (h + 1) * DH), slice(i * DH, (i + 1) * DH)
        here = core == h // pair
        key = jnp.where(here, enter_ref[at, :], enter_other[at, :])
        grad = jnp.where(here, enter_ref[low, :], enter_other[low, :])
        decay = jnp.exp(key_other[pl.ds(heads * DH + h, 1), :])
        si = jnp.where(first, key, decay * key + key_other[pl.ds(h * DH, DH), :])
        so = jnp.where(first, decay * grad + grad_other[pl.ds(h * DH, DH), :], grad)
        si = jnp.concatenate(pieces(si, 2), axis=0)
        hi, lo = pieces(so, 2)
        so = jnp.concatenate([hi, lo], axis=0)
        so_wide = jnp.concatenate([hi, lo], axis=1)
        room[0, h] = dq[:, mine] + start_w[:, mine] * fold(dot(ga_ref[:, cols], si, NT))
        room[1, h] = dk[:, mine] + end_w[:, mine] * fold(dot(v_ref[:, cols], so, NT))
        room[2, h] = dv[:, mine] + end_w[:, mine] * fold(dot(k_ref[:, cols], so_wide, NN))
        for j in range(3):
            copy = pltpu.make_async_copy(room.at[j, h], outs[j].at[:, pl.ds(h * DH, DH)], sems.at[j, h])
            copy.start()
            copies.append(copy)
    for copy in copies:
        copy.wait()


def local(queries, keys, values, log_decay, out_weight, grad_out):
    rows, width = queries.shape
    heads = log_decay.shape[0]
    pair = heads // 2
    z = lax.axis_index("head")
    seq = lax.axis_index("seq")
    place = jnp.stack([z, seq % 2, (seq // 2) % 4, seq // 8]).astype(jnp.int32)

    def along_z(array):
        pairs = []
        for i in range(32):
            for j in range(8):
                pairs.append((i * 8 + j, i * 8 + (j + (1 if i % 2 == 0 else -1)) % 8))
        return lax.ppermute(array, ("seq", "head"), pairs)

    def along_seq(array, dy=0, dx=0, flip=False):
        pairs = []
        for i in range(32):
            a, b, c = i // 8, (i // 2) % 4, i % 2
            pairs.append((i, ((a + dy) % 4) * 8 + ((b + dx) % 4) * 2 + (1 - c if flip else c)))
        return lax.ppermute(array, "seq", pairs)

    def other(array):
        return along_seq(array, flip=True)

    def in_hbm(array):
        return pltpu.with_memory_space_constraint(array, pltpu.HBM)

    b0 = other(grad_out)
    key_own, b0 = call(
        functools.partial(open_kernel, heads), (f32(heads * DH + 8, DH), bf16(*grad_out.shape)),
        in_hbm(keys), in_hbm(values), log_decay, b0,
        specs=[ANY] * 2 + [VMEM] * 2,
        scratch=[pltpu.VMEM((rows, width), jnp.bfloat16)] * 2 + [pltpu.SemaphoreType.DMA((2,))],
    )
    a1 = along_z(grad_out)
    b1 = along_z(b0)

    key_other = other(key_own)
    sent, chip, a1 = call(
        functools.partial(chip_key_kernel, heads), (bf16(pair * DH + 16, DH), f32(pair * DH, DH), bf16(*grad_out.shape)),
        place, key_own, key_other, a1, specs=[SMEM] + [VMEM] * 3,
    )
    from_x = [along_seq(sent, dx=d) for d in (2, 1, 3)]
    from_x = [from_x[1], from_x[0], from_x[2]]
    a2 = along_z(a1)
    b1_here = other(b1)
    b2 = along_z(b1)
    key_in, key_row, table, a2 = call(
        functools.partial(row_key_kernel, pair),
        (f32(pair * DH, DH), f32(pair * DH, DH), f32(8 * pair, DH), bf16(*grad_out.shape)),
        place, sent, chip, *from_x, a2, specs=[SMEM] + [VMEM] * 6,
    )
    a3 = along_z(a2)
    b2_here = other(b2)
    b3 = along_z(b2)
    a4 = along_z(a3)
    b3_here = other(b3)

    qd = grad_out.shape[1]
    acc, w, qw, row, col = call(
        first_kernel,
        (f32(rows, width), bf16(3, width, qd), bf16(heads, 2 * DH, rows), f32(heads, rows), f32(rows, heads)),
        place, in_hbm(out_weight), in_hbm(grad_out), in_hbm(queries), log_decay, a1, b1_here, a2, b2_here,
        specs=[SMEM] + [ANY] * 3 + [VMEM] * 5,
        scratch=[
            pltpu.VMEM((5, width, qd), jnp.bfloat16), pltpu.VMEM((rows, qd), jnp.bfloat16),
            pltpu.VMEM((rows, width), jnp.bfloat16), pltpu.SemaphoreType.DMA((10,)),
        ],
    )
    (acc,) = call(second_kernel, (f32(rows, width),), acc, a3, b3_here, w)
    ga, grad_own = call(
        functools.partial(late_kernel, heads), (bf16(rows, width), f32(heads * DH, DH)), acc, a4, w, qw
    )

    grad_other = other(grad_own)
    sent, chip = call(
        functools.partial(chip_grad_kernel, heads), (bf16(pair * DH, DH), f32(pair * DH, DH)),
        place, key_own, key_other, grad_own, grad_other, specs=[SMEM] + [VMEM] * 4,
    )
    from_x = [along_seq(sent, dx=d) for d in (2, 1, 3)]
    from_x = [from_x[1], from_x[0], from_x[2]]
    def local_part(first):
        *parts, tie = call(
            functools.partial(local_kernel, pair, first), (f32(rows, pair * DH),) * 5 + (f32(8, DH),),
            queries, keys, values, ga, row, col,
        )
        dq, dk, dv, start_w, end_w = parts
        return (start_w, end_w, dq, dk, dv), tie

    low, tie = local_part(0)
    high, tie_high = local_part(pair)
    grad_in, *sent, _ = call(
        functools.partial(row_grad_kernel, pair),
        (f32(pair * DH, DH),) + (bf16(pair * DH + 16, DH),) * 3 + (f32(8, DH),),
        place, chip, *from_x, key_row, table, tie, specs=[SMEM] + [VMEM] * 7,
    )
    from_y = [along_seq(sent[d - 1], dy=d) for d in (2, 1, 3)]
    from_y = [from_y[1], from_y[0], from_y[2]]
    enter, _ = call(
        functools.partial(enter_kernel, pair), (f32(2 * pair * DH, DH), f32(8, DH)),
        place, key_in, grad_in, table, *from_y, tie_high, specs=[SMEM] + [VMEM] * 7,
    )
    enter_other = other(enter)

    return pl.pallas_call(
        functools.partial(close_kernel, heads),
        out_shape=(f32(rows, width),) * 3,
        in_specs=[SMEM] + [VMEM] * 17,
        out_specs=(ANY,) * 3,
        scratch_shapes=[pltpu.VMEM((3, heads, rows, DH), jnp.float32), pltpu.SemaphoreType.DMA((3, heads))],
        compiler_params=pltpu.CompilerParams(vmem_limit_bytes=24 * 2**20),
    )(place, enter, enter_other, key_other, grad_other, ga, keys, values, *low, *high)


def solution(mesh):
    return jax.shard_map(
        local,
        mesh=mesh,
        in_specs=(
            P("seq", "head"),
            P("seq", "head"),
            P("seq", "head"),
            P("head", "seq"),
            P("head", None),
            P("seq", "head"),
        ),
        out_specs=(P("seq", "head"), P("seq", "head"), P("seq", "head")),
        check_vma=False,
    )
```

time: 200 us -> 79.1 us (0.40)
  blocking collectives: 64.8 us -> 0 us
  waiting for transfers between devices: 62.8 us -> 23.7 us
  matrix products: 36.4 us -> 0 us
  starting transfers between devices: 0.12 us -> 34.4 us
  Pallas kernels: 0 us -> 19.1 us
  local copies, waits for them, and re-layouts: 14.6 us -> 0.72 us
  between operations: 14.6 us -> 0.93 us
  other arithmetic: 5.98 us -> 0.08 us
    unnamed x1 -> x0, blocking collectives: 64.8 us -> none
    all_gather x3 -> x0, waiting for transfers between devices: 62 us -> none  [the longest x1 40.3 us: local(): cotangent = lax.all_gather(grad_out, 'head', axis=1, tiled=True)]
    dot_general x11 -> x0, matrix products: 36.4 us -> none  [the longest x1 12.4 us: local(): jnp.einsum('mh,mhde->hde', fwd_weight, all_keys, precision=lax.Precision....]
    ppermute x0 -> x23, starting transfers between devices: none -> 34.4 us  [the longest x16 22.5 us: along_seq(): return lax.ppermute(array, 'seq', pairs)]
    ppermute x0 -> x23, waiting for transfers between devices: none -> 23.7 us  [the longest x16 13.2 us: along_seq(): return lax.ppermute(array, 'seq', pairs)]
    pallas_call x0 -> x12, Pallas kernels: none -> 19.1 us  [the longest x11 16.3 us: call(): pl.pallas_call(kernel, out_shape=outs, in_specs=specs or [VMEM] * len(arg...]
    unnamed x28 -> x10, local copies, waits for them, and re-layouts: 9.21 us -> 0.72 us
    reshape x3 -> x0, local copies, waits for them, and re-layouts: 4.98 us -> none  [the longest x2 4.11 us: heads_view(): return array.reshape(tok_rows, head_count, DH)]
  transfers between devices with their start and end apart: 3 -> 23, of which waited for: 2 -> 13; matrix products, arithmetic and copies ran while one was open for 21% -> 0% of each run, Pallas kernels for 0% -> 14%
where the time goes in v1:
time: 79.1 us; the launch traced here: 78.9 us
  starting transfers between devices  34.4 us (43%)
  waiting for transfers between devices  23.7 us (30%)
  Pallas kernels  19.1 us (24%)
  between operations  0.93 us (1%)
    ppermute x16, starting transfers between devices, along_seq(): return lax.ppermute(array, 'seq', pairs)  22.5 us
    pallas_call x11, Pallas kernels, call(): pl.pallas_call(kernel, out_shape=outs, in_specs=specs or [VMEM] * len(arg...  16.3 us
    ppermute x16, waiting for transfers between devices, along_seq(): return lax.ppermute(array, 'seq', pairs)  13.2 us
    ppermute x7, starting transfers between devices, along_z(): return lax.ppermute(array, ('seq', 'head'), pairs)  11.9 us
    ppermute x7, waiting for transfers between devices, along_z(): return lax.ppermute(array, ('seq', 'head'), pairs)  10.5 us
    pallas_call x1, Pallas kernels, local(): pl.pallas_call(functools.partial(close_kernel, heads), out_shape=(f32(row...  2.78 us
  transfers between devices with their start and end apart: 23, of which 13 were waited for; matrix products, arithmetic and copies ran while one was open for 0% of the time, Pallas kernels for 14%

profile of v1, /device:TPU:1, one launch (start us, length us, event | category | flops | bytes accessed | tf_op | source)
XLA Modules:
  0.0 78.9 jit_solution(12501578286338473237)
XLA Ops:
  0.6 3.3 %collective-permute-start = (bf16[512,384]{1,0:T(8,128)(2,1)}, bf16[512,384]{1,0:T(8,128)(2,1)S(1)}, u32[]{:S(2)}, u32[]{:S(2)}) collective-permute-start(bf16[512,384]{1,0:T(8,128)(2,1)} %c_hbm.1), channel_id=1, source_target_pairs={{0,8},{8,0},{16,24},{24,16},{32,40},{40,32},{48,56},{56,48},{64,72... | collective-permute-start | bytes 1179656 | tf_op jit(solution)/shard_map/ppermute | solution.py:372
  4.0 1.6 %collective-permute-done.tie_ref = bf16[512,384]{1,0:T(8,128)(2,1)S(1)} collective-permute-done((bf16[512,384]{1,0:T(8,128)(2,1)}, bf16[512,384]{1,0:T(8,128)(2,1)S(1)}, u32[]{:S(2)}, u32[]{:S(2)}) %collective-permute-start) | collective-permute-done | bytes 393248 | tf_op jit(solution)/shard_map/ppermute | solution.py:372
  6.2 1.8 %shard_map.85 = (f32[520,128]{1,0:T(8,128)S(1)}, bf16[512,384]{1,0:T(8,128)(2,1)S(1)}) custom-call(bf16[512,512]{1,0:T(8,128)(2,1)} %k_ref.5, bf16[512,512]{1,0:T(8,128)(2,1)} %v_ref.5, f32[4,512]{1,0:T(4,128)S(1)} %copy-done.3, bf16[512,384]{1,0:T(8,128)(2,1)S(1)} %collective-permute-done.tie_ref), custom_call_target="tpu_custom_call" | custom-call | tf_op jit(solution)/shard_map/pallas_call | solution.py:33
  8.0 3.9 %collective-permute-start.7 = (bf16[512,384]{1,0:T(8,128)(2,1)S(1)}, bf16[512,384]{1,0:T(8,128)(2,1)S(1)}, u32[]{:S(2)}, u32[]{:S(2)}) collective-permute-start(bf16[512,384]{1,0:T(8,128)(2,1)S(1)} %get-tuple-element.43), channel_id=1, source_target_pairs={{0,1},{1,2},{2,3},{3,4},{4,5},{5,6},{6,7},{7,0},{8,15},{9,8},{10,9... | collective-permute-start | bytes 1179656 | tf_op jit(solution)/shard_map/ppermute | solution.py:365
  12.7 3.9 %collective-permute-done.7 = bf16[512,384]{1,0:T(8,128)(2,1)S(1)} collective-permute-done((bf16[512,384]{1,0:T(8,128)(2,1)S(1)}, bf16[512,384]{1,0:T(8,128)(2,1)S(1)}, u32[]{:S(2)}, u32[]{:S(2)}) %collective-permute-start.7) | collective-permute-done | bytes 393248 | tf_op jit(solution)/shard_map/ppermute | solution.py:365
  16.6 3.1 %collective-permute-start.9 = (bf16[512,384]{1,0:T(8,128)(2,1)S(1)}, bf16[512,384]{1,0:T(8,128)(2,1)S(1)}, u32[]{:S(2)}, u32[]{:S(2)}) collective-permute-start(bf16[512,384]{1,0:T(8,128)(2,1)S(1)} %collective-permute-done.7), channel_id=1, source_target_pairs={{0,1},{1,2},{2,3},{3,4},{4,5},{5,6},{6,7},{7,0},{8,15},{9,8},{10,9... | collective-permute-start | bytes 1179656 | tf_op jit(solution)/shard_map/ppermute | solution.py:365
  19.7 1.2 %collective-permute-done.2.tie_ref = bf16[512,384]{1,0:T(8,128)(2,1)S(1)} collective-permute-done((bf16[512,384]{1,0:T(8,128)(2,1)}, bf16[512,384]{1,0:T(8,128)(2,1)S(1)}, u32[]{:S(2)}, u32[]{:S(2)}) %collective-permute-start.2) | collective-permute-done | bytes 393248 | tf_op jit(solution)/shard_map/ppermute | solution.py:365
  21.6 3.1 %collective-permute-start.6 = (bf16[512,384]{1,0:T(8,128)(2,1)S(1)}, bf16[512,384]{1,0:T(8,128)(2,1)S(1)}, u32[]{:S(2)}, u32[]{:S(2)}) collective-permute-start(bf16[512,384]{1,0:T(8,128)(2,1)S(1)} %get-tuple-element.41.a1), channel_id=1, source_target_pairs={{0,1},{1,2},{2,3},{3,4},{4,5},{5,6},{6,7},{7,0},{8,15},{9,8},{10,9... | collective-permute-start | bytes 1179656 | tf_op jit(solution)/shard_map/ppermute | solution.py:365
  24.6 2.5 %collective-permute-start.5 = (bf16[272,128]{1,0:T(8,128)(2,1)S(1)}, bf16[272,128]{1,0:T(8,128)(2,1)S(1)}, u32[]{:S(2)}, u32[]{:S(2)}) collective-permute-start(bf16[272,128]{1,0:T(8,128)(2,1)S(1)} %get-tuple-element.39.sent_ref), channel_id=1, source_target_pairs={{0,48},{8,56},{16,0},{24,8},{32,16},{40,24},{48,32},{56,40},{64,11... | collective-permute-start | bytes 208904 | tf_op jit(solution)/shard_map/ppermute | solution.py:372
  28.3 1.5 %collective-permute-done.5.r3 = bf16[272,128]{1,0:T(8,128)(2,1)S(1)} collective-permute-done((bf16[272,128]{1,0:T(8,128)(2,1)S(1)}, bf16[272,128]{1,0:T(8,128)(2,1)S(1)}, u32[]{:S(2)}, u32[]{:S(2)}) %collective-permute-start.5) | collective-permute-done | bytes 69664 | tf_op jit(solution)/shard_map/ppermute | solution.py:372
  29.9 2.6 %collective-permute-done.4.r2 = bf16[272,128]{1,0:T(8,128)(2,1)S(1)} collective-permute-done((bf16[272,128]{1,0:T(8,128)(2,1)S(1)}, bf16[272,128]{1,0:T(8,128)(2,1)S(1)}, u32[]{:S(2)}, u32[]{:S(2)}) %collective-permute-start.4) | collective-permute-done | bytes 69664 | tf_op jit(solution)/shard_map/ppermute | solution.py:372
  32.5 1.3 %collective-permute-done.3.r1 = bf16[272,128]{1,0:T(8,128)(2,1)S(1)} collective-permute-done((bf16[272,128]{1,0:T(8,128)(2,1)S(1)}, bf16[272,128]{1,0:T(8,128)(2,1)S(1)}, u32[]{:S(2)}, u32[]{:S(2)}) %collective-permute-start.3) | collective-permute-done | bytes 69664 | tf_op jit(solution)/shard_map/ppermute | solution.py:372
  35.2 1.6 %collective-permute-start.13 = (bf16[512,384]{1,0:T(8,128)(2,1)S(1)}, bf16[512,384]{1,0:T(8,128)(2,1)S(1)}, u32[]{:S(2)}, u32[]{:S(2)}) collective-permute-start(bf16[512,384]{1,0:T(8,128)(2,1)S(1)} %collective-permute-done.12), channel_id=1, source_target_pairs={{0,8},{8,0},{16,24},{24,16},{32,40},{40,32},{48,56},{56,48},{64,72... | collective-permute-start | bytes 1179656 | tf_op jit(solution)/shard_map/ppermute | solution.py:372
  36.7 4.7 %collective-permute-done.11.a3 = bf16[512,384]{1,0:T(8,128)(2,1)S(1)} collective-permute-done((bf16[512,384]{1,0:T(8,128)(2,1)S(1)}, bf16[512,384]{1,0:T(8,128)(2,1)S(1)}, u32[]{:S(2)}, u32[]{:S(2)}) %collective-permute-start.11) | collective-permute-done | bytes 393248 | tf_op jit(solution)/shard_map/ppermute | solution.py:365
  41.4 0.9 %collective-permute-start.14 = (bf16[512,384]{1,0:T(8,128)(2,1)S(1)}, bf16[512,384]{1,0:T(8,128)(2,1)S(1)}, u32[]{:S(2)}, u32[]{:S(2)}) collective-permute-start(bf16[512,384]{1,0:T(8,128)(2,1)S(1)} %collective-permute-done.11.a3), channel_id=1, source_target_pairs={{0,1},{1,2},{2,3},{3,4},{4,5},{5,6},{6,7},{7,0},{8,15},{9,8},{10,9... | collective-permute-start | bytes 1179656 | tf_op jit(solution)/shard_map/ppermute | solution.py:365
  42.4 4.6 %shard_map.88 = (f32[512,512]{1,0:T(8,128)S(1)}, bf16[3,512,384]{2,1,0:T(8,128)(2,1)S(1)}, bf16[4,256,512]{2,1,0:T(8,128)(2,1)S(1)}, f32[4,512]{1,0:T(4,128)S(1)}, f32[512,4]{1,0:T(8,128)S(1)}) custom-call(s32[4]{0:T(128)S(1)} %pad_add_fusion.place_ref, bf16[512,3072]{1,0:T(8,128)(2,1)} %w_hbm.1, bf16[512,384]{1,0:T(8,128)(2,1)} %c_hbm.1, ...), custom_call_target="tpu_custom_call" | custom-call | tf_op jit(solution)/shard_map/pallas_call | solution.py:33
  47.0 0.8 shard_map.89.acc_ref
  48.4 0.9 %shard_map.90 = (bf16[512,512]{1,0:T(8,128)(2,1)S(1)}, f32[512,128]{1,0:T(8,128)S(1)}) custom-call(f32[512,512]{1,0:T(8,128)S(1)} %shard_map.89.acc_ref, bf16[512,384]{1,0:T(8,128)(2,1)S(1)} %collective-permute-done.14.a4, bf16[3,512,384]{2,1,0:T(8,128)(2,1)S(1)} %get-tuple-element.46.w_ref, bf16[4,256,512]{2,1,0:T(8,128)(2,1)S(1)} %get-tuple-element.47.qw_ref), custom_call_target="tpu_custom_call" | custom-call | tf_op jit(solution)/shard_map/pallas_call | solution.py:33
  49.3 4.6 %collective-permute-start.15 = (f32[512,128]{1,0:T(8,128)S(1)}, f32[512,128]{1,0:T(8,128)S(1)}, u32[]{:S(2)}, u32[]{:S(2)}) collective-permute-start(f32[512,128]{1,0:T(8,128)S(1)} %get-tuple-element.48.grad_ref), channel_id=1, source_target_pairs={{0,8},{8,0},{16,24},{24,16},{32,40},{40,32},{48,56},{56,48},{64,72... | collective-permute-start | bytes 786440 | tf_op jit(solution)/shard_map/ppermute | solution.py:372
  53.9 1.2 %collective-permute-done.15.grad_other = f32[512,128]{1,0:T(8,128)S(1)} collective-permute-done((f32[512,128]{1,0:T(8,128)S(1)}, f32[512,128]{1,0:T(8,128)S(1)}, u32[]{:S(2)}, u32[]{:S(2)}) %collective-permute-start.15) | collective-permute-done | bytes 262176 | tf_op jit(solution)/shard_map/ppermute | solution.py:372
  57.4 2.0 %shard_map.92 = (f32[512,256]{1,0:T(8,128)S(1)}, f32[512,256]{1,0:T(8,128)S(1)}, f32[512,256]{1,0:T(8,128)S(1)}, f32[512,256]{1,0:T(8,128)S(1)}, f32[512,256]{1,0:T(8,128)S(1)}, /*index=5*/f32[8,128]{1,0:T(8,128)S(1)}) custom-call(bf16[512,512]{1,0:T(8,128)(2,1)S(1)} %copy-done.2, bf16[512,512]{1,0:T(8,128)(2,1)S(1)} %copy-done, ...), custom_call_target="tpu_custom_call" | custom-call | tf_op jit(solution)/shard_map/pallas_call | solution.py:33
  59.5 1.5 %collective-permute-done.17.r2 = bf16[256,128]{1,0:T(8,128)(2,1)S(1)} collective-permute-done((bf16[256,128]{1,0:T(8,128)(2,1)S(1)}, bf16[256,128]{1,0:T(8,128)(2,1)S(1)}, u32[]{:S(2)}, u32[]{:S(2)}) %collective-permute-start.17) | collective-permute-done | bytes 65568 | tf_op jit(solution)/shard_map/ppermute | solution.py:372
  60.9 1.8 %collective-permute-done.16.r1 = bf16[256,128]{1,0:T(8,128)(2,1)S(1)} collective-permute-done((bf16[256,128]{1,0:T(8,128)(2,1)S(1)}, bf16[256,128]{1,0:T(8,128)(2,1)S(1)}, u32[]{:S(2)}, u32[]{:S(2)}) %collective-permute-start.16) | collective-permute-done | bytes 65568 | tf_op jit(solution)/shard_map/ppermute | solution.py:372
  62.7 1.2 %shard_map.93 = (f32[256,128]{1,0:T(8,128)S(1)}, bf16[272,128]{1,0:T(8,128)(2,1)S(1)}, bf16[272,128]{1,0:T(8,128)(2,1)S(1)}, bf16[272,128]{1,0:T(8,128)(2,1)S(1)}, f32[8,128]{1,0:T(8,128)}) custom-call(s32[4]{0:T(128)S(1)} %pad_add_fusion.place_ref, f32[256,128]{1,0:T(8,128)S(1)} %get-tuple-element.49.chip_ref, ...), custom_call_target="tpu_custom_call" | custom-call | tf_op jit(solution)/shard_map/pallas_call | solution.py:33
  63.9 1.3 %collective-permute-start.19 = (bf16[272,128]{1,0:T(8,128)(2,1)S(1)}, bf16[272,128]{1,0:T(8,128)(2,1)S(1)}, u32[]{:S(2)}, u32[]{:S(2)}) collective-permute-start(bf16[272,128]{1,0:T(8,128)(2,1)S(1)} %get-tuple-element.58), channel_id=1, source_target_pairs={{0,64},{8,72},{16,80},{24,88},{32,96},{40,104},{48,112},{56,120},{... | collective-permute-start | bytes 208904 | tf_op jit(solution)/shard_map/ppermute | solution.py:372
  65.2 2.6 %collective-permute-start.20 = (bf16[272,128]{1,0:T(8,128)(2,1)S(1)}, bf16[272,128]{1,0:T(8,128)(2,1)S(1)}, u32[]{:S(2)}, u32[]{:S(2)}) collective-permute-start(bf16[272,128]{1,0:T(8,128)(2,1)S(1)} %get-tuple-element.59), channel_id=1, source_target_pairs={{0,128},{8,136},{16,144},{24,152},{32,160},{40,168},{48,176},{56,1... | collective-permute-start | bytes 208904 | tf_op jit(solution)/shard_map/ppermute | solution.py:372
  67.8 1.1 %collective-permute-start.21 = (bf16[272,128]{1,0:T(8,128)(2,1)S(1)}, bf16[272,128]{1,0:T(8,128)(2,1)S(1)}, u32[]{:S(2)}, u32[]{:S(2)}) collective-permute-start(bf16[272,128]{1,0:T(8,128)(2,1)S(1)} %get-tuple-element.60), channel_id=1, source_target_pairs={{0,192},{8,200},{16,208},{24,216},{32,224},{40,232},{48,240},{56,2... | collective-permute-start | bytes 208904 | tf_op jit(solution)/shard_map/ppermute | solution.py:372
  68.9 2.0 %shard_map.94 = (f32[512,256]{1,0:T(8,128)S(1)}, f32[512,256]{1,0:T(8,128)S(1)}, f32[512,256]{1,0:T(8,128)S(1)}, f32[512,256]{1,0:T(8,128)S(1)}, f32[512,256]{1,0:T(8,128)S(1)}, /*index=5*/f32[8,128]{1,0:T(8,128)S(1)}) custom-call(bf16[512,512]{1,0:T(8,128)(2,1)S(1)} %copy-done.2, bf16[512,512]{1,0:T(8,128)(2,1)S(1)} %copy-done, ...), custom_call_target="tpu_custom_call" | custom-call | tf_op jit(solution)/shard_map/pallas_call | solution.py:33
  71.6 1.2 %shard_map.95 = (f32[512,128]{1,0:T(8,128)S(1)}, f32[8,128]{1,0:T(8,128)}) custom-call(s32[4]{0:T(128)S(1)} %pad_add_fusion.place_ref, f32[256,128]{1,0:T(8,128)S(1)} %get-tuple-element.42.key_in, f32[256,128]{1,0:T(8,128)S(1)} %get-tuple-element.57.grad_in, f32[16,128]{1,0:T(8,128)S(1)} %get-tuple-element.52.table_ref, ...), custom_call_target="tpu_custom_call" | custom-call | tf_op jit(solution)/shard_map/pallas_call | solution.py:33
  72.7 2.1 %collective-permute-start.22 = (f32[512,128]{1,0:T(8,128)S(1)}, f32[512,128]{1,0:T(8,128)S(1)}, u32[]{:S(2)}, u32[]{:S(2)}) collective-permute-start(f32[512,128]{1,0:T(8,128)S(1)} %get-tuple-element.62.enter_ref), channel_id=1, source_target_pairs={{0,8},{8,0},{16,24},{24,16},{32,40},{40,32},{48,56},{56,48},{64,72... | collective-permute-start | bytes 786440 | tf_op jit(solution)/shard_map/ppermute | solution.py:372
  74.8 1.2 %collective-permute-done.22.enter_other = f32[512,128]{1,0:T(8,128)S(1)} collective-permute-done((f32[512,128]{1,0:T(8,128)S(1)}, f32[512,128]{1,0:T(8,128)S(1)}, u32[]{:S(2)}, u32[]{:S(2)}) %collective-permute-start.22) | collective-permute-done | bytes 262176 | tf_op jit(solution)/shard_map/ppermute | solution.py:372
  76.0 2.8 %shard_map.96 = (f32[512,512]{1,0:T(8,128)}, f32[512,512]{1,0:T(8,128)}, f32[512,512]{1,0:T(8,128)}) custom-call(s32[4]{0:T(128)S(1)} %pad_add_fusion.place_ref, f32[512,128]{1,0:T(8,128)S(1)} %get-tuple-element.62.enter_ref, f32[512,128]{1,0:T(8,128)S(1)} %collective-permute-done.22.enter_other, f32[520,128]{1,0:T(8,128)S(1)} %collective-permute-done.1.key_other, ...), custom_call_target="tpu_custom_call" | custom-call | tf_op jit(solution)/shard_map/pallas_call | solution.py:457
  (37 shorter events, 8.5 us)
Async XLA Ops:
  0.6 4.9 %collective-permute-start = (bf16[512,384]{1,0:T(8,128)(2,1)}, bf16[512,384]{1,0:T(8,128)(2,1)S(1)}, u32[]{:S(2)}, u32[]{:S(2)}) collective-permute-start(bf16[512,384]{1,0:T(8,128)(2,1)} %c_hbm.1), channel_id=1, source_target_pairs={{0,8},{8,0},{16,24},{24,16},{32,40},{40,32},{48,56},{56,48},{64,72... | collective-permute-start | bytes 1179656 | tf_op jit(solution)/shard_map/ppermute | solution.py:372
  5.5 0.7 copy-start.3
  6.2 36.2 %copy-start.4 = (f32[4,512]{1,0:T(4,128)S(1)}, f32[4,512]{1,0:T(4,128)}, u32[]{:S(2)}) copy-start(f32[4,512]{1,0:T(4,128)} %ld_ref.3) | copy-start | bytes 24580
  8.0 8.6 %collective-permute-start.7 = (bf16[512,384]{1,0:T(8,128)(2,1)S(1)}, bf16[512,384]{1,0:T(8,128)(2,1)S(1)}, u32[]{:S(2)}, u32[]{:S(2)}) collective-permute-start(bf16[512,384]{1,0:T(8,128)(2,1)S(1)} %get-tuple-element.43), channel_id=1, source_target_pairs={{0,1},{1,2},{2,3},{3,4},{4,5},{5,6},{6,7},{7,0},{8,15},{9,8},{10,9... | collective-permute-start | bytes 1179656 | tf_op jit(solution)/shard_map/ppermute | solution.py:365
  11.9 9.0 %collective-permute-start.2 = (bf16[512,384]{1,0:T(8,128)(2,1)}, bf16[512,384]{1,0:T(8,128)(2,1)S(1)}, u32[]{:S(2)}, u32[]{:S(2)}) collective-permute-start(bf16[512,384]{1,0:T(8,128)(2,1)} %c_hbm.1), channel_id=1, source_target_pairs={{0,1},{1,2},{2,3},{3,4},{4,5},{5,6},{6,7},{7,0},{8,15},{9,8},{10,9... | collective-permute-start | bytes 1179656 | tf_op jit(solution)/shard_map/ppermute | solution.py:365
  12.6 8.3 %collective-permute-start.1 = (f32[520,128]{1,0:T(8,128)S(1)}, f32[520,128]{1,0:T(8,128)S(1)}, u32[]{:S(2)}, u32[]{:S(2)}) collective-permute-start(f32[520,128]{1,0:T(8,128)S(1)} %get-tuple-element.38.key_ref), channel_id=1, source_target_pairs={{0,8},{8,0},{16,24},{24,16},{32,40},{40,32},{48,56},{56,48},{64,72... | collective-permute-start | bytes 798728 | tf_op jit(solution)/shard_map/ppermute | solution.py:372
  16.6 11.6 %collective-permute-start.9 = (bf16[512,384]{1,0:T(8,128)(2,1)S(1)}, bf16[512,384]{1,0:T(8,128)(2,1)S(1)}, u32[]{:S(2)}, u32[]{:S(2)}) collective-permute-start(bf16[512,384]{1,0:T(8,128)(2,1)S(1)} %collective-permute-done.7), channel_id=1, source_target_pairs={{0,1},{1,2},{2,3},{3,4},{4,5},{5,6},{6,7},{7,0},{8,15},{9,8},{10,9... | collective-permute-start | bytes 1179656 | tf_op jit(solution)/shard_map/ppermute | solution.py:365
  21.6 12.2 %collective-permute-start.6 = (bf16[512,384]{1,0:T(8,128)(2,1)S(1)}, bf16[512,384]{1,0:T(8,128)(2,1)S(1)}, u32[]{:S(2)}, u32[]{:S(2)}) collective-permute-start(bf16[512,384]{1,0:T(8,128)(2,1)S(1)} %get-tuple-element.41.a1), channel_id=1, source_target_pairs={{0,1},{1,2},{2,3},{3,4},{4,5},{5,6},{6,7},{7,0},{8,15},{9,8},{10,9... | collective-permute-start | bytes 1179656 | tf_op jit(solution)/shard_map/ppermute | solution.py:365
  24.6 5.2 %collective-permute-start.5 = (bf16[272,128]{1,0:T(8,128)(2,1)S(1)}, bf16[272,128]{1,0:T(8,128)(2,1)S(1)}, u32[]{:S(2)}, u32[]{:S(2)}) collective-permute-start(bf16[272,128]{1,0:T(8,128)(2,1)S(1)} %get-tuple-element.39.sent_ref), channel_id=1, source_target_pairs={{0,48},{8,56},{16,0},{24,8},{32,16},{40,24},{48,32},{56,40},{64,11... | collective-permute-start | bytes 208904 | tf_op jit(solution)/shard_map/ppermute | solution.py:372
  27.1 5.3 %collective-permute-start.4 = (bf16[272,128]{1,0:T(8,128)(2,1)S(1)}, bf16[272,128]{1,0:T(8,128)(2,1)S(1)}, u32[]{:S(2)}, u32[]{:S(2)}) collective-permute-start(bf16[272,128]{1,0:T(8,128)(2,1)S(1)} %get-tuple-element.39.sent_ref), channel_id=1, source_target_pairs={{0,32},{8,40},{16,48},{24,56},{32,0},{40,8},{48,16},{56,24},{64,96... | collective-permute-start | bytes 208904 | tf_op jit(solution)/shard_map/ppermute | solution.py:372
  27.6 6.1 %collective-permute-start.3 = (bf16[272,128]{1,0:T(8,128)(2,1)S(1)}, bf16[272,128]{1,0:T(8,128)(2,1)S(1)}, u32[]{:S(2)}, u32[]{:S(2)}) collective-permute-start(bf16[272,128]{1,0:T(8,128)(2,1)S(1)} %get-tuple-element.39.sent_ref), channel_id=1, source_target_pairs={{0,16},{8,24},{16,32},{24,40},{32,48},{40,56},{48,0},{56,8},{64,80... | collective-permute-start | bytes 208904 | tf_op jit(solution)/shard_map/ppermute | solution.py:372
  28.3 6.9 %collective-permute-start.12 = (bf16[512,384]{1,0:T(8,128)(2,1)S(1)}, bf16[512,384]{1,0:T(8,128)(2,1)S(1)}, u32[]{:S(2)}, u32[]{:S(2)}) collective-permute-start(bf16[512,384]{1,0:T(8,128)(2,1)S(1)} %collective-permute-done.9), channel_id=1, source_target_pairs={{0,1},{1,2},{2,3},{3,4},{4,5},{5,6},{6,7},{7,0},{8,15},{9,8},{10,9... | collective-permute-start | bytes 1179656 | tf_op jit(solution)/shard_map/ppermute | solution.py:365
  34.4 7.0 %collective-permute-start.11 = (bf16[512,384]{1,0:T(8,128)(2,1)S(1)}, bf16[512,384]{1,0:T(8,128)(2,1)S(1)}, u32[]{:S(2)}, u32[]{:S(2)}) collective-permute-start(bf16[512,384]{1,0:T(8,128)(2,1)S(1)} %get-tuple-element.44.a2), channel_id=1, source_target_pairs={{0,1},{1,2},{2,3},{3,4},{4,5},{5,6},{6,7},{7,0},{8,15},{9,8},{10,9... | collective-permute-start | bytes 1179656 | tf_op jit(solution)/shard_map/ppermute | solution.py:365
  34.5 7.8 %collective-permute-start.8 = (bf16[512,384]{1,0:T(8,128)(2,1)S(1)}, bf16[512,384]{1,0:T(8,128)(2,1)S(1)}, u32[]{:S(2)}, u32[]{:S(2)}) collective-permute-start(bf16[512,384]{1,0:T(8,128)(2,1)S(1)} %collective-permute-done.7), channel_id=1, source_target_pairs={{0,8},{8,0},{16,24},{24,16},{32,40},{40,32},{48,56},{56,48},{64,72... | collective-permute-start | bytes 1179656 | tf_op jit(solution)/shard_map/ppermute | solution.py:372
  35.0 7.4 %collective-permute-start.10 = (bf16[512,384]{1,0:T(8,128)(2,1)S(1)}, bf16[512,384]{1,0:T(8,128)(2,1)S(1)}, u32[]{:S(2)}, u32[]{:S(2)}) collective-permute-start(bf16[512,384]{1,0:T(8,128)(2,1)S(1)} %collective-permute-done.9), channel_id=1, source_target_pairs={{0,8},{8,0},{16,24},{24,16},{32,40},{40,32},{48,56},{56,48},{64,72... | collective-permute-start | bytes 1179656 | tf_op jit(solution)/shard_map/ppermute | solution.py:372
  35.2 11.8 %collective-permute-start.13 = (bf16[512,384]{1,0:T(8,128)(2,1)S(1)}, bf16[512,384]{1,0:T(8,128)(2,1)S(1)}, u32[]{:S(2)}, u32[]{:S(2)}) collective-permute-start(bf16[512,384]{1,0:T(8,128)(2,1)S(1)} %collective-permute-done.12), channel_id=1, source_target_pairs={{0,8},{8,0},{16,24},{24,16},{32,40},{40,32},{48,56},{56,48},{64,72... | collective-permute-start | bytes 1179656 | tf_op jit(solution)/shard_map/ppermute | solution.py:372
  41.4 6.9 %collective-permute-start.14 = (bf16[512,384]{1,0:T(8,128)(2,1)S(1)}, bf16[512,384]{1,0:T(8,128)(2,1)S(1)}, u32[]{:S(2)}, u32[]{:S(2)}) collective-permute-start(bf16[512,384]{1,0:T(8,128)(2,1)S(1)} %collective-permute-done.11.a3), channel_id=1, source_target_pairs={{0,1},{1,2},{2,3},{3,4},{4,5},{5,6},{6,7},{7,0},{8,15},{9,8},{10,9... | collective-permute-start | bytes 1179656 | tf_op jit(solution)/shard_map/ppermute | solution.py:365
  47.7 9.7 %copy-start = (bf16[512,512]{1,0:T(8,128)(2,1)S(1)}, bf16[512,512]{1,0:T(8,128)(2,1)}, u32[]{:S(2)}) copy-start(bf16[512,512]{1,0:T(8,128)(2,1)} %k_ref.5) | copy-start | bytes 1572868
  47.7 9.7 %copy-start.1 = (bf16[512,512]{1,0:T(8,128)(2,1)S(1)}, bf16[512,512]{1,0:T(8,128)(2,1)}, u32[]{:S(2)}) copy-start(bf16[512,512]{1,0:T(8,128)(2,1)} %v_ref.5) | copy-start | bytes 1572868
  47.7 9.7 %copy-start.2 = (bf16[512,512]{1,0:T(8,128)(2,1)S(1)}, bf16[512,512]{1,0:T(8,128)(2,1)}, u32[]{:S(2)}) copy-start(bf16[512,512]{1,0:T(8,128)(2,1)} %q_ref.3) | copy-start | bytes 1572868
  49.3 5.7 %collective-permute-start.15 = (f32[512,128]{1,0:T(8,128)S(1)}, f32[512,128]{1,0:T(8,128)S(1)}, u32[]{:S(2)}, u32[]{:S(2)}) collective-permute-start(f32[512,128]{1,0:T(8,128)S(1)} %get-tuple-element.48.grad_ref), channel_id=1, source_target_pairs={{0,8},{8,0},{16,24},{24,16},{32,40},{40,32},{48,56},{56,48},{64,72... | collective-permute-start | bytes 786440 | tf_op jit(solution)/shard_map/ppermute | solution.py:372
  55.6 3.8 %collective-permute-start.18 = (bf16[256,128]{1,0:T(8,128)(2,1)S(1)}, bf16[256,128]{1,0:T(8,128)(2,1)S(1)}, u32[]{:S(2)}, u32[]{:S(2)}) collective-permute-start(bf16[256,128]{1,0:T(8,128)(2,1)S(1)} %get-tuple-element.50), channel_id=1, source_target_pairs={{0,48},{8,56},{16,0},{24,8},{32,16},{40,24},{48,32},{56,40},{64,11... | collective-permute-start | bytes 196616 | tf_op jit(solution)/shard_map/ppermute | solution.py:372
  56.3 4.7 %collective-permute-start.17 = (bf16[256,128]{1,0:T(8,128)(2,1)S(1)}, bf16[256,128]{1,0:T(8,128)(2,1)S(1)}, u32[]{:S(2)}, u32[]{:S(2)}) collective-permute-start(bf16[256,128]{1,0:T(8,128)(2,1)S(1)} %get-tuple-element.50), channel_id=1, source_target_pairs={{0,32},{8,40},{16,48},{24,56},{32,0},{40,8},{48,16},{56,24},{64,96... | collective-permute-start | bytes 196616 | tf_op jit(solution)/shard_map/ppermute | solution.py:372
  56.8 5.9 %collective-permute-start.16 = (bf16[256,128]{1,0:T(8,128)(2,1)S(1)}, bf16[256,128]{1,0:T(8,128)(2,1)S(1)}, u32[]{:S(2)}, u32[]{:S(2)}) collective-permute-start(bf16[256,128]{1,0:T(8,128)(2,1)S(1)} %get-tuple-element.50), channel_id=1, source_target_pairs={{0,16},{8,24},{16,32},{24,40},{32,48},{40,56},{48,0},{56,8},{64,80... | collective-permute-start | bytes 196616 | tf_op jit(solution)/shard_map/ppermute | solution.py:372
  63.9 7.0 %collective-permute-start.19 = (bf16[272,128]{1,0:T(8,128)(2,1)S(1)}, bf16[272,128]{1,0:T(8,128)(2,1)S(1)}, u32[]{:S(2)}, u32[]{:S(2)}) collective-permute-start(bf16[272,128]{1,0:T(8,128)(2,1)S(1)} %get-tuple-element.58), channel_id=1, source_target_pairs={{0,64},{8,72},{16,80},{24,88},{32,96},{40,104},{48,112},{56,120},{... | collective-permute-start | bytes 208904 | tf_op jit(solution)/shard_map/ppermute | solution.py:372
  65.2 5.7 %collective-permute-start.20 = (bf16[272,128]{1,0:T(8,128)(2,1)S(1)}, bf16[272,128]{1,0:T(8,128)(2,1)S(1)}, u32[]{:S(2)}, u32[]{:S(2)}) collective-permute-start(bf16[272,128]{1,0:T(8,128)(2,1)S(1)} %get-tuple-element.59), channel_id=1, source_target_pairs={{0,128},{8,136},{16,144},{24,152},{32,160},{40,168},{48,176},{56,1... | collective-permute-start | bytes 208904 | tf_op jit(solution)/shard_map/ppermute | solution.py:372
  67.8 3.8 %collective-permute-start.21 = (bf16[272,128]{1,0:T(8,128)(2,1)S(1)}, bf16[272,128]{1,0:T(8,128)(2,1)S(1)}, u32[]{:S(2)}, u32[]{:S(2)}) collective-permute-start(bf16[272,128]{1,0:T(8,128)(2,1)S(1)} %get-tuple-element.60), channel_id=1, source_target_pairs={{0,192},{8,200},{16,208},{24,216},{32,224},{40,232},{48,240},{56,2... | collective-permute-start | bytes 208904 | tf_op jit(solution)/shard_map/ppermute | solution.py:372
  72.7 3.2 %collective-permute-start.22 = (f32[512,128]{1,0:T(8,128)S(1)}, f32[512,128]{1,0:T(8,128)S(1)}, u32[]{:S(2)}, u32[]{:S(2)}) collective-permute-start(f32[512,128]{1,0:T(8,128)S(1)} %get-tuple-element.62.enter_ref), channel_id=1, source_target_pairs={{0,8},{8,0},{16,24},{24,16},{32,40},{40,32},{48,56},{56,48},{64,72... | collective-permute-start | bytes 786440 | tf_op jit(solution)/shard_map/ppermute | solution.py:372

commit v2 on v1

--- a/solution.py
+++ b/solution.py
@@ -13,7 +13,6 @@
 TN = (((0,), (0,)), ((), ()))
 VMEM = pl.BlockSpec(memory_space=pltpu.VMEM)
 ANY = pl.BlockSpec(memory_space=pl.ANY)
-SMEM = pl.BlockSpec(memory_space=pltpu.SMEM)
 
 
 def dot(a, b, dims):
@@ -126,15 +125,15 @@
 
 
 def first_kernel(
-    place_ref, w_hbm, c_hbm, q_hbm, ld_ref, a1, b1, a2, b2,
+    w_hbm, c_hbm, q_hbm, ld_ref, a1, b1, a2, b2, a3,
     acc_ref, w_ref, qw_ref, row_ref, col_ref, near_ref, c_ref, q_ref, sems,
 ):
-    z, side = place_ref[0], 1 - 2 * place_ref[1]
+    z, side = lax.axis_index("head"), 1 - 2 * core_index()
     rows, width = c_ref.shape
     heads = ld_ref.shape[0]
-    targets = [near_ref.at[i] for i in range(5)] + [w_ref.at[i] for i in range(3)]
+    targets = [near_ref.at[i] for i in range(6)] + [w_ref.at[i] for i in range(2)]
     copies = [pltpu.make_async_copy(c_hbm, c_ref, sems.at[8]), pltpu.make_async_copy(q_hbm, q_ref, sems.at[9])]
-    for i, (offset, target) in enumerate(zip((0, -1, 1, -2, 2, -3, 3, 4), targets)):
+    for i, (offset, target) in enumerate(zip((0, -1, 1, -2, 2, -3, 4, 3), targets)):
         at = lax.rem(z + offset * side + 8, 8) * width
         copies.append(pltpu.make_async_copy(w_hbm.at[:, pl.ds(pl.multiple_of(at, 128), width)], target, sems.at[i]))
     for copy in copies:
@@ -155,26 +154,44 @@
     for part in range(2):
         at = pl.ds(part * half, half)
         acc = dot(c_ref[at, :], near_ref[0], NT)
-        for i, ref in enumerate((a1, b1, a2, b2)):
+        for i, ref in enumerate((a1, b1, a2, b2, a3)):
             acc += dot(ref[at, :], near_ref[i + 1], NT)
         acc_ref[at, :] = acc
 
 
-def second_kernel(acc_ref, a3, b3, w_ref, out_ref):
+def second_kernel(acc_ref, a4, w_ref, out_ref):
     half = acc_ref.shape[0] // 2
     for part in range(2):
         at = pl.ds(part * half, half)
-        out_ref[at, :] = acc_ref[at, :] + dot(a3[at, :], w_ref[0], NT) + dot(b3[at, :], w_ref[1], NT)
-
-
-def late_kernel(heads, acc_ref, a4, w_ref, qw_ref, ga_ref, state_ref):
+        out_ref[at, :] = acc_ref[at, :] + dot(a4[at, :], w_ref[0], NT)
+
+
+def late_kernel(heads, acc_ref, a4, b3, w_ref, qw_ref, ga_ref, state_ref):
     half = acc_ref.shape[0] // 2
     for part in range(2):
         at = pl.ds(part * half, half)
-        ga_ref[at, :] = (acc_ref[at, :] + dot(a4[at, :], w_ref[2], NT)).astype(jnp.bfloat16)
+        ga_ref[at, :] = (
+            acc_ref[at, :] + dot(a4[at, :], w_ref[0], NT) + dot(b3[at, :], w_ref[1], NT)
+        ).astype(jnp.bfloat16)
     for h in range(heads):
         both = dot(qw_ref[h], ga_ref[:, h * DH : (h + 1) * DH], NN)
         state_ref[pl.ds(h * DH, DH), :] = both[:DH] + both[DH:]
+
+
+def gate_kernel(x_ref, tie_ref, out_ref):
+    out_ref[...] = x_ref[...]
+
+
+def core_index():
+    return lax.rem(lax.axis_index("seq"), 2)
+
+
+def x_index():
+    return lax.rem(lax.div(lax.axis_index("seq"), 2), 4)
+
+
+def y_index():
+    return lax.div(lax.axis_index("seq"), 8)
 
 
 def one_row(tile, i):
@@ -196,9 +213,9 @@
     return one_row(tail, 3 * j) + one_row(tail, 3 * j + 1) + one_row(tail, 3 * j + 2)
 
 
-def chip_key_kernel(heads, place_ref, key_ref, key_other, tie_ref, sent_ref, chip_ref, tied_ref):
+def chip_key_kernel(heads, key_ref, key_other, tie_ref, sent_ref, chip_ref, tied_ref):
     tied_ref[...] = tie_ref[...]
-    core = place_ref[1]
+    core = core_index()
     pair = heads // 2
     first = core == 0
     totals = []
@@ -214,8 +231,8 @@
     sent_ref[pl.ds(pair * DH, 16), :] = tail_of(totals)
 
 
-def chip_grad_kernel(heads, place_ref, key_ref, key_other, grad_ref, grad_other, sent_ref, chip_ref):
-    core = place_ref[1]
+def chip_grad_kernel(heads, key_ref, key_other, grad_ref, grad_other, sent_ref, chip_ref):
+    core = core_index()
     pair = heads // 2
     first = core == 0
     for j in range(pair):
@@ -240,13 +257,14 @@
     return sum(t * flag((low < p) & (p < high)) for t, p in zip(totals, place))
 
 
-def row_key_kernel(pair, place_ref, sent_ref, chip_ref, r1, r2, r3, tie_ref, in_ref, whole_ref, table_ref, tied_ref):
+def row_key_kernel(pair, sent_ref, chip_ref, r1, r2, r3, tie_ref, in_ref, whole_ref, table_ref, tail_ref, tied_ref):
     tied_ref[...] = tie_ref[...]
-    x = place_ref[2]
+    x = x_index()
     n = pair * DH
     refs = (sent_ref, r1, r2, r3)
     place = chip_places(x)
     tails = [ref[pl.ds(n, 16), :] for ref in refs]
+    row_totals = []
     for j in range(pair):
         totals = [total_in(tail, j) for tail in tails]
         at = pl.ds(j * DH, DH)
@@ -258,41 +276,41 @@
             inside += jnp.exp(between(totals, place, place[d], x)) * flag(place[d] < x) * state
         in_ref[at, :] = inside
         whole_ref[at, :] = whole
-        lines = totals + [
-            jnp.exp(between(totals, place, -1, x)), jnp.exp(between(totals, place, x, 4)), sum(totals), jnp.zeros_like(totals[0])
-        ]
+        lines = [jnp.exp(between(totals, place, -1, p)) for p in place]
+        lines += [jnp.exp(between(totals, place, x, p)) * flag(p > x) for p in place[1:]]
+        lines += [jnp.exp(between(totals, place, -1, x)), jnp.exp(between(totals, place, x, 4))]
         for i, line in enumerate(lines):
-            table_ref[pl.ds(8 * j + i, 1), :] = line
-
-
-def row_grad_kernel(pair, place_ref, chip_ref, r1, r2, r3, whole_key, table_ref, tie_ref, in_ref, s1, s2, s3, tied_ref):
-    x, y = place_ref[2], place_ref[3]
+            table_ref[pl.ds(16 * j + i, 1), :] = line
+        table_ref[pl.ds(16 * j + 9, 7), :] = jnp.zeros((7, DH), jnp.float32)
+        row_totals.append(sum(totals))
+    tail_ref[...] = tail_of(row_totals)
+
+
+def row_grad_kernel(pair, chip_ref, r1, r2, r3, whole_key, table_ref, tail_ref, _, in_ref, s1, s2, s3):
+    y = y_index()
     n = pair * DH
-    refs = (chip_ref, r1, r2, r3)
-    place = chip_places(x)
-    row_totals = []
+    refs = (r1, r2, r3)
+
+    def line(j, i):
+        return table_ref[pl.ds(16 * j + i, 1), :]
+
     for j in range(pair):
-        totals = [table_ref[pl.ds(8 * j + d, 1), :] for d in range(4)]
-        row_totals.append(table_ref[pl.ds(8 * j + 6, 1), :])
         at = pl.ds(j * DH, DH)
         inside = 0.0
-        whole = jnp.exp(between(totals, place, -1, x)) * chip_ref[at, :]
-        for d in range(1, 4):
+        whole = line(j, 0) * chip_ref[at, :]
+        for d in range(3):
             state = refs[d][at, :].astype(jnp.float32)
-            whole += jnp.exp(between(totals, place, -1, place[d])) * state
-            inside += jnp.exp(between(totals, place, x, place[d])) * flag(place[d] > x) * state
+            whole += line(j, 1 + d) * state
+            inside += line(j, 4 + d) * state
         in_ref[at, :] = inside
         for dy, ref in ((1, s1), (2, s2), (3, s3)):
             ref[at, :] = jnp.where(y + dy < 4, whole_key[at, :], whole).astype(jnp.bfloat16)
-    tail = tail_of(row_totals)
     for ref in (s1, s2, s3):
-        ref[pl.ds(n, 16), :] = tail
-    tied_ref[...] = tie_ref[...]
-
-
-def enter_kernel(pair, place_ref, key_in, grad_in, table_ref, r1, r2, r3, tie_ref, enter_ref, tied_ref):
-    tied_ref[...] = tie_ref[...]
-    y = place_ref[3]
+        ref[pl.ds(n, 16), :] = tail_ref[...]
+
+
+def enter_kernel(pair, key_in, grad_in, table_ref, r1, r2, r3, _, enter_ref):
+    y = y_index()
     n = pair * DH
     refs = (r1, r2, r3)
     place = [lax.rem(y - d + 4, 4) for d in (1, 2, 3)]
@@ -301,7 +319,7 @@
         totals = [total_in(tail, j) for tail in tails]
         at = pl.ds(j * DH, DH)
         key, grad = key_in[at, :], grad_in[at, :]
-        into, out = table_ref[pl.ds(8 * j + 4, 1), :], table_ref[pl.ds(8 * j + 5, 1), :]
+        into, out = table_ref[pl.ds(16 * j + 7, 1), :], table_ref[pl.ds(16 * j + 8, 1), :]
         for d in range(3):
             p = place[d]
             gap = sum(t * flag(((p < q) & (q < y)) | ((y < q) & (q < p))) for t, q in zip(totals, place))
@@ -313,9 +331,9 @@
         enter_ref[pl.ds((pair + j) * DH, DH), :] = grad
 
 
-def close_kernel(heads, place_ref, enter_ref, enter_other, key_other, grad_other, ga_ref, k_ref, v_ref, *refs):
+def close_kernel(heads, enter_ref, enter_other, key_other, grad_other, ga_ref, k_ref, v_ref, *refs):
     halves, outs, room, sems = (refs[:5], refs[5:10]), refs[10:13], refs[13], refs[14]
-    core = place_ref[1]
+    core = core_index()
     pair = heads // 2
     first = core == 0
     copies = []
@@ -338,13 +356,20 @@
         hi, lo = pieces(so, 2)
         so = jnp.concatenate([hi, lo], axis=0)
         so_wide = jnp.concatenate([hi, lo], axis=1)
-        room[0, h] = dq[:, mine] + start_w[:, mine] * fold(dot(ga_ref[:, cols], si, NT))
-        room[1, h] = dk[:, mine] + end_w[:, mine] * fold(dot(v_ref[:, cols], so, NT))
-        room[2, h] = dv[:, mine] + end_w[:, mine] * fold(dot(k_ref[:, cols], so_wide, NN))
-        for j in range(3):
-            copy = pltpu.make_async_copy(room.at[j, h], outs[j].at[:, pl.ds(h * DH, DH)], sems.at[j, h])
-            copy.start()
-            copies.append(copy)
+        for part in range(4):
+            step = ga_ref.shape[0] // 4
+            rows = pl.ds(part * step, step)
+            room[0, h, rows] = dq[rows, mine] + start_w[rows, mine] * fold(dot(ga_ref[rows, cols], si, NT))
+            room[1, h, rows] = dk[rows, mine] + end_w[rows, mine] * fold(dot(v_ref[rows, cols], so, NT))
+            room[2, h, rows] = dv[rows, mine] + end_w[rows, mine] * fold(dot(k_ref[rows, cols], so_wide, NN))
+            if part % 2:
+                at = pl.ds((part - 1) * step, 2 * step)
+                for j in range(3):
+                    copy = pltpu.make_async_copy(
+                        room.at[j, h, at], outs[j].at[at, pl.ds(h * DH, DH)], sems.at[j, 2 * h + part // 2]
+                    )
+                    copy.start()
+                    copies.append(copy)
     for copy in copies:
         copy.wait()
 
@@ -353,9 +378,6 @@
     rows, width = queries.shape
     heads = log_decay.shape[0]
     pair = heads // 2
-    z = lax.axis_index("head")
-    seq = lax.axis_index("seq")
-    place = jnp.stack([z, seq % 2, (seq // 2) % 4, seq // 8]).astype(jnp.int32)
 
     def along_z(array):
         pairs = []
@@ -390,44 +412,43 @@
     key_other = other(key_own)
     sent, chip, a1 = call(
         functools.partial(chip_key_kernel, heads), (bf16(pair * DH + 16, DH), f32(pair * DH, DH), bf16(*grad_out.shape)),
-        place, key_own, key_other, a1, specs=[SMEM] + [VMEM] * 3,
+        key_own, key_other, a1, specs=[VMEM] * 3,
     )
     from_x = [along_seq(sent, dx=d) for d in (2, 1, 3)]
     from_x = [from_x[1], from_x[0], from_x[2]]
     a2 = along_z(a1)
     b1_here = other(b1)
     b2 = along_z(b1)
-    key_in, key_row, table, a2 = call(
+    b2_here = other(b2)
+    key_in, key_row, table, tail, b2 = call(
         functools.partial(row_key_kernel, pair),
-        (f32(pair * DH, DH), f32(pair * DH, DH), f32(8 * pair, DH), bf16(*grad_out.shape)),
-        place, sent, chip, *from_x, a2, specs=[SMEM] + [VMEM] * 6,
+        (f32(pair * DH, DH), f32(pair * DH, DH), f32(16 * pair, DH), bf16(16, DH), bf16(*grad_out.shape)),
+        sent, chip, *from_x, b2, specs=[VMEM] * 6,
     )
     a3 = along_z(a2)
-    b2_here = other(b2)
     b3 = along_z(b2)
     a4 = along_z(a3)
-    b3_here = other(b3)
 
     qd = grad_out.shape[1]
     acc, w, qw, row, col = call(
         first_kernel,
-        (f32(rows, width), bf16(3, width, qd), bf16(heads, 2 * DH, rows), f32(heads, rows), f32(rows, heads)),
-        place, in_hbm(out_weight), in_hbm(grad_out), in_hbm(queries), log_decay, a1, b1_here, a2, b2_here,
-        specs=[SMEM] + [ANY] * 3 + [VMEM] * 5,
+        (f32(rows, width), bf16(2, width, qd), bf16(heads, 2 * DH, rows), f32(heads, rows), f32(rows, heads)),
+        in_hbm(out_weight), in_hbm(grad_out), in_hbm(queries), log_decay, a1, b1_here, a2, b2_here, a3,
+        specs=[ANY] * 3 + [VMEM] * 6,
         scratch=[
-            pltpu.VMEM((5, width, qd), jnp.bfloat16), pltpu.VMEM((rows, qd), jnp.bfloat16),
+            pltpu.VMEM((6, width, qd), jnp.bfloat16), pltpu.VMEM((rows, qd), jnp.bfloat16),
             pltpu.VMEM((rows, width), jnp.bfloat16), pltpu.SemaphoreType.DMA((10,)),
         ],
     )
-    (acc,) = call(second_kernel, (f32(rows, width),), acc, a3, b3_here, w)
+    b3_here = other(call(gate_kernel, (bf16(*grad_out.shape),), b3, acc)[0])
     ga, grad_own = call(
-        functools.partial(late_kernel, heads), (bf16(rows, width), f32(heads * DH, DH)), acc, a4, w, qw
+        functools.partial(late_kernel, heads), (bf16(rows, width), f32(heads * DH, DH)), acc, a4, b3_here, w, qw
     )
 
     grad_other = other(grad_own)
     sent, chip = call(
         functools.partial(chip_grad_kernel, heads), (bf16(pair * DH, DH), f32(pair * DH, DH)),
-        place, key_own, key_other, grad_own, grad_other, specs=[SMEM] + [VMEM] * 4,
+        key_own, key_other, grad_own, grad_other, specs=[VMEM] * 4,
     )
     from_x = [along_seq(sent, dx=d) for d in (2, 1, 3)]
     from_x = [from_x[1], from_x[0], from_x[2]]
@@ -441,27 +462,27 @@
 
     low, tie = local_part(0)
     high, tie_high = local_part(pair)
-    grad_in, *sent, _ = call(
+    grad_in, *sent = call(
         functools.partial(row_grad_kernel, pair),
-        (f32(pair * DH, DH),) + (bf16(pair * DH + 16, DH),) * 3 + (f32(8, DH),),
-        place, chip, *from_x, key_row, table, tie, specs=[SMEM] + [VMEM] * 7,
+        (f32(pair * DH, DH),) + (bf16(pair * DH + 16, DH),) * 3,
+        chip, *from_x, key_row, table, tail, tie, specs=[VMEM] * 8,
     )
     from_y = [along_seq(sent[d - 1], dy=d) for d in (2, 1, 3)]
     from_y = [from_y[1], from_y[0], from_y[2]]
-    enter, _ = call(
-        functools.partial(enter_kernel, pair), (f32(2 * pair * DH, DH), f32(8, DH)),
-        place, key_in, grad_in, table, *from_y, tie_high, specs=[SMEM] + [VMEM] * 7,
+    (enter,) = call(
+        functools.partial(enter_kernel, pair), (f32(2 * pair * DH, DH),),
+        key_in, grad_in, table, *from_y, tie_high, specs=[VMEM] * 7,
     )
     enter_other = other(enter)
 
     return pl.pallas_call(
         functools.partial(close_kernel, heads),
         out_shape=(f32(rows, width),) * 3,
-        in_specs=[SMEM] + [VMEM] * 17,
+        in_specs=[VMEM] * 17,
         out_specs=(ANY,) * 3,
-        scratch_shapes=[pltpu.VMEM((3, heads, rows, DH), jnp.float32), pltpu.SemaphoreType.DMA((3, heads))],
+        scratch_shapes=[pltpu.VMEM((3, heads, rows, DH), jnp.float32), pltpu.SemaphoreType.DMA((3, 2 * heads))],
         compiler_params=pltpu.CompilerParams(vmem_limit_bytes=24 * 2**20),
-    )(place, enter, enter_other, key_other, grad_other, ga, keys, values, *low, *high)
+    )(enter, enter_other, key_other, grad_other, ga, keys, values, *low, *high)
 
 
 def solution(mesh):

time: 79.1 us -> 69.5 us (0.88)
  waiting for transfers between devices: 23.7 us -> 16 us
  Pallas kernels: 19.1 us -> 14 us
  starting transfers between devices: 34.4 us -> 37.7 us
    pallas_call x11, Pallas kernels: 16.3 us -> 11.8 us  [call(): pl.pallas_call(kernel, out_shape=outs, in_specs=specs or [VMEM] * len(arg...]
    ppermute x7, waiting for transfers between devices: 10.5 us -> 6.58 us  [along_z(): return lax.ppermute(array, ('seq', 'head'), pairs)]
    ppermute x16, waiting for transfers between devices: 13.2 us -> 9.47 us  [along_seq(): return lax.ppermute(array, 'seq', pairs)]
    ppermute x7, starting transfers between devices: 11.9 us -> 14 us  [along_z(): return lax.ppermute(array, ('seq', 'head'), pairs)]
    ppermute x16, starting transfers between devices: 22.5 us -> 23.7 us  [along_seq(): return lax.ppermute(array, 'seq', pairs)]
  transfers between devices with their start and end apart: 23 -> 23, of which waited for: 13 -> 13; matrix products, arithmetic and copies ran while one was open for 0% -> 0% of each run, Pallas kernels for 14% -> 15%
where the time goes in v2:
time: 69.5 us; the launch traced here: 69.4 us
  starting transfers between devices  37.7 us (54%)
  waiting for transfers between devices  16 us (23%)
  Pallas kernels  14 us (20%)
  between operations  0.93 us (1%)
  local copies, waits for them, and re-layouts  0.72 us (1%)
    ppermute x16, starting transfers between devices, along_seq(): return lax.ppermute(array, 'seq', pairs)  23.7 us
    ppermute x7, starting transfers between devices, along_z(): return lax.ppermute(array, ('seq', 'head'), pairs)  14 us
    pallas_call x11, Pallas kernels, call(): pl.pallas_call(kernel, out_shape=outs, in_specs=specs or [VMEM] * len(arg...  11.8 us
    ppermute x16, waiting for transfers between devices, along_seq(): return lax.ppermute(array, 'seq', pairs)  9.47 us
    ppermute x7, waiting for transfers between devices, along_z(): return lax.ppermute(array, ('seq', 'head'), pairs)  6.58 us
    pallas_call x1, Pallas kernels, local(): pl.pallas_call(functools.partial(close_kernel, heads), out_shape=(f32(row...  2.15 us
  transfers between devices with their start and end apart: 23, of which 13 were waited for; matrix products, arithmetic and copies ran while one was open for 0% of the time, Pallas kernels for 15%

profile of v2, /device:TPU:1, one launch (start us, length us, event | category | flops | bytes accessed | tf_op | source)
XLA Modules:
  0.0 69.4 jit_solution(17285858350220304755)
XLA Ops:
  0.6 3.3 %collective-permute-start = (bf16[512,384]{1,0:T(8,128)(2,1)}, bf16[512,384]{1,0:T(8,128)(2,1)S(1)}, u32[]{:S(2)}, u32[]{:S(2)}) collective-permute-start(bf16[512,384]{1,0:T(8,128)(2,1)} %c_hbm.1), channel_id=1, source_target_pairs={{0,8},{8,0},{16,24},{24,16},{32,40},{40,32},{48,56},{56,48},{64,72... | collective-permute-start | bytes 1179656 | tf_op jit(solution)/shard_map/ppermute | solution.py:394
  4.0 3.8 %collective-permute-start.2 = (bf16[512,384]{1,0:T(8,128)(2,1)}, bf16[512,384]{1,0:T(8,128)(2,1)S(1)}, u32[]{:S(2)}, u32[]{:S(2)}) collective-permute-start(bf16[512,384]{1,0:T(8,128)(2,1)} %c_hbm.1), channel_id=1, source_target_pairs={{0,1},{1,2},{2,3},{3,4},{4,5},{5,6},{6,7},{7,0},{8,15},{9,8},{10,9... | collective-permute-start | bytes 1179656 | tf_op jit(solution)/shard_map/ppermute | solution.py:387
  8.5 1.8 %shard_map.85 = (f32[520,128]{1,0:T(8,128)S(1)}, bf16[512,384]{1,0:T(8,128)(2,1)S(1)}) custom-call(bf16[512,512]{1,0:T(8,128)(2,1)} %k_ref.5, bf16[512,512]{1,0:T(8,128)(2,1)} %v_ref.5, f32[4,512]{1,0:T(4,128)S(1)} %copy-done.3, bf16[512,384]{1,0:T(8,128)(2,1)S(1)} %collective-permute-done.tie_ref), custom_call_target="tpu_custom_call" | custom-call | tf_op jit(solution)/shard_map/pallas_call | solution.py:32
  10.3 1.6 %collective-permute-start.6 = (bf16[512,384]{1,0:T(8,128)(2,1)S(1)}, bf16[512,384]{1,0:T(8,128)(2,1)S(1)}, u32[]{:S(2)}, u32[]{:S(2)}) collective-permute-start(bf16[512,384]{1,0:T(8,128)(2,1)S(1)} %get-tuple-element.41), channel_id=1, source_target_pairs={{0,1},{1,2},{2,3},{3,4},{4,5},{5,6},{6,7},{7,0},{8,15},{9,8},{10,9... | collective-permute-start | bytes 1179656 | tf_op jit(solution)/shard_map/ppermute | solution.py:387
  11.9 0.9 %collective-permute-done.2.tie_ref = bf16[512,384]{1,0:T(8,128)(2,1)S(1)} collective-permute-done((bf16[512,384]{1,0:T(8,128)(2,1)}, bf16[512,384]{1,0:T(8,128)(2,1)S(1)}, u32[]{:S(2)}, u32[]{:S(2)}) %collective-permute-start.2) | collective-permute-done | bytes 393248 | tf_op jit(solution)/shard_map/ppermute | solution.py:387
  13.5 2.5 %collective-permute-start.9 = (bf16[512,384]{1,0:T(8,128)(2,1)S(1)}, bf16[512,384]{1,0:T(8,128)(2,1)S(1)}, u32[]{:S(2)}, u32[]{:S(2)}) collective-permute-start(bf16[512,384]{1,0:T(8,128)(2,1)S(1)} %get-tuple-element.43.a1), channel_id=1, source_target_pairs={{0,1},{1,2},{2,3},{3,4},{4,5},{5,6},{6,7},{7,0},{8,15},{9,8},{10,9... | collective-permute-start | bytes 1179656 | tf_op jit(solution)/shard_map/ppermute | solution.py:387
  16.0 1.3 %collective-permute-done.6 = bf16[512,384]{1,0:T(8,128)(2,1)S(1)} collective-permute-done((bf16[512,384]{1,0:T(8,128)(2,1)S(1)}, bf16[512,384]{1,0:T(8,128)(2,1)S(1)}, u32[]{:S(2)}, u32[]{:S(2)}) %collective-permute-start.6) | collective-permute-done | bytes 393248 | tf_op jit(solution)/shard_map/ppermute | solution.py:387
  17.3 2.8 %collective-permute-start.7 = (bf16[512,384]{1,0:T(8,128)(2,1)S(1)}, bf16[512,384]{1,0:T(8,128)(2,1)S(1)}, u32[]{:S(2)}, u32[]{:S(2)}) collective-permute-start(bf16[512,384]{1,0:T(8,128)(2,1)S(1)} %collective-permute-done.6), channel_id=1, source_target_pairs={{0,1},{1,2},{2,3},{3,4},{4,5},{5,6},{6,7},{7,0},{8,15},{9,8},{10,9... | collective-permute-start | bytes 1179656 | tf_op jit(solution)/shard_map/ppermute | solution.py:387
  20.1 2.5 %collective-permute-start.5 = (bf16[272,128]{1,0:T(8,128)(2,1)S(1)}, bf16[272,128]{1,0:T(8,128)(2,1)S(1)}, u32[]{:S(2)}, u32[]{:S(2)}) collective-permute-start(bf16[272,128]{1,0:T(8,128)(2,1)S(1)} %get-tuple-element.39.sent_ref), channel_id=1, source_target_pairs={{0,48},{8,56},{16,0},{24,8},{32,16},{40,24},{48,32},{56,40},{64,11... | collective-permute-start | bytes 208904 | tf_op jit(solution)/shard_map/ppermute | solution.py:394
  23.7 1.5 %collective-permute-done.5.r3 = bf16[272,128]{1,0:T(8,128)(2,1)S(1)} collective-permute-done((bf16[272,128]{1,0:T(8,128)(2,1)S(1)}, bf16[272,128]{1,0:T(8,128)(2,1)S(1)}, u32[]{:S(2)}, u32[]{:S(2)}) %collective-permute-start.5) | collective-permute-done | bytes 69664 | tf_op jit(solution)/shard_map/ppermute | solution.py:394
  25.2 1.0 %collective-permute-start.11 = (bf16[512,384]{1,0:T(8,128)(2,1)S(1)}, bf16[512,384]{1,0:T(8,128)(2,1)S(1)}, u32[]{:S(2)}, u32[]{:S(2)}) collective-permute-start(bf16[512,384]{1,0:T(8,128)(2,1)S(1)} %collective-permute-done.9.a2), channel_id=1, source_target_pairs={{0,1},{1,2},{2,3},{3,4},{4,5},{5,6},{6,7},{7,0},{8,15},{9,8},{10,9... | collective-permute-start | bytes 1179656 | tf_op jit(solution)/shard_map/ppermute | solution.py:387
  26.1 1.4 %collective-permute-start.10 = (bf16[512,384]{1,0:T(8,128)(2,1)S(1)}, bf16[512,384]{1,0:T(8,128)(2,1)S(1)}, u32[]{:S(2)}, u32[]{:S(2)}) collective-permute-start(bf16[512,384]{1,0:T(8,128)(2,1)S(1)} %collective-permute-done.7.tie_ref), channel_id=1, source_target_pairs={{0,8},{8,0},{16,24},{24,16},{32,40},{40,32},{48,56},{56,48},{64,72... | collective-permute-start | bytes 1179656 | tf_op jit(solution)/shard_map/ppermute | solution.py:394
  29.1 3.0 %collective-permute-done.11.a3 = bf16[512,384]{1,0:T(8,128)(2,1)S(1)} collective-permute-done((bf16[512,384]{1,0:T(8,128)(2,1)S(1)}, bf16[512,384]{1,0:T(8,128)(2,1)S(1)}, u32[]{:S(2)}, u32[]{:S(2)}) %collective-permute-start.11) | collective-permute-done | bytes 393248 | tf_op jit(solution)/shard_map/ppermute | solution.py:387
  32.1 1.9 %collective-permute-start.12 = (bf16[512,384]{1,0:T(8,128)(2,1)S(1)}, bf16[512,384]{1,0:T(8,128)(2,1)S(1)}, u32[]{:S(2)}, u32[]{:S(2)}) collective-permute-start(bf16[512,384]{1,0:T(8,128)(2,1)S(1)} %collective-permute-done.11.a3), channel_id=1, source_target_pairs={{0,1},{1,2},{2,3},{3,4},{4,5},{5,6},{6,7},{7,0},{8,15},{9,8},{10,9... | collective-permute-start | bytes 1179656 | tf_op jit(solution)/shard_map/ppermute | solution.py:387
  34.0 4.3 %shard_map.88 = (f32[512,512]{1,0:T(8,128)S(1)}, bf16[2,512,384]{2,1,0:T(8,128)(2,1)S(1)}, bf16[4,256,512]{2,1,0:T(8,128)(2,1)S(1)}, f32[4,512]{1,0:T(4,128)S(1)}, f32[512,4]{1,0:T(8,128)S(1)}) custom-call(bf16[512,3072]{1,0:T(8,128)(2,1)} %w_hbm.1, bf16[512,384]{1,0:T(8,128)(2,1)} %c_hbm.1, bf16[512,512]{1,0:T(8,128)(2,1)} %q_ref.3, ...), custom_call_target="tpu_custom_call" | custom-call | tf_op jit(solution)/shard_map/pallas_call | solution.py:32
  38.4 0.8 %collective-permute-start.14 = (bf16[512,384]{1,0:T(8,128)(2,1)S(1)}, bf16[512,384]{1,0:T(8,128)(2,1)S(1)}, u32[]{:S(2)}, u32[]{:S(2)}) collective-permute-start(bf16[512,384]{1,0:T(8,128)(2,1)S(1)} %shard_map.89), channel_id=1, source_target_pairs={{0,8},{8,0},{16,24},{24,16},{32,40},{40,32},{48,56},{56,48},{64,72... | collective-permute-start | bytes 1179656 | tf_op jit(solution)/shard_map/ppermute | solution.py:394
  39.2 1.4 %collective-permute-done.12.a4 = bf16[512,384]{1,0:T(8,128)(2,1)S(1)} collective-permute-done((bf16[512,384]{1,0:T(8,128)(2,1)S(1)}, bf16[512,384]{1,0:T(8,128)(2,1)S(1)}, u32[]{:S(2)}, u32[]{:S(2)}) %collective-permute-start.12) | collective-permute-done | bytes 393248 | tf_op jit(solution)/shard_map/ppermute | solution.py:387
  40.5 1.2 %shard_map.90 = (bf16[512,512]{1,0:T(8,128)(2,1)S(1)}, f32[512,128]{1,0:T(8,128)S(1)}) custom-call(f32[512,512]{1,0:T(8,128)S(1)} %get-tuple-element.44.tie_ref.acc_ref, bf16[512,384]{1,0:T(8,128)(2,1)S(1)} %collective-permute-done.12.a4, bf16[512,384]{1,0:T(8,128)(2,1)S(1)} %collective-permute-done.14.b3, bf16[2,512,384]{2,1,0:T(8,128)(2,1)S(1)} %get-tuple-element.46.w_ref, ...), custom_call_target="tpu_custom_call" | custom-call | tf_op jit(solution)/shard_map/pallas_call | solution.py:32
  41.7 3.2 %collective-permute-start.15 = (f32[512,128]{1,0:T(8,128)S(1)}, f32[512,128]{1,0:T(8,128)S(1)}, u32[]{:S(2)}, u32[]{:S(2)}) collective-permute-start(f32[512,128]{1,0:T(8,128)S(1)} %get-tuple-element.48.grad_ref), channel_id=1, source_target_pairs={{0,8},{8,0},{16,24},{24,16},{32,40},{40,32},{48,56},{56,48},{64,72... | collective-permute-start | bytes 786440 | tf_op jit(solution)/shard_map/ppermute | solution.py:394
  44.9 1.2 %collective-permute-done.15.grad_other = f32[512,128]{1,0:T(8,128)S(1)} collective-permute-done((f32[512,128]{1,0:T(8,128)S(1)}, f32[512,128]{1,0:T(8,128)S(1)}, u32[]{:S(2)}, u32[]{:S(2)}) %collective-permute-start.15) | collective-permute-done | bytes 262176 | tf_op jit(solution)/shard_map/ppermute | solution.py:394
  46.1 3.5 %collective-permute-start.18 = (bf16[256,128]{1,0:T(8,128)(2,1)S(1)}, bf16[256,128]{1,0:T(8,128)(2,1)S(1)}, u32[]{:S(2)}, u32[]{:S(2)}) collective-permute-start(bf16[256,128]{1,0:T(8,128)(2,1)S(1)} %get-tuple-element.50), channel_id=1, source_target_pairs={{0,48},{8,56},{16,0},{24,8},{32,16},{40,24},{48,32},{56,40},{64,11... | collective-permute-start | bytes 196616 | tf_op jit(solution)/shard_map/ppermute | solution.py:394
  50.3 2.0 %shard_map.92 = (f32[512,256]{1,0:T(8,128)S(1)}, f32[512,256]{1,0:T(8,128)S(1)}, f32[512,256]{1,0:T(8,128)S(1)}, f32[512,256]{1,0:T(8,128)S(1)}, f32[512,256]{1,0:T(8,128)S(1)}, /*index=5*/f32[8,128]{1,0:T(8,128)S(1)}) custom-call(bf16[512,512]{1,0:T(8,128)(2,1)S(1)} %copy-done.2, bf16[512,512]{1,0:T(8,128)(2,1)S(1)} %copy-done, ...), custom_call_target="tpu_custom_call" | custom-call | tf_op jit(solution)/shard_map/pallas_call | solution.py:32
  52.3 2.0 %collective-permute-done.17.r2 = bf16[256,128]{1,0:T(8,128)(2,1)S(1)} collective-permute-done((bf16[256,128]{1,0:T(8,128)(2,1)S(1)}, bf16[256,128]{1,0:T(8,128)(2,1)S(1)}, u32[]{:S(2)}, u32[]{:S(2)}) %collective-permute-start.17) | collective-permute-done | bytes 65568 | tf_op jit(solution)/shard_map/ppermute | solution.py:394
  54.3 1.1 %collective-permute-done.16.r1 = bf16[256,128]{1,0:T(8,128)(2,1)S(1)} collective-permute-done((bf16[256,128]{1,0:T(8,128)(2,1)S(1)}, bf16[256,128]{1,0:T(8,128)(2,1)S(1)}, u32[]{:S(2)}, u32[]{:S(2)}) %collective-permute-start.16) | collective-permute-done | bytes 65568 | tf_op jit(solution)/shard_map/ppermute | solution.py:394
  55.6 1.4 %collective-permute-start.19 = (bf16[272,128]{1,0:T(8,128)(2,1)S(1)}, bf16[272,128]{1,0:T(8,128)(2,1)S(1)}, u32[]{:S(2)}, u32[]{:S(2)}) collective-permute-start(bf16[272,128]{1,0:T(8,128)(2,1)S(1)} %get-tuple-element.59), channel_id=1, source_target_pairs={{0,64},{8,72},{16,80},{24,88},{32,96},{40,104},{48,112},{56,120},{... | collective-permute-start | bytes 208904 | tf_op jit(solution)/shard_map/ppermute | solution.py:394
  56.9 2.6 %collective-permute-start.20 = (bf16[272,128]{1,0:T(8,128)(2,1)S(1)}, bf16[272,128]{1,0:T(8,128)(2,1)S(1)}, u32[]{:S(2)}, u32[]{:S(2)}) collective-permute-start(bf16[272,128]{1,0:T(8,128)(2,1)S(1)} %get-tuple-element.60), channel_id=1, source_target_pairs={{0,128},{8,136},{16,144},{24,152},{32,160},{40,168},{48,176},{56,1... | collective-permute-start | bytes 208904 | tf_op jit(solution)/shard_map/ppermute | solution.py:394
  59.5 1.1 %collective-permute-start.21 = (bf16[272,128]{1,0:T(8,128)(2,1)S(1)}, bf16[272,128]{1,0:T(8,128)(2,1)S(1)}, u32[]{:S(2)}, u32[]{:S(2)}) collective-permute-start(bf16[272,128]{1,0:T(8,128)(2,1)S(1)} %get-tuple-element.61), channel_id=1, source_target_pairs={{0,192},{8,200},{16,208},{24,216},{32,224},{40,232},{48,240},{56,2... | collective-permute-start | bytes 208904 | tf_op jit(solution)/shard_map/ppermute | solution.py:394
  60.6 2.0 %shard_map.94 = (f32[512,256]{1,0:T(8,128)S(1)}, f32[512,256]{1,0:T(8,128)S(1)}, f32[512,256]{1,0:T(8,128)S(1)}, f32[512,256]{1,0:T(8,128)S(1)}, f32[512,256]{1,0:T(8,128)S(1)}, /*index=5*/f32[8,128]{1,0:T(8,128)S(1)}) custom-call(bf16[512,512]{1,0:T(8,128)(2,1)S(1)} %copy-done.2, bf16[512,512]{1,0:T(8,128)(2,1)S(1)} %copy-done, ...), custom_call_target="tpu_custom_call" | custom-call | tf_op jit(solution)/shard_map/pallas_call | solution.py:32
  62.7 0.9 %collective-permute-done.21.r3 = bf16[272,128]{1,0:T(8,128)(2,1)S(1)} collective-permute-done((bf16[272,128]{1,0:T(8,128)(2,1)S(1)}, bf16[272,128]{1,0:T(8,128)(2,1)S(1)}, u32[]{:S(2)}, u32[]{:S(2)}) %collective-permute-start.21) | collective-permute-done | bytes 69664 | tf_op jit(solution)/shard_map/ppermute | solution.py:394
  63.8 2.1 %collective-permute-start.22 = (f32[512,128]{1,0:T(8,128)S(1)}, f32[512,128]{1,0:T(8,128)S(1)}, u32[]{:S(2)}, u32[]{:S(2)}) collective-permute-start(f32[512,128]{1,0:T(8,128)S(1)} %shard_map.95.enter_ref), channel_id=1, source_target_pairs={{0,8},{8,0},{16,24},{24,16},{32,40},{40,32},{48,56},{56,48},{64,72... | collective-permute-start | bytes 786440 | tf_op jit(solution)/shard_map/ppermute | solution.py:394
  65.9 1.2 %collective-permute-done.22.enter_other = f32[512,128]{1,0:T(8,128)S(1)} collective-permute-done((f32[512,128]{1,0:T(8,128)S(1)}, f32[512,128]{1,0:T(8,128)S(1)}, u32[]{:S(2)}, u32[]{:S(2)}) %collective-permute-start.22) | collective-permute-done | bytes 262176 | tf_op jit(solution)/shard_map/ppermute | solution.py:394
  67.1 2.2 %shard_map.96 = (f32[512,512]{1,0:T(8,128)}, f32[512,512]{1,0:T(8,128)}, f32[512,512]{1,0:T(8,128)}) custom-call(f32[512,128]{1,0:T(8,128)S(1)} %shard_map.95.enter_ref, f32[512,128]{1,0:T(8,128)S(1)} %collective-permute-done.22.enter_other, f32[520,128]{1,0:T(8,128)S(1)} %collective-permute-done.1.key_other, ...), custom_call_target="tpu_custom_call" | custom-call | tf_op jit(solution)/shard_map/pallas_call | solution.py:478
  (36 shorter events, 5.1 us)
Async XLA Ops:
  0.6 7.2 %collective-permute-start = (bf16[512,384]{1,0:T(8,128)(2,1)}, bf16[512,384]{1,0:T(8,128)(2,1)S(1)}, u32[]{:S(2)}, u32[]{:S(2)}) collective-permute-start(bf16[512,384]{1,0:T(8,128)(2,1)} %c_hbm.1), channel_id=1, source_target_pairs={{0,8},{8,0},{16,24},{24,16},{32,40},{40,32},{48,56},{56,48},{64,72... | collective-permute-start | bytes 1179656 | tf_op jit(solution)/shard_map/ppermute | solution.py:394
  4.0 8.9 %collective-permute-start.2 = (bf16[512,384]{1,0:T(8,128)(2,1)}, bf16[512,384]{1,0:T(8,128)(2,1)S(1)}, u32[]{:S(2)}, u32[]{:S(2)}) collective-permute-start(bf16[512,384]{1,0:T(8,128)(2,1)} %c_hbm.1), channel_id=1, source_target_pairs={{0,1},{1,2},{2,3},{3,4},{4,5},{5,6},{6,7},{7,0},{8,15},{9,8},{10,9... | collective-permute-start | bytes 1179656 | tf_op jit(solution)/shard_map/ppermute | solution.py:387
  7.8 0.7 %copy-start.3 = (f32[4,512]{1,0:T(4,128)S(1)}, f32[4,512]{1,0:T(4,128)}, u32[]{:S(2)}) copy-start(f32[4,512]{1,0:T(4,128)} %ld_ref.3) | copy-start | bytes 24580
  8.5 25.5 %copy-start.4 = (f32[4,512]{1,0:T(4,128)S(1)}, f32[4,512]{1,0:T(4,128)}, u32[]{:S(2)}) copy-start(f32[4,512]{1,0:T(4,128)} %ld_ref.3) | copy-start | bytes 24580
  10.3 7.0 %collective-permute-start.6 = (bf16[512,384]{1,0:T(8,128)(2,1)S(1)}, bf16[512,384]{1,0:T(8,128)(2,1)S(1)}, u32[]{:S(2)}, u32[]{:S(2)}) collective-permute-start(bf16[512,384]{1,0:T(8,128)(2,1)S(1)} %get-tuple-element.41), channel_id=1, source_target_pairs={{0,1},{1,2},{2,3},{3,4},{4,5},{5,6},{6,7},{7,0},{8,15},{9,8},{10,9... | collective-permute-start | bytes 1179656 | tf_op jit(solution)/shard_map/ppermute | solution.py:387
  11.9 1.5 %collective-permute-start.1 = (f32[520,128]{1,0:T(8,128)S(1)}, f32[520,128]{1,0:T(8,128)S(1)}, u32[]{:S(2)}, u32[]{:S(2)}) collective-permute-start(f32[520,128]{1,0:T(8,128)S(1)} %get-tuple-element.38.key_ref), channel_id=1, source_target_pairs={{0,8},{8,0},{16,24},{24,16},{32,40},{40,32},{48,56},{56,48},{64,72... | collective-permute-start | bytes 798728 | tf_op jit(solution)/shard_map/ppermute | solution.py:394
  13.5 11.7 %collective-permute-start.9 = (bf16[512,384]{1,0:T(8,128)(2,1)S(1)}, bf16[512,384]{1,0:T(8,128)(2,1)S(1)}, u32[]{:S(2)}, u32[]{:S(2)}) collective-permute-start(bf16[512,384]{1,0:T(8,128)(2,1)S(1)} %get-tuple-element.43.a1), channel_id=1, source_target_pairs={{0,1},{1,2},{2,3},{3,4},{4,5},{5,6},{6,7},{7,0},{8,15},{9,8},{10,9... | collective-permute-start | bytes 1179656 | tf_op jit(solution)/shard_map/ppermute | solution.py:387
  17.3 8.9 %collective-permute-start.7 = (bf16[512,384]{1,0:T(8,128)(2,1)S(1)}, bf16[512,384]{1,0:T(8,128)(2,1)S(1)}, u32[]{:S(2)}, u32[]{:S(2)}) collective-permute-start(bf16[512,384]{1,0:T(8,128)(2,1)S(1)} %collective-permute-done.6), channel_id=1, source_target_pairs={{0,1},{1,2},{2,3},{3,4},{4,5},{5,6},{6,7},{7,0},{8,15},{9,8},{10,9... | collective-permute-start | bytes 1179656 | tf_op jit(solution)/shard_map/ppermute | solution.py:387
  20.1 5.1 %collective-permute-start.5 = (bf16[272,128]{1,0:T(8,128)(2,1)S(1)}, bf16[272,128]{1,0:T(8,128)(2,1)S(1)}, u32[]{:S(2)}, u32[]{:S(2)}) collective-permute-start(bf16[272,128]{1,0:T(8,128)(2,1)S(1)} %get-tuple-element.39.sent_ref), channel_id=1, source_target_pairs={{0,48},{8,56},{16,0},{24,8},{32,16},{40,24},{48,32},{56,40},{64,11... | collective-permute-start | bytes 208904 | tf_op jit(solution)/shard_map/ppermute | solution.py:394
  22.5 5.2 %collective-permute-start.4 = (bf16[272,128]{1,0:T(8,128)(2,1)S(1)}, bf16[272,128]{1,0:T(8,128)(2,1)S(1)}, u32[]{:S(2)}, u32[]{:S(2)}) collective-permute-start(bf16[272,128]{1,0:T(8,128)(2,1)S(1)} %get-tuple-element.39.sent_ref), channel_id=1, source_target_pairs={{0,32},{8,40},{16,48},{24,56},{32,0},{40,8},{48,16},{56,24},{64,96... | collective-permute-start | bytes 208904 | tf_op jit(solution)/shard_map/ppermute | solution.py:394
  23.1 5.4 %collective-permute-start.3 = (bf16[272,128]{1,0:T(8,128)(2,1)S(1)}, bf16[272,128]{1,0:T(8,128)(2,1)S(1)}, u32[]{:S(2)}, u32[]{:S(2)}) collective-permute-start(bf16[272,128]{1,0:T(8,128)(2,1)S(1)} %get-tuple-element.39.sent_ref), channel_id=1, source_target_pairs={{0,16},{8,24},{16,32},{24,40},{32,48},{40,56},{48,0},{56,8},{64,80... | collective-permute-start | bytes 208904 | tf_op jit(solution)/shard_map/ppermute | solution.py:394
  25.2 8.8 %collective-permute-start.8 = (bf16[512,384]{1,0:T(8,128)(2,1)S(1)}, bf16[512,384]{1,0:T(8,128)(2,1)S(1)}, u32[]{:S(2)}, u32[]{:S(2)}) collective-permute-start(bf16[512,384]{1,0:T(8,128)(2,1)S(1)} %collective-permute-done.6), channel_id=1, source_target_pairs={{0,8},{8,0},{16,24},{24,16},{32,40},{40,32},{48,56},{56,48},{64,72... | collective-permute-start | bytes 1179656 | tf_op jit(solution)/shard_map/ppermute | solution.py:394
  25.2 6.9 %collective-permute-start.11 = (bf16[512,384]{1,0:T(8,128)(2,1)S(1)}, bf16[512,384]{1,0:T(8,128)(2,1)S(1)}, u32[]{:S(2)}, u32[]{:S(2)}) collective-permute-start(bf16[512,384]{1,0:T(8,128)(2,1)S(1)} %collective-permute-done.9.a2), channel_id=1, source_target_pairs={{0,1},{1,2},{2,3},{3,4},{4,5},{5,6},{6,7},{7,0},{8,15},{9,8},{10,9... | collective-permute-start | bytes 1179656 | tf_op jit(solution)/shard_map/ppermute | solution.py:387
  26.1 7.8 %collective-permute-start.10 = (bf16[512,384]{1,0:T(8,128)(2,1)S(1)}, bf16[512,384]{1,0:T(8,128)(2,1)S(1)}, u32[]{:S(2)}, u32[]{:S(2)}) collective-permute-start(bf16[512,384]{1,0:T(8,128)(2,1)S(1)} %collective-permute-done.7.tie_ref), channel_id=1, source_target_pairs={{0,8},{8,0},{16,24},{24,16},{32,40},{40,32},{48,56},{56,48},{64,72... | collective-permute-start | bytes 1179656 | tf_op jit(solution)/shard_map/ppermute | solution.py:394
  28.7 9.6 %collective-permute-start.13 = (bf16[512,384]{1,0:T(8,128)(2,1)S(1)}, bf16[512,384]{1,0:T(8,128)(2,1)S(1)}, u32[]{:S(2)}, u32[]{:S(2)}) collective-permute-start(bf16[512,384]{1,0:T(8,128)(2,1)S(1)} %get-tuple-element.45), channel_id=1, source_target_pairs={{0,1},{1,2},{2,3},{3,4},{4,5},{5,6},{6,7},{7,0},{8,15},{9,8},{10,9... | collective-permute-start | bytes 1179656 | tf_op jit(solution)/shard_map/ppermute | solution.py:387
  32.1 8.4 %collective-permute-start.12 = (bf16[512,384]{1,0:T(8,128)(2,1)S(1)}, bf16[512,384]{1,0:T(8,128)(2,1)S(1)}, u32[]{:S(2)}, u32[]{:S(2)}) collective-permute-start(bf16[512,384]{1,0:T(8,128)(2,1)S(1)} %collective-permute-done.11.a3), channel_id=1, source_target_pairs={{0,1},{1,2},{2,3},{3,4},{4,5},{5,6},{6,7},{7,0},{8,15},{9,8},{10,9... | collective-permute-start | bytes 1179656 | tf_op jit(solution)/shard_map/ppermute | solution.py:387
  38.3 12.0 %copy-start = (bf16[512,512]{1,0:T(8,128)(2,1)S(1)}, bf16[512,512]{1,0:T(8,128)(2,1)}, u32[]{:S(2)}) copy-start(bf16[512,512]{1,0:T(8,128)(2,1)} %k_ref.5) | copy-start | bytes 1572868
  38.3 12.0 %copy-start.1 = (bf16[512,512]{1,0:T(8,128)(2,1)S(1)}, bf16[512,512]{1,0:T(8,128)(2,1)}, u32[]{:S(2)}) copy-start(bf16[512,512]{1,0:T(8,128)(2,1)} %v_ref.5) | copy-start | bytes 1572868
  38.3 12.0 %copy-start.2 = (bf16[512,512]{1,0:T(8,128)(2,1)S(1)}, bf16[512,512]{1,0:T(8,128)(2,1)}, u32[]{:S(2)}) copy-start(bf16[512,512]{1,0:T(8,128)(2,1)} %q_ref.3) | copy-start | bytes 1572868
  38.4 2.2 %collective-permute-start.14 = (bf16[512,384]{1,0:T(8,128)(2,1)S(1)}, bf16[512,384]{1,0:T(8,128)(2,1)S(1)}, u32[]{:S(2)}, u32[]{:S(2)}) collective-permute-start(bf16[512,384]{1,0:T(8,128)(2,1)S(1)} %shard_map.89), channel_id=1, source_target_pairs={{0,8},{8,0},{16,24},{24,16},{32,40},{40,32},{48,56},{56,48},{64,72... | collective-permute-start | bytes 1179656 | tf_op jit(solution)/shard_map/ppermute | solution.py:394
  41.7 4.4 %collective-permute-start.15 = (f32[512,128]{1,0:T(8,128)S(1)}, f32[512,128]{1,0:T(8,128)S(1)}, u32[]{:S(2)}, u32[]{:S(2)}) collective-permute-start(f32[512,128]{1,0:T(8,128)S(1)} %get-tuple-element.48.grad_ref), channel_id=1, source_target_pairs={{0,8},{8,0},{16,24},{24,16},{32,40},{40,32},{48,56},{56,48},{64,72... | collective-permute-start | bytes 786440 | tf_op jit(solution)/shard_map/ppermute | solution.py:394
  46.1 6.2 %collective-permute-start.18 = (bf16[256,128]{1,0:T(8,128)(2,1)S(1)}, bf16[256,128]{1,0:T(8,128)(2,1)S(1)}, u32[]{:S(2)}, u32[]{:S(2)}) collective-permute-start(bf16[256,128]{1,0:T(8,128)(2,1)S(1)} %get-tuple-element.50), channel_id=1, source_target_pairs={{0,48},{8,56},{16,0},{24,8},{32,16},{40,24},{48,32},{56,40},{64,11... | collective-permute-start | bytes 196616 | tf_op jit(solution)/shard_map/ppermute | solution.py:394
  49.6 4.7 %collective-permute-start.17 = (bf16[256,128]{1,0:T(8,128)(2,1)S(1)}, bf16[256,128]{1,0:T(8,128)(2,1)S(1)}, u32[]{:S(2)}, u32[]{:S(2)}) collective-permute-start(bf16[256,128]{1,0:T(8,128)(2,1)S(1)} %get-tuple-element.50), channel_id=1, source_target_pairs={{0,32},{8,40},{16,48},{24,56},{32,0},{40,8},{48,16},{56,24},{64,96... | collective-permute-start | bytes 196616 | tf_op jit(solution)/shard_map/ppermute | solution.py:394
  49.6 5.9 %collective-permute-start.16 = (bf16[256,128]{1,0:T(8,128)(2,1)S(1)}, bf16[256,128]{1,0:T(8,128)(2,1)S(1)}, u32[]{:S(2)}, u32[]{:S(2)}) collective-permute-start(bf16[256,128]{1,0:T(8,128)(2,1)S(1)} %get-tuple-element.50), channel_id=1, source_target_pairs={{0,16},{8,24},{16,32},{24,40},{32,48},{40,56},{48,0},{56,8},{64,80... | collective-permute-start | bytes 196616 | tf_op jit(solution)/shard_map/ppermute | solution.py:394
  55.6 7.1 %collective-permute-start.19 = (bf16[272,128]{1,0:T(8,128)(2,1)S(1)}, bf16[272,128]{1,0:T(8,128)(2,1)S(1)}, u32[]{:S(2)}, u32[]{:S(2)}) collective-permute-start(bf16[272,128]{1,0:T(8,128)(2,1)S(1)} %get-tuple-element.59), channel_id=1, source_target_pairs={{0,64},{8,72},{16,80},{24,88},{32,96},{40,104},{48,112},{56,120},{... | collective-permute-start | bytes 208904 | tf_op jit(solution)/shard_map/ppermute | solution.py:394
  56.9 5.8 %collective-permute-start.20 = (bf16[272,128]{1,0:T(8,128)(2,1)S(1)}, bf16[272,128]{1,0:T(8,128)(2,1)S(1)}, u32[]{:S(2)}, u32[]{:S(2)}) collective-permute-start(bf16[272,128]{1,0:T(8,128)(2,1)S(1)} %get-tuple-element.60), channel_id=1, source_target_pairs={{0,128},{8,136},{16,144},{24,152},{32,160},{40,168},{48,176},{56,1... | collective-permute-start | bytes 208904 | tf_op jit(solution)/shard_map/ppermute | solution.py:394
  59.5 4.1 %collective-permute-start.21 = (bf16[272,128]{1,0:T(8,128)(2,1)S(1)}, bf16[272,128]{1,0:T(8,128)(2,1)S(1)}, u32[]{:S(2)}, u32[]{:S(2)}) collective-permute-start(bf16[272,128]{1,0:T(8,128)(2,1)S(1)} %get-tuple-element.61), channel_id=1, source_target_pairs={{0,192},{8,200},{16,208},{24,216},{32,224},{40,232},{48,240},{56,2... | collective-permute-start | bytes 208904 | tf_op jit(solution)/shard_map/ppermute | solution.py:394
  63.8 3.3 %collective-permute-start.22 = (f32[512,128]{1,0:T(8,128)S(1)}, f32[512,128]{1,0:T(8,128)S(1)}, u32[]{:S(2)}, u32[]{:S(2)}) collective-permute-start(f32[512,128]{1,0:T(8,128)S(1)} %shard_map.95.enter_ref), channel_id=1, source_target_pairs={{0,8},{8,0},{16,24},{24,16},{32,40},{40,32},{48,56},{56,48},{64,72... | collective-permute-start | bytes 786440 | tf_op jit(solution)/shard_map/ppermute | solution.py:394

commit v3 on v2

--- a/solution.py
+++ b/solution.py
@@ -65,16 +65,17 @@
     return sum(dot(since, p, NT) for p in pieces(ld, 3))
 
 
-def open_kernel(heads, k_hbm, v_hbm, ld_ref, tie_ref, state_ref, tied_ref, k_ref, v_ref, sems):
-    copies = [pltpu.make_async_copy(src, dst, sems.at[i]) for i, (src, dst) in enumerate(((k_hbm, k_ref), (v_hbm, v_ref)))]
+def open_kernel(heads, k_hbm, v_hbm, ld_hbm, tie_ref, state_ref, tied_ref, k_ref, v_ref, ld_ref, sems):
+    copies = [pltpu.make_async_copy(src, dst, sems.at[i]) for i, (src, dst) in enumerate(((ld_hbm, ld_ref), (k_hbm, k_ref), (v_hbm, v_ref)))]
     for copy in copies:
         copy.start()
     tied_ref[...] = tie_ref[...]
     n = k_ref.shape[0]
+    copies[0].wait()
     row, total = running(ld_ref[...])
     state_ref[pl.ds(heads * DH, heads), :] = total
     state_ref[pl.ds(heads * DH + heads, 8 - heads), :] = jnp.zeros((8 - heads, DH), jnp.float32)
-    for copy in copies:
+    for copy in copies[1:]:
         copy.wait()
     for h in range(heads):
         cols = slice(h * DH, (h + 1) * DH)
@@ -82,6 +83,10 @@
         hi, lo = pieces(kt, 2)
         v = v_ref[:, cols]
         state_ref[pl.ds(h * DH, DH), :] = dot(hi, v, NN) + dot(lo, v, NN)
+
+
+def head_columns(position):
+    return pl.ds(pl.multiple_of(lax.rem(core_index() * 2 + position, 4) * DH, DH), DH)
 
 
 def local_kernel(heads, first, q_ref, k_ref, v_ref, ga_ref, row_ref, col_ref, dq_ref, dk_ref, dv_ref, start_ref, end_ref, tie_ref):
@@ -92,7 +97,7 @@
     keep = s <= t
     for i in range(heads):
         h = first + i
-        cols, to = slice(h * DH, (h + 1) * DH), slice(i * DH, (i + 1) * DH)
+        cols, to = head_columns(h), slice(i * DH, (i + 1) * DH)
         col = col_ref[:, h : h + 1]
         start_ref[:, to] = jnp.broadcast_to(jnp.exp(col) * (1.0 / DH), (n, DH))
         end_ref[:, to] = jnp.broadcast_to(jnp.exp(row_ref[h : h + 1, n - 1 : n] - col) * (1.0 / DH), (n, DH))
@@ -125,22 +130,27 @@
 
 
 def first_kernel(
-    w_hbm, c_hbm, q_hbm, ld_ref, a1, b1, a2, b2, a3,
-    acc_ref, w_ref, qw_ref, row_ref, col_ref, near_ref, c_ref, q_ref, sems,
+    w_hbm, c_hbm, q_hbm, ld_hbm, a1, b1, a2, b2, a3,
+    acc_ref, w_ref, qw_ref, row_ref, col_ref, near_ref, c_ref, q_ref, ld_ref, sems,
 ):
     z, side = lax.axis_index("head"), 1 - 2 * core_index()
     rows, width = c_ref.shape
     heads = ld_ref.shape[0]
     targets = [near_ref.at[i] for i in range(6)] + [w_ref.at[i] for i in range(2)]
+    decays = pltpu.make_async_copy(ld_hbm, ld_ref, sems.at[10])
+    decays.start()
     copies = [pltpu.make_async_copy(c_hbm, c_ref, sems.at[8]), pltpu.make_async_copy(q_hbm, q_ref, sems.at[9])]
     for i, (offset, target) in enumerate(zip((0, -1, 1, -2, 2, -3, 4, 3), targets)):
         at = lax.rem(z + offset * side + 8, 8) * width
         copies.append(pltpu.make_async_copy(w_hbm.at[:, pl.ds(pl.multiple_of(at, 128), width)], target, sems.at[i]))
     for copy in copies:
         copy.start()
+    decays.wait()
     row, _ = running(ld_ref[...])
-    row_ref[...] = row
-    col_ref[...] = running_columns(ld_ref[...])
+    col = running_columns(ld_ref[...])
+    swap = core_index() == 1
+    row_ref[...] = jnp.where(swap, jnp.concatenate([row[heads // 2 :], row[: heads // 2]], axis=0), row)
+    col_ref[...] = jnp.where(swap, jnp.concatenate([col[:, heads // 2 :], col[:, : heads // 2]], axis=1), col)
     copies[1].wait()
     for h in range(heads):
         qt = q_ref[:, h * DH : (h + 1) * DH].T.astype(jnp.float32) * jnp.exp(row[h : h + 1, :])
@@ -249,8 +259,8 @@
     return jnp.where(condition, 1.0, 0.0)
 
 
-def chip_places(x):
-    return [lax.rem(x - d + 4, 4) for d in range(4)]
+def places(x):
+    return [jnp.bitwise_xor(x, d) for d in range(4)]
 
 
 def between(totals, place, low, high):
@@ -262,7 +272,7 @@
     x = x_index()
     n = pair * DH
     refs = (sent_ref, r1, r2, r3)
-    place = chip_places(x)
+    place = places(x)
     tails = [ref[pl.ds(n, 16), :] for ref in refs]
     row_totals = []
     for j in range(pair):
@@ -286,7 +296,7 @@
     tail_ref[...] = tail_of(row_totals)
 
 
-def row_grad_kernel(pair, chip_ref, r1, r2, r3, whole_key, table_ref, tail_ref, _, in_ref, s1, s2, s3):
+def row_grad_kernel(pair, chip_ref, r1, r3, r2, whole_key, table_ref, tail_ref, _, in_ref, s1, s2, s3):
     y = y_index()
     n = pair * DH
     refs = (r1, r2, r3)
@@ -304,16 +314,16 @@
             inside += line(j, 4 + d) * state
         in_ref[at, :] = inside
         for dy, ref in ((1, s1), (2, s2), (3, s3)):
-            ref[at, :] = jnp.where(y + dy < 4, whole_key[at, :], whole).astype(jnp.bfloat16)
+            ref[at, :] = jnp.where(jnp.bitwise_xor(y, dy) > y, whole_key[at, :], whole).astype(jnp.bfloat16)
     for ref in (s1, s2, s3):
         ref[pl.ds(n, 16), :] = tail_ref[...]
 
 
-def enter_kernel(pair, key_in, grad_in, table_ref, r1, r2, r3, _, enter_ref):
+def enter_kernel(pair, key_in, grad_in, table_ref, r2, r1, r3, _, enter_ref):
     y = y_index()
     n = pair * DH
     refs = (r1, r2, r3)
-    place = [lax.rem(y - d + 4, 4) for d in (1, 2, 3)]
+    place = places(y)[1:]
     tails = [ref[pl.ds(n, 16), :] for ref in refs]
     for j in range(pair):
         totals = [total_in(tail, j) for tail in tails]
@@ -331,45 +341,69 @@
         enter_ref[pl.ds((pair + j) * DH, DH), :] = grad
 
 
-def close_kernel(heads, enter_ref, enter_other, key_other, grad_other, ga_ref, k_ref, v_ref, *refs):
-    halves, outs, room, sems = (refs[:5], refs[5:10]), refs[10:13], refs[13], refs[14]
+def closed(first, i, part, enter_ref, key_other, grad_other, ga_ref, k_ref, v_ref, start_w, end_w, dq, dk, dv, states):
     core = core_index()
+    heads = key_other.shape[0] // DH
     pair = heads // 2
-    first = core == 0
-    copies = []
+    cols = head_columns(first + i)
+    if i not in states:
+        h = lax.rem(core * pair + first + i, heads)
+        key = enter_ref[pl.ds(i * DH, DH), :]
+        grad = enter_ref[pl.ds((pair + i) * DH, DH), :]
+        decay = jnp.exp(one_row(key_other[heads * DH :, :], h))
+        si = jnp.where(core == 0, key, decay * key + key_other[cols, :])
+        so = jnp.where(core == 0, decay * grad + grad_other[cols, :], grad)
+        hi, lo = pieces(so, 2)
+        states[i] = jnp.concatenate(pieces(si, 2), axis=0), jnp.concatenate([hi, lo], axis=0), jnp.concatenate([hi, lo], axis=1)
+    si, so, so_wide = states[i]
+    mine = slice(i * DH, (i + 1) * DH)
+    step = ga_ref.shape[0] // 4
+    rows = pl.ds(part * step, step)
 
     def fold(x):
         return x[:, :DH] + x[:, DH:]
 
-    for h in range(heads):
-        start_w, end_w, dq, dk, dv = halves[h // pair]
-        i = h % pair
-        at, low = pl.ds(i * DH, DH), pl.ds((pair + i) * DH, DH)
-        cols, mine = slice(h * DH, (h + 1) * DH), slice(i * DH, (i + 1) * DH)
-        here = core == h // pair
-        key = jnp.where(here, enter_ref[at, :], enter_other[at, :])
-        grad = jnp.where(here, enter_ref[low, :], enter_other[low, :])
-        decay = jnp.exp(key_other[pl.ds(heads * DH + h, 1), :])
-        si = jnp.where(first, key, decay * key + key_other[pl.ds(h * DH, DH), :])
-        so = jnp.where(first, decay * grad + grad_other[pl.ds(h * DH, DH), :], grad)
-        si = jnp.concatenate(pieces(si, 2), axis=0)
-        hi, lo = pieces(so, 2)
-        so = jnp.concatenate([hi, lo], axis=0)
-        so_wide = jnp.concatenate([hi, lo], axis=1)
+    return (
+        dq[rows, mine] + start_w[rows, mine] * fold(dot(ga_ref[rows, cols], si, NT)),
+        dk[rows, mine] + end_w[rows, mine] * fold(dot(v_ref[rows, cols], so, NT)),
+        dv[rows, mine] + end_w[rows, mine] * fold(dot(k_ref[rows, cols], so_wide, NN)),
+    )
+
+
+def own_kernel(first, *refs):
+    *inputs, out_ref = refs
+    step = out_ref.shape[2] // 4
+    states = {}
+    for i in range(out_ref.shape[1]):
         for part in range(4):
-            step = ga_ref.shape[0] // 4
-            rows = pl.ds(part * step, step)
-            room[0, h, rows] = dq[rows, mine] + start_w[rows, mine] * fold(dot(ga_ref[rows, cols], si, NT))
-            room[1, h, rows] = dk[rows, mine] + end_w[rows, mine] * fold(dot(v_ref[rows, cols], so, NT))
-            room[2, h, rows] = dv[rows, mine] + end_w[rows, mine] * fold(dot(k_ref[rows, cols], so_wide, NN))
+            for j, value in enumerate(closed(first, i, part, *inputs, states)):
+                out_ref[j, i, pl.ds(part * step, step)] = value
+
+
+def rest_kernel(first, *refs):
+    *inputs, own_ref, gq_ref, gk_ref, gv_ref, room, sems = refs
+    outs = (gq_ref, gk_ref, gv_ref)
+    pair, n = own_ref.shape[1:3]
+    step = n // 4
+    copies = []
+
+    def send(src, j, position, at, sem):
+        copy = pltpu.make_async_copy(src, outs[j].at[at, head_columns(position)], sem)
+        copy.start()
+        copies.append(copy)
+
+    for i in range(pair):
+        for j in range(3):
+            send(own_ref.at[j, i], j, i, pl.ds(0, n), sems.at[j, i])
+    states = {}
+    for i in range(pair):
+        for part in range(4):
+            for j, value in enumerate(closed(first, i, part, *inputs, states)):
+                room[j, i, pl.ds(part * step, step)] = value
             if part % 2:
                 at = pl.ds((part - 1) * step, 2 * step)
                 for j in range(3):
-                    copy = pltpu.make_async_copy(
-                        room.at[j, h, at], outs[j].at[at, pl.ds(h * DH, DH)], sems.at[j, 2 * h + part // 2]
-                    )
-                    copy.start()
-                    copies.append(copy)
+                    send(room.at[j, i, at], j, first + i, at, sems.at[j, pair + 2 * i + part // 2])
     for copy in copies:
         copy.wait()
 
@@ -390,7 +424,7 @@
         pairs = []
         for i in range(32):
             a, b, c = i // 8, (i // 2) % 4, i % 2
-            pairs.append((i, ((a + dy) % 4) * 8 + ((b + dx) % 4) * 2 + (1 - c if flip else c)))
+            pairs.append((i, (a ^ dy) * 8 + (b ^ dx) * 2 + (1 - c if flip else c)))
         return lax.ppermute(array, "seq", pairs)
 
     def other(array):
@@ -400,26 +434,27 @@
         return pltpu.with_memory_space_constraint(array, pltpu.HBM)
 
     b0 = other(grad_out)
-    key_own, b0 = call(
-        functools.partial(open_kernel, heads), (f32(heads * DH + 8, DH), bf16(*grad_out.shape)),
-        in_hbm(keys), in_hbm(values), log_decay, b0,
-        specs=[ANY] * 2 + [VMEM] * 2,
-        scratch=[pltpu.VMEM((rows, width), jnp.bfloat16)] * 2 + [pltpu.SemaphoreType.DMA((2,))],
+    tie0 = jnp.zeros((8, DH), jnp.float32)
+    key_own, _ = call(
+        functools.partial(open_kernel, heads), (f32(heads * DH + 8, DH), f32(8, DH)),
+        in_hbm(keys), in_hbm(values), in_hbm(log_decay), tie0,
+        specs=[ANY] * 3 + [VMEM],
+        scratch=[pltpu.VMEM((rows, width), jnp.bfloat16)] * 2 + [pltpu.VMEM((heads, rows), jnp.float32), pltpu.SemaphoreType.DMA((3,))],
     )
     a1 = along_z(grad_out)
     b1 = along_z(b0)
 
     key_other = other(key_own)
-    sent, chip, a1 = call(
+    sent, chip, b1 = call(
         functools.partial(chip_key_kernel, heads), (bf16(pair * DH + 16, DH), f32(pair * DH, DH), bf16(*grad_out.shape)),
-        key_own, key_other, a1, specs=[VMEM] * 3,
+        key_own, key_other, b1, specs=[VMEM] * 3,
     )
     from_x = [along_seq(sent, dx=d) for d in (2, 1, 3)]
     from_x = [from_x[1], from_x[0], from_x[2]]
     a2 = along_z(a1)
-    b1_here = other(b1)
     b2 = along_z(b1)
     b2_here = other(b2)
+    b1_here = other(call(gate_kernel, (bf16(*grad_out.shape),), b1, b2)[0])
     key_in, key_row, table, tail, b2 = call(
         functools.partial(row_key_kernel, pair),
         (f32(pair * DH, DH), f32(pair * DH, DH), f32(16 * pair, DH), bf16(16, DH), bf16(*grad_out.shape)),
@@ -433,11 +468,11 @@
     acc, w, qw, row, col = call(
         first_kernel,
         (f32(rows, width), bf16(2, width, qd), bf16(heads, 2 * DH, rows), f32(heads, rows), f32(rows, heads)),
-        in_hbm(out_weight), in_hbm(grad_out), in_hbm(queries), log_decay, a1, b1_here, a2, b2_here, a3,
-        specs=[ANY] * 3 + [VMEM] * 6,
+        in_hbm(out_weight), in_hbm(grad_out), in_hbm(queries), in_hbm(log_decay), a1, b1_here, a2, b2_here, a3,
+        specs=[ANY] * 4 + [VMEM] * 5,
         scratch=[
             pltpu.VMEM((6, width, qd), jnp.bfloat16), pltpu.VMEM((rows, qd), jnp.bfloat16),
-            pltpu.VMEM((rows, width), jnp.bfloat16), pltpu.SemaphoreType.DMA((10,)),
+            pltpu.VMEM((rows, width), jnp.bfloat16), pltpu.VMEM((heads, rows), jnp.float32), pltpu.SemaphoreType.DMA((11,)),
         ],
     )
     b3_here = other(call(gate_kernel, (bf16(*grad_out.shape),), b3, acc)[0])
@@ -465,24 +500,27 @@
     grad_in, *sent = call(
         functools.partial(row_grad_kernel, pair),
         (f32(pair * DH, DH),) + (bf16(pair * DH + 16, DH),) * 3,
-        chip, *from_x, key_row, table, tail, tie, specs=[VMEM] * 8,
+        chip, from_x[0], from_x[2], from_x[1], key_row, table, tail, tie, specs=[VMEM] * 8,
     )
     from_y = [along_seq(sent[d - 1], dy=d) for d in (2, 1, 3)]
     from_y = [from_y[1], from_y[0], from_y[2]]
     (enter,) = call(
         functools.partial(enter_kernel, pair), (f32(2 * pair * DH, DH),),
-        key_in, grad_in, table, *from_y, tie_high, specs=[VMEM] * 7,
+        key_in, grad_in, table, from_y[1], from_y[0], from_y[2], tie_high, specs=[VMEM] * 7,
     )
     enter_other = other(enter)
 
+    (own,) = call(
+        functools.partial(own_kernel, 0), (f32(3, pair, rows, DH),), enter, key_other, grad_other, ga, keys, values, *low
+    )
     return pl.pallas_call(
-        functools.partial(close_kernel, heads),
+        functools.partial(rest_kernel, pair),
         out_shape=(f32(rows, width),) * 3,
-        in_specs=[VMEM] * 17,
+        in_specs=[VMEM] * 12,
         out_specs=(ANY,) * 3,
-        scratch_shapes=[pltpu.VMEM((3, heads, rows, DH), jnp.float32), pltpu.SemaphoreType.DMA((3, 2 * heads))],
+        scratch_shapes=[pltpu.VMEM((3, pair, rows, DH), jnp.float32), pltpu.SemaphoreType.DMA((3, 3 * pair))],
         compiler_params=pltpu.CompilerParams(vmem_limit_bytes=24 * 2**20),
-    )(enter, enter_other, key_other, grad_other, ga, keys, values, *low, *high)
+    )(enter_other, key_other, grad_other, ga, keys, values, *high, own)
 
 
 def solution(mesh):

time: 69.5 us -> 66.2 us (0.953)
  waiting for transfers between devices: 16 us -> 12.3 us
  starting transfers between devices: 37.7 us -> 38.5 us
  local copies, waits for them, and re-layouts: 0.72 us -> 0.02 us
    ppermute x16, waiting for transfers between devices: 9.47 us -> 5.68 us  [along_seq(): return lax.ppermute(array, 'seq', pairs)]
    ppermute x7, starting transfers between devices: 14 us -> 15.8 us  [along_z(): return lax.ppermute(array, ('seq', 'head'), pairs)]
    ppermute x16, starting transfers between devices: 23.7 us -> 22.6 us  [along_seq(): return lax.ppermute(array, 'seq', pairs)]
    unnamed x10 -> x6, local copies, waits for them, and re-layouts: 0.72 us -> 0.02 us
    pallas_call x11 -> x13, Pallas kernels: 11.8 us -> 12.4 us  [call(): pl.pallas_call(kernel, out_shape=outs, in_specs=specs or [VMEM] * len(arg...]
  transfers between devices with their start and end apart: 23 -> 23, of which waited for: 13 -> 11; matrix products, arithmetic and copies ran while one was open for 0% -> 0% of each run, Pallas kernels for 15% -> 17%
where the time goes in v3:
time: 66.2 us; the launch traced here: 66 us
  starting transfers between devices  38.5 us (58%)
  Pallas kernels  14.2 us (21%)
  waiting for transfers between devices  12.3 us (19%)
  between operations  0.94 us (1%)
    ppermute x16, starting transfers between devices, along_seq(): return lax.ppermute(array, 'seq', pairs)  22.6 us
    ppermute x7, starting transfers between devices, along_z(): return lax.ppermute(array, ('seq', 'head'), pairs)  15.8 us
    pallas_call x13, Pallas kernels, call(): pl.pallas_call(kernel, out_shape=outs, in_specs=specs or [VMEM] * len(arg...  12.4 us
    ppermute x7, waiting for transfers between devices, along_z(): return lax.ppermute(array, ('seq', 'head'), pairs)  6.66 us
    ppermute x16, waiting for transfers between devices, along_seq(): return lax.ppermute(array, 'seq', pairs)  5.68 us
    pallas_call x1, Pallas kernels, local(): pl.pallas_call(functools.partial(rest_kernel, pair), out_shape=(f32(rows,...  1.85 us
  transfers between devices with their start and end apart: 23, of which 11 were waited for; matrix products, arithmetic and copies ran while one was open for 0% of the time, Pallas kernels for 17%

profile of v3, /device:TPU:1, one launch (start us, length us, event | category | flops | bytes accessed | tf_op | source)
XLA Modules:
  0.0 66.0 jit_solution(10000632103959413474)
XLA Ops:
  0.6 3.3 %collective-permute-start.1 = (bf16[512,384]{1,0:T(8,128)(2,1)}, bf16[512,384]{1,0:T(8,128)(2,1)S(1)}, u32[]{:S(2)}, u32[]{:S(2)}) collective-permute-start(bf16[512,384]{1,0:T(8,128)(2,1)} %c_hbm.1), channel_id=1, source_target_pairs={{0,8},{8,0},{16,24},{24,16},{32,40},{40,32},{48,56},{56,48},{64,72... | collective-permute-start | bytes 1179656 | tf_op jit(solution)/shard_map/ppermute | solution.py:428
  4.0 3.8 %collective-permute-start.7 = (bf16[512,384]{1,0:T(8,128)(2,1)}, bf16[512,384]{1,0:T(8,128)(2,1)S(1)}, u32[]{:S(2)}, u32[]{:S(2)}) collective-permute-start(bf16[512,384]{1,0:T(8,128)(2,1)} %c_hbm.1), channel_id=1, source_target_pairs={{0,1},{1,2},{2,3},{3,4},{4,5},{5,6},{6,7},{7,0},{8,15},{9,8},{10,9... | collective-permute-start | bytes 1179656 | tf_op jit(solution)/shard_map/ppermute | solution.py:421
  7.8 1.6 %collective-permute-start.2 = (bf16[512,384]{1,0:T(8,128)(2,1)S(1)}, bf16[512,384]{1,0:T(8,128)(2,1)S(1)}, u32[]{:S(2)}, u32[]{:S(2)}) collective-permute-start(bf16[512,384]{1,0:T(8,128)(2,1)S(1)} %collective-permute-done.1), channel_id=1, source_target_pairs={{0,1},{1,2},{2,3},{3,4},{4,5},{5,6},{6,7},{7,0},{8,15},{9,8},{10,9... | collective-permute-start | bytes 1179656 | tf_op jit(solution)/shard_map/ppermute | solution.py:421
  9.4 1.8 %shard_map.85 = (f32[520,128]{1,0:T(8,128)S(1)}, f32[8,128]{1,0:T(8,128)}) custom-call(bf16[512,512]{1,0:T(8,128)(2,1)} %refs_4_.3, bf16[512,512]{1,0:T(8,128)(2,1)} %refs_5_.3, f32[4,512]{1,0:T(4,128)} %ld_hbm.3, f32[8,128]{1,0:T(8,128)S(1)} %broadcast_in_dim.3.tie_ref), custom_call_target="tpu_custom_call" | custom-call | tf_op jit(solution)/shard_map/pallas_call | solution.py:32
  11.3 1.5 %collective-permute-done.7.a1 = bf16[512,384]{1,0:T(8,128)(2,1)S(1)} collective-permute-done((bf16[512,384]{1,0:T(8,128)(2,1)}, bf16[512,384]{1,0:T(8,128)(2,1)S(1)}, u32[]{:S(2)}, u32[]{:S(2)}) %collective-permute-start.7) | collective-permute-done | bytes 393248 | tf_op jit(solution)/shard_map/ppermute | solution.py:421
  12.8 3.0 %collective-permute-start.9 = (bf16[512,384]{1,0:T(8,128)(2,1)S(1)}, bf16[512,384]{1,0:T(8,128)(2,1)S(1)}, u32[]{:S(2)}, u32[]{:S(2)}) collective-permute-start(bf16[512,384]{1,0:T(8,128)(2,1)S(1)} %collective-permute-done.7.a1), channel_id=1, source_target_pairs={{0,1},{1,2},{2,3},{3,4},{4,5},{5,6},{6,7},{7,0},{8,15},{9,8},{10,9... | collective-permute-start | bytes 1179656 | tf_op jit(solution)/shard_map/ppermute | solution.py:421
  15.8 1.1 %collective-permute-done.2.tie_ref = bf16[512,384]{1,0:T(8,128)(2,1)S(1)} collective-permute-done((bf16[512,384]{1,0:T(8,128)(2,1)S(1)}, bf16[512,384]{1,0:T(8,128)(2,1)S(1)}, u32[]{:S(2)}, u32[]{:S(2)}) %collective-permute-start.2) | collective-permute-done | bytes 393248 | tf_op jit(solution)/shard_map/ppermute | solution.py:421
  17.0 3.2 %collective-permute-start.6 = (bf16[512,384]{1,0:T(8,128)(2,1)S(1)}, bf16[512,384]{1,0:T(8,128)(2,1)S(1)}, u32[]{:S(2)}, u32[]{:S(2)}) collective-permute-start(bf16[512,384]{1,0:T(8,128)(2,1)S(1)} %get-tuple-element.40.x_ref), channel_id=1, source_target_pairs={{0,1},{1,2},{2,3},{3,4},{4,5},{5,6},{6,7},{7,0},{8,15},{9,8},{10,9... | collective-permute-start | bytes 1179656 | tf_op jit(solution)/shard_map/ppermute | solution.py:421
  20.2 2.5 %collective-permute-start.5 = (bf16[272,128]{1,0:T(8,128)(2,1)S(1)}, bf16[272,128]{1,0:T(8,128)(2,1)S(1)}, u32[]{:S(2)}, u32[]{:S(2)}) collective-permute-start(bf16[272,128]{1,0:T(8,128)(2,1)S(1)} %get-tuple-element.38.sent_ref), channel_id=1, source_target_pairs={{0,48},{8,56},{16,32},{24,40},{32,16},{40,24},{48,0},{56,8},{64,11... | collective-permute-start | bytes 208904 | tf_op jit(solution)/shard_map/ppermute | solution.py:428
  23.5 0.8 %collective-permute-start.11 = (bf16[512,384]{1,0:T(8,128)(2,1)S(1)}, bf16[512,384]{1,0:T(8,128)(2,1)S(1)}, u32[]{:S(2)}, u32[]{:S(2)}) collective-permute-start(bf16[512,384]{1,0:T(8,128)(2,1)S(1)} %collective-permute-done.9.a2), channel_id=1, source_target_pairs={{0,1},{1,2},{2,3},{3,4},{4,5},{5,6},{6,7},{7,0},{8,15},{9,8},{10,9... | collective-permute-start | bytes 1179656 | tf_op jit(solution)/shard_map/ppermute | solution.py:421
  24.3 1.1 %collective-permute-done.6.tie_ref = bf16[512,384]{1,0:T(8,128)(2,1)S(1)} collective-permute-done((bf16[512,384]{1,0:T(8,128)(2,1)S(1)}, bf16[512,384]{1,0:T(8,128)(2,1)S(1)}, u32[]{:S(2)}, u32[]{:S(2)}) %collective-permute-start.6) | collective-permute-done | bytes 393248 | tf_op jit(solution)/shard_map/ppermute | solution.py:421
  25.4 2.2 %collective-permute-start.8 = (bf16[512,384]{1,0:T(8,128)(2,1)S(1)}, bf16[512,384]{1,0:T(8,128)(2,1)S(1)}, u32[]{:S(2)}, u32[]{:S(2)}) collective-permute-start(bf16[512,384]{1,0:T(8,128)(2,1)S(1)} %shard_map.88), channel_id=1, source_target_pairs={{0,8},{8,0},{16,24},{24,16},{32,40},{40,32},{48,56},{56,48},{64,72... | collective-permute-start | bytes 1179656 | tf_op jit(solution)/shard_map/ppermute | solution.py:428
  28.3 1.1 %collective-permute-start.13 = (bf16[512,384]{1,0:T(8,128)(2,1)S(1)}, bf16[512,384]{1,0:T(8,128)(2,1)S(1)}, u32[]{:S(2)}, u32[]{:S(2)}) collective-permute-start(bf16[512,384]{1,0:T(8,128)(2,1)S(1)} %get-tuple-element.43), channel_id=1, source_target_pairs={{0,1},{1,2},{2,3},{3,4},{4,5},{5,6},{6,7},{7,0},{8,15},{9,8},{10,9... | collective-permute-start | bytes 1179656 | tf_op jit(solution)/shard_map/ppermute | solution.py:421
  29.4 1.0 %collective-permute-done.11.a3 = bf16[512,384]{1,0:T(8,128)(2,1)S(1)} collective-permute-done((bf16[512,384]{1,0:T(8,128)(2,1)S(1)}, bf16[512,384]{1,0:T(8,128)(2,1)S(1)}, u32[]{:S(2)}, u32[]{:S(2)}) %collective-permute-start.11) | collective-permute-done | bytes 393248 | tf_op jit(solution)/shard_map/ppermute | solution.py:421
  30.4 2.3 %collective-permute-start.12 = (bf16[512,384]{1,0:T(8,128)(2,1)S(1)}, bf16[512,384]{1,0:T(8,128)(2,1)S(1)}, u32[]{:S(2)}, u32[]{:S(2)}) collective-permute-start(bf16[512,384]{1,0:T(8,128)(2,1)S(1)} %collective-permute-done.11.a3), channel_id=1, source_target_pairs={{0,1},{1,2},{2,3},{3,4},{4,5},{5,6},{6,7},{7,0},{8,15},{9,8},{10,9... | collective-permute-start | bytes 1179656 | tf_op jit(solution)/shard_map/ppermute | solution.py:421
  32.7 4.1 %shard_map.89 = (f32[512,512]{1,0:T(8,128)S(1)}, bf16[2,512,384]{2,1,0:T(8,128)(2,1)S(1)}, bf16[4,256,512]{2,1,0:T(8,128)(2,1)S(1)}, f32[4,512]{1,0:T(4,128)S(1)}, f32[512,4]{1,0:T(8,128)S(1)}) custom-call(bf16[512,3072]{1,0:T(8,128)(2,1)} %w_hbm.1, bf16[512,384]{1,0:T(8,128)(2,1)} %c_hbm.1, bf16[512,512]{1,0:T(8,128)(2,1)} %q_ref.3, f32[4,512]{1,0:T(4,128)} %ld_hbm.3, ...), custom_call_target="tpu_custom_call" | custom-call | tf_op jit(solution)/shard_map/pallas_call | solution.py:32
  36.9 0.7 collective-permute-start.14
  37.5 1.9 %collective-permute-done.12.a4 = bf16[512,384]{1,0:T(8,128)(2,1)S(1)} collective-permute-done((bf16[512,384]{1,0:T(8,128)(2,1)S(1)}, bf16[512,384]{1,0:T(8,128)(2,1)S(1)}, u32[]{:S(2)}, u32[]{:S(2)}) %collective-permute-start.12) | collective-permute-done | bytes 393248 | tf_op jit(solution)/shard_map/ppermute | solution.py:421
  39.5 1.2 %shard_map.91 = (bf16[512,512]{1,0:T(8,128)(2,1)S(1)}, f32[512,128]{1,0:T(8,128)S(1)}) custom-call(f32[512,512]{1,0:T(8,128)S(1)} %get-tuple-element.42.tie_ref.acc_ref, bf16[512,384]{1,0:T(8,128)(2,1)S(1)} %collective-permute-done.12.a4, bf16[512,384]{1,0:T(8,128)(2,1)S(1)} %collective-permute-done.14.b3, bf16[2,512,384]{2,1,0:T(8,128)(2,1)S(1)} %get-tuple-element.44.w_ref, ...), custom_call_target="tpu_custom_call" | custom-call | tf_op jit(solution)/shard_map/pallas_call | solution.py:32
  40.6 2.2 %collective-permute-start.15 = (f32[512,128]{1,0:T(8,128)S(1)}, f32[512,128]{1,0:T(8,128)S(1)}, u32[]{:S(2)}, u32[]{:S(2)}) collective-permute-start(f32[512,128]{1,0:T(8,128)S(1)} %get-tuple-element.46.grad_ref), channel_id=1, source_target_pairs={{0,8},{8,0},{16,24},{24,16},{32,40},{40,32},{48,56},{56,48},{64,72... | collective-permute-start | bytes 786440 | tf_op jit(solution)/shard_map/ppermute | solution.py:428
  42.9 1.2 %collective-permute-done.15.grad_other.refs_2_ = f32[512,128]{1,0:T(8,128)S(1)} collective-permute-done((f32[512,128]{1,0:T(8,128)S(1)}, f32[512,128]{1,0:T(8,128)S(1)}, u32[]{:S(2)}, u32[]{:S(2)}) %collective-permute-start.15) | collective-permute-done | bytes 262176 | tf_op jit(solution)/shard_map/ppermute | solution.py:428
  44.1 2.8 %collective-permute-start.18 = (bf16[256,128]{1,0:T(8,128)(2,1)S(1)}, bf16[256,128]{1,0:T(8,128)(2,1)S(1)}, u32[]{:S(2)}, u32[]{:S(2)}) collective-permute-start(bf16[256,128]{1,0:T(8,128)(2,1)S(1)} %get-tuple-element.48), channel_id=1, source_target_pairs={{0,32},{8,40},{16,48},{24,56},{32,0},{40,8},{48,16},{56,24},{64,96... | collective-permute-start | bytes 196616 | tf_op jit(solution)/shard_map/ppermute | solution.py:428
  46.9 0.9 %collective-permute-start.17 = (bf16[256,128]{1,0:T(8,128)(2,1)S(1)}, bf16[256,128]{1,0:T(8,128)(2,1)S(1)}, u32[]{:S(2)}, u32[]{:S(2)}) collective-permute-start(bf16[256,128]{1,0:T(8,128)(2,1)S(1)} %get-tuple-element.48), channel_id=1, source_target_pairs={{0,48},{8,56},{16,32},{24,40},{32,16},{40,24},{48,0},{56,8},{64,11... | collective-permute-start | bytes 196616 | tf_op jit(solution)/shard_map/ppermute | solution.py:428
  47.8 2.0 %shard_map.93 = (f32[512,256]{1,0:T(8,128)S(1)}, f32[512,256]{1,0:T(8,128)S(1)}, f32[512,256]{1,0:T(8,128)S(1)}, f32[512,256]{1,0:T(8,128)S(1)}, f32[512,256]{1,0:T(8,128)S(1)}, /*index=5*/f32[8,128]{1,0:T(8,128)S(1)}) custom-call(bf16[512,512]{1,0:T(8,128)(2,1)S(1)} %copy-done.2, bf16[512,512]{1,0:T(8,128)(2,1)S(1)} %copy-done, ...), custom_call_target="tpu_custom_call" | custom-call | tf_op jit(solution)/shard_map/pallas_call | solution.py:32
  49.8 1.4 %collective-permute-done.17.r3 = bf16[256,128]{1,0:T(8,128)(2,1)S(1)} collective-permute-done((bf16[256,128]{1,0:T(8,128)(2,1)S(1)}, bf16[256,128]{1,0:T(8,128)(2,1)S(1)}, u32[]{:S(2)}, u32[]{:S(2)}) %collective-permute-start.17) | collective-permute-done | bytes 65568 | tf_op jit(solution)/shard_map/ppermute | solution.py:428
  51.3 3.0 %collective-permute-start.19 = (bf16[272,128]{1,0:T(8,128)(2,1)S(1)}, bf16[272,128]{1,0:T(8,128)(2,1)S(1)}, u32[]{:S(2)}, u32[]{:S(2)}) collective-permute-start(bf16[272,128]{1,0:T(8,128)(2,1)S(1)} %get-tuple-element.57), channel_id=1, source_target_pairs={{0,128},{8,136},{16,144},{24,152},{32,160},{40,168},{48,176},{56,1... | collective-permute-start | bytes 208904 | tf_op jit(solution)/shard_map/ppermute | solution.py:428
  55.1 2.1 %shard_map.95 = (f32[512,256]{1,0:T(8,128)S(1)}, f32[512,256]{1,0:T(8,128)S(1)}, f32[512,256]{1,0:T(8,128)S(1)}, f32[512,256]{1,0:T(8,128)S(1)}, f32[512,256]{1,0:T(8,128)S(1)}, /*index=5*/f32[8,128]{1,0:T(8,128)S(1)}) custom-call(bf16[512,512]{1,0:T(8,128)(2,1)S(1)} %copy-done.2, bf16[512,512]{1,0:T(8,128)(2,1)S(1)} %copy-done, ...), custom_call_target="tpu_custom_call" | custom-call | tf_op jit(solution)/shard_map/pallas_call | solution.py:32
  57.5 1.9 %collective-permute-done.21.r3 = bf16[272,128]{1,0:T(8,128)(2,1)S(1)} collective-permute-done((bf16[272,128]{1,0:T(8,128)(2,1)S(1)}, bf16[272,128]{1,0:T(8,128)(2,1)S(1)}, u32[]{:S(2)}, u32[]{:S(2)}) %collective-permute-start.21) | collective-permute-done | bytes 69664 | tf_op jit(solution)/shard_map/ppermute | solution.py:428
  59.5 3.3 %collective-permute-start.22 = (f32[512,128]{1,0:T(8,128)S(1)}, f32[512,128]{1,0:T(8,128)S(1)}, u32[]{:S(2)}, u32[]{:S(2)}) collective-permute-start(f32[512,128]{1,0:T(8,128)S(1)} %shard_map.96.refs_0_), channel_id=1, source_target_pairs={{0,8},{8,0},{16,24},{24,16},{32,40},{40,32},{48,56},{56,48},{64,72... | collective-permute-start | bytes 786440 | tf_op jit(solution)/shard_map/ppermute | solution.py:428
  62.8 0.6 shard_map.97.refs_11_
  63.4 0.5 collective-permute-done.22.refs_0_
  64.0 1.9 %shard_map.98 = (f32[512,512]{1,0:T(8,128)}, f32[512,512]{1,0:T(8,128)}, f32[512,512]{1,0:T(8,128)}) custom-call(f32[512,128]{1,0:T(8,128)S(1)} %collective-permute-done.22.refs_0_, f32[520,128]{1,0:T(8,128)S(1)} %collective-permute-done.key_other.refs_1_, f32[512,128]{1,0:T(8,128)S(1)} %collective-permute-done.15.grad_other.refs_2_, ...), custom_call_target="tpu_custom_call" | custom-call | tf_op jit(solution)/shard_map/pallas_call | solution.py:516
  (35 shorter events, 3.0 us)
Async XLA Ops:
  0.6 7.2 %collective-permute-start.1 = (bf16[512,384]{1,0:T(8,128)(2,1)}, bf16[512,384]{1,0:T(8,128)(2,1)S(1)}, u32[]{:S(2)}, u32[]{:S(2)}) collective-permute-start(bf16[512,384]{1,0:T(8,128)(2,1)} %c_hbm.1), channel_id=1, source_target_pairs={{0,8},{8,0},{16,24},{24,16},{32,40},{40,32},{48,56},{56,48},{64,72... | collective-permute-start | bytes 1179656 | tf_op jit(solution)/shard_map/ppermute | solution.py:428
  4.0 8.9 %collective-permute-start.7 = (bf16[512,384]{1,0:T(8,128)(2,1)}, bf16[512,384]{1,0:T(8,128)(2,1)S(1)}, u32[]{:S(2)}, u32[]{:S(2)}) collective-permute-start(bf16[512,384]{1,0:T(8,128)(2,1)} %c_hbm.1), channel_id=1, source_target_pairs={{0,1},{1,2},{2,3},{3,4},{4,5},{5,6},{6,7},{7,0},{8,15},{9,8},{10,9... | collective-permute-start | bytes 1179656 | tf_op jit(solution)/shard_map/ppermute | solution.py:421
  7.8 9.1 %collective-permute-start.2 = (bf16[512,384]{1,0:T(8,128)(2,1)S(1)}, bf16[512,384]{1,0:T(8,128)(2,1)S(1)}, u32[]{:S(2)}, u32[]{:S(2)}) collective-permute-start(bf16[512,384]{1,0:T(8,128)(2,1)S(1)} %collective-permute-done.1), channel_id=1, source_target_pairs={{0,1},{1,2},{2,3},{3,4},{4,5},{5,6},{6,7},{7,0},{8,15},{9,8},{10,9... | collective-permute-start | bytes 1179656 | tf_op jit(solution)/shard_map/ppermute | solution.py:421
  11.2 4.6 %collective-permute-start = (f32[520,128]{1,0:T(8,128)S(1)}, f32[520,128]{1,0:T(8,128)S(1)}, u32[]{:S(2)}, u32[]{:S(2)}) collective-permute-start(f32[520,128]{1,0:T(8,128)S(1)} %get-tuple-element.37.key_ref), channel_id=1, source_target_pairs={{0,8},{8,0},{16,24},{24,16},{32,40},{40,32},{48,56},{56,48},{64,72... | collective-permute-start | bytes 798728 | tf_op jit(solution)/shard_map/ppermute | solution.py:428
  12.8 10.6 %collective-permute-start.9 = (bf16[512,384]{1,0:T(8,128)(2,1)S(1)}, bf16[512,384]{1,0:T(8,128)(2,1)S(1)}, u32[]{:S(2)}, u32[]{:S(2)}) collective-permute-start(bf16[512,384]{1,0:T(8,128)(2,1)S(1)} %collective-permute-done.7.a1), channel_id=1, source_target_pairs={{0,1},{1,2},{2,3},{3,4},{4,5},{5,6},{6,7},{7,0},{8,15},{9,8},{10,9... | collective-permute-start | bytes 1179656 | tf_op jit(solution)/shard_map/ppermute | solution.py:421
  17.0 8.3 %collective-permute-start.6 = (bf16[512,384]{1,0:T(8,128)(2,1)S(1)}, bf16[512,384]{1,0:T(8,128)(2,1)S(1)}, u32[]{:S(2)}, u32[]{:S(2)}) collective-permute-start(bf16[512,384]{1,0:T(8,128)(2,1)S(1)} %get-tuple-element.40.x_ref), channel_id=1, source_target_pairs={{0,1},{1,2},{2,3},{3,4},{4,5},{5,6},{6,7},{7,0},{8,15},{9,8},{10,9... | collective-permute-start | bytes 1179656 | tf_op jit(solution)/shard_map/ppermute | solution.py:421
  20.2 7.4 %collective-permute-start.5 = (bf16[272,128]{1,0:T(8,128)(2,1)S(1)}, bf16[272,128]{1,0:T(8,128)(2,1)S(1)}, u32[]{:S(2)}, u32[]{:S(2)}) collective-permute-start(bf16[272,128]{1,0:T(8,128)(2,1)S(1)} %get-tuple-element.38.sent_ref), channel_id=1, source_target_pairs={{0,48},{8,56},{16,32},{24,40},{32,16},{40,24},{48,0},{56,8},{64,11... | collective-permute-start | bytes 208904 | tf_op jit(solution)/shard_map/ppermute | solution.py:428
  22.7 5.4 %collective-permute-start.4 = (bf16[272,128]{1,0:T(8,128)(2,1)S(1)}, bf16[272,128]{1,0:T(8,128)(2,1)S(1)}, u32[]{:S(2)}, u32[]{:S(2)}) collective-permute-start(bf16[272,128]{1,0:T(8,128)(2,1)S(1)} %get-tuple-element.38.sent_ref), channel_id=1, source_target_pairs={{0,32},{8,40},{16,48},{24,56},{32,0},{40,8},{48,16},{56,24},{64,96... | collective-permute-start | bytes 208904 | tf_op jit(solution)/shard_map/ppermute | solution.py:428
  23.2 4.9 %collective-permute-start.3 = (bf16[272,128]{1,0:T(8,128)(2,1)S(1)}, bf16[272,128]{1,0:T(8,128)(2,1)S(1)}, u32[]{:S(2)}, u32[]{:S(2)}) collective-permute-start(bf16[272,128]{1,0:T(8,128)(2,1)S(1)} %get-tuple-element.38.sent_ref), channel_id=1, source_target_pairs={{0,16},{8,24},{16,0},{24,8},{32,48},{40,56},{48,32},{56,40},{64,80... | collective-permute-start | bytes 208904 | tf_op jit(solution)/shard_map/ppermute | solution.py:428
  23.5 6.9 %collective-permute-start.11 = (bf16[512,384]{1,0:T(8,128)(2,1)S(1)}, bf16[512,384]{1,0:T(8,128)(2,1)S(1)}, u32[]{:S(2)}, u32[]{:S(2)}) collective-permute-start(bf16[512,384]{1,0:T(8,128)(2,1)S(1)} %collective-permute-done.9.a2), channel_id=1, source_target_pairs={{0,1},{1,2},{2,3},{3,4},{4,5},{5,6},{6,7},{7,0},{8,15},{9,8},{10,9... | collective-permute-start | bytes 1179656 | tf_op jit(solution)/shard_map/ppermute | solution.py:421
  25.4 7.3 %collective-permute-start.8 = (bf16[512,384]{1,0:T(8,128)(2,1)S(1)}, bf16[512,384]{1,0:T(8,128)(2,1)S(1)}, u32[]{:S(2)}, u32[]{:S(2)}) collective-permute-start(bf16[512,384]{1,0:T(8,128)(2,1)S(1)} %shard_map.88), channel_id=1, source_target_pairs={{0,8},{8,0},{16,24},{24,16},{32,40},{40,32},{48,56},{56,48},{64,72... | collective-permute-start | bytes 1179656 | tf_op jit(solution)/shard_map/ppermute | solution.py:428
  27.6 5.1 %collective-permute-start.10 = (bf16[512,384]{1,0:T(8,128)(2,1)S(1)}, bf16[512,384]{1,0:T(8,128)(2,1)S(1)}, u32[]{:S(2)}, u32[]{:S(2)}) collective-permute-start(bf16[512,384]{1,0:T(8,128)(2,1)S(1)} %collective-permute-done.6.tie_ref), channel_id=1, source_target_pairs={{0,8},{8,0},{16,24},{24,16},{32,40},{40,32},{48,56},{56,48},{64,72... | collective-permute-start | bytes 1179656 | tf_op jit(solution)/shard_map/ppermute | solution.py:428
  28.3 8.5 %collective-permute-start.13 = (bf16[512,384]{1,0:T(8,128)(2,1)S(1)}, bf16[512,384]{1,0:T(8,128)(2,1)S(1)}, u32[]{:S(2)}, u32[]{:S(2)}) collective-permute-start(bf16[512,384]{1,0:T(8,128)(2,1)S(1)} %get-tuple-element.43), channel_id=1, source_target_pairs={{0,1},{1,2},{2,3},{3,4},{4,5},{5,6},{6,7},{7,0},{8,15},{9,8},{10,9... | collective-permute-start | bytes 1179656 | tf_op jit(solution)/shard_map/ppermute | solution.py:421
  30.4 9.1 %collective-permute-start.12 = (bf16[512,384]{1,0:T(8,128)(2,1)S(1)}, bf16[512,384]{1,0:T(8,128)(2,1)S(1)}, u32[]{:S(2)}, u32[]{:S(2)}) collective-permute-start(bf16[512,384]{1,0:T(8,128)(2,1)S(1)} %collective-permute-done.11.a3), channel_id=1, source_target_pairs={{0,1},{1,2},{2,3},{3,4},{4,5},{5,6},{6,7},{7,0},{8,15},{9,8},{10,9... | collective-permute-start | bytes 1179656 | tf_op jit(solution)/shard_map/ppermute | solution.py:421
  36.8 11.0 %copy-start = (bf16[512,512]{1,0:T(8,128)(2,1)S(1)}, bf16[512,512]{1,0:T(8,128)(2,1)}, u32[]{:S(2)}) copy-start(bf16[512,512]{1,0:T(8,128)(2,1)} %refs_4_.3) | copy-start | bytes 1572868
  36.8 11.0 %copy-start.1 = (bf16[512,512]{1,0:T(8,128)(2,1)S(1)}, bf16[512,512]{1,0:T(8,128)(2,1)}, u32[]{:S(2)}) copy-start(bf16[512,512]{1,0:T(8,128)(2,1)} %refs_5_.3) | copy-start | bytes 1572868
  36.8 10.9 %copy-start.2 = (bf16[512,512]{1,0:T(8,128)(2,1)S(1)}, bf16[512,512]{1,0:T(8,128)(2,1)}, u32[]{:S(2)}) copy-start(bf16[512,512]{1,0:T(8,128)(2,1)} %q_ref.3) | copy-start | bytes 1572868
  36.9 2.6 %collective-permute-start.14 = (bf16[512,384]{1,0:T(8,128)(2,1)S(1)}, bf16[512,384]{1,0:T(8,128)(2,1)S(1)}, u32[]{:S(2)}, u32[]{:S(2)}) collective-permute-start(bf16[512,384]{1,0:T(8,128)(2,1)S(1)} %shard_map.90), channel_id=1, source_target_pairs={{0,8},{8,0},{16,24},{24,16},{32,40},{40,32},{48,56},{56,48},{64,72... | collective-permute-start | bytes 1179656 | tf_op jit(solution)/shard_map/ppermute | solution.py:428
  40.6 3.4 %collective-permute-start.15 = (f32[512,128]{1,0:T(8,128)S(1)}, f32[512,128]{1,0:T(8,128)S(1)}, u32[]{:S(2)}, u32[]{:S(2)}) collective-permute-start(f32[512,128]{1,0:T(8,128)S(1)} %get-tuple-element.46.grad_ref), channel_id=1, source_target_pairs={{0,8},{8,0},{16,24},{24,16},{32,40},{40,32},{48,56},{56,48},{64,72... | collective-permute-start | bytes 786440 | tf_op jit(solution)/shard_map/ppermute | solution.py:428
  44.1 5.8 %collective-permute-start.18 = (bf16[256,128]{1,0:T(8,128)(2,1)S(1)}, bf16[256,128]{1,0:T(8,128)(2,1)S(1)}, u32[]{:S(2)}, u32[]{:S(2)}) collective-permute-start(bf16[256,128]{1,0:T(8,128)(2,1)S(1)} %get-tuple-element.48), channel_id=1, source_target_pairs={{0,32},{8,40},{16,48},{24,56},{32,0},{40,8},{48,16},{56,24},{64,96... | collective-permute-start | bytes 196616 | tf_op jit(solution)/shard_map/ppermute | solution.py:428
  46.9 4.3 %collective-permute-start.17 = (bf16[256,128]{1,0:T(8,128)(2,1)S(1)}, bf16[256,128]{1,0:T(8,128)(2,1)S(1)}, u32[]{:S(2)}, u32[]{:S(2)}) collective-permute-start(bf16[256,128]{1,0:T(8,128)(2,1)S(1)} %get-tuple-element.48), channel_id=1, source_target_pairs={{0,48},{8,56},{16,32},{24,40},{32,16},{40,24},{48,0},{56,8},{64,11... | collective-permute-start | bytes 196616 | tf_op jit(solution)/shard_map/ppermute | solution.py:428
  47.8 3.5 %collective-permute-start.16 = (bf16[256,128]{1,0:T(8,128)(2,1)S(1)}, bf16[256,128]{1,0:T(8,128)(2,1)S(1)}, u32[]{:S(2)}, u32[]{:S(2)}) collective-permute-start(bf16[256,128]{1,0:T(8,128)(2,1)S(1)} %get-tuple-element.48), channel_id=1, source_target_pairs={{0,16},{8,24},{16,0},{24,8},{32,48},{40,56},{48,32},{56,40},{64,80... | collective-permute-start | bytes 196616 | tf_op jit(solution)/shard_map/ppermute | solution.py:428
  51.3 5.8 %collective-permute-start.19 = (bf16[272,128]{1,0:T(8,128)(2,1)S(1)}, bf16[272,128]{1,0:T(8,128)(2,1)S(1)}, u32[]{:S(2)}, u32[]{:S(2)}) collective-permute-start(bf16[272,128]{1,0:T(8,128)(2,1)S(1)} %get-tuple-element.57), channel_id=1, source_target_pairs={{0,128},{8,136},{16,144},{24,152},{32,160},{40,168},{48,176},{56,1... | collective-permute-start | bytes 208904 | tf_op jit(solution)/shard_map/ppermute | solution.py:428
  54.3 3.2 %collective-permute-start.20 = (bf16[272,128]{1,0:T(8,128)(2,1)S(1)}, bf16[272,128]{1,0:T(8,128)(2,1)S(1)}, u32[]{:S(2)}, u32[]{:S(2)}) collective-permute-start(bf16[272,128]{1,0:T(8,128)(2,1)S(1)} %get-tuple-element.58), channel_id=1, source_target_pairs={{0,64},{8,72},{16,80},{24,88},{32,96},{40,104},{48,112},{56,120},{... | collective-permute-start | bytes 208904 | tf_op jit(solution)/shard_map/ppermute | solution.py:428
  54.7 4.7 %collective-permute-start.21 = (bf16[272,128]{1,0:T(8,128)(2,1)S(1)}, bf16[272,128]{1,0:T(8,128)(2,1)S(1)}, u32[]{:S(2)}, u32[]{:S(2)}) collective-permute-start(bf16[272,128]{1,0:T(8,128)(2,1)S(1)} %get-tuple-element.59), channel_id=1, source_target_pairs={{0,192},{8,200},{16,208},{24,216},{32,224},{40,232},{48,240},{56,2... | collective-permute-start | bytes 208904 | tf_op jit(solution)/shard_map/ppermute | solution.py:428
  59.5 4.4 %collective-permute-start.22 = (f32[512,128]{1,0:T(8,128)S(1)}, f32[512,128]{1,0:T(8,128)S(1)}, u32[]{:S(2)}, u32[]{:S(2)}) collective-permute-start(f32[512,128]{1,0:T(8,128)S(1)} %shard_map.96.refs_0_), channel_id=1, source_target_pairs={{0,8},{8,0},{16,24},{24,16},{32,40},{40,32},{48,56},{56,48},{64,72... | collective-permute-start | bytes 786440 | tf_op jit(solution)/shard_map/ppermute | solution.py:428

commit v4 on v3

--- a/solution.py
+++ b/solution.py
@@ -89,7 +89,7 @@
     return pl.ds(pl.multiple_of(lax.rem(core_index() * 2 + position, 4) * DH, DH), DH)
 
 
-def local_kernel(heads, first, q_ref, k_ref, v_ref, ga_ref, row_ref, col_ref, dq_ref, dk_ref, dv_ref, start_ref, end_ref, tie_ref):
+def local_kernel(heads, first, _, q_ref, k_ref, v_ref, ga_ref, row_ref, col_ref, dq_ref, dk_ref, dv_ref, start_ref, end_ref, tie_ref):
     n = q_ref.shape[0]
     step = n // 2
     s = lax.broadcasted_iota(jnp.int32, (step, step), 0)
@@ -130,7 +130,7 @@
 
 
 def first_kernel(
-    w_hbm, c_hbm, q_hbm, ld_hbm, a1, b1, a2, b2, a3,
+    w_hbm, c_hbm, q_hbm, ld_hbm, a1, b1, a2, b2, a3, _,
     acc_ref, w_ref, qw_ref, row_ref, col_ref, near_ref, c_ref, q_ref, ld_ref, sems,
 ):
     z, side = lax.axis_index("head"), 1 - 2 * core_index()
@@ -176,20 +176,22 @@
         out_ref[at, :] = acc_ref[at, :] + dot(a4[at, :], w_ref[0], NT)
 
 
-def late_kernel(heads, acc_ref, a4, b3, w_ref, qw_ref, ga_ref, state_ref):
+def late_kernel(heads, acc_ref, a4, b3, w_ref, qw_ref, ga_ref, own_ref, theirs_ref):
     half = acc_ref.shape[0] // 2
     for part in range(2):
         at = pl.ds(part * half, half)
         ga_ref[at, :] = (
             acc_ref[at, :] + dot(a4[at, :], w_ref[0], NT) + dot(b3[at, :], w_ref[1], NT)
         ).astype(jnp.bfloat16)
-    for h in range(heads):
-        both = dot(qw_ref[h], ga_ref[:, h * DH : (h + 1) * DH], NN)
-        state_ref[pl.ds(h * DH, DH), :] = both[:DH] + both[DH:]
-
-
-def gate_kernel(x_ref, tie_ref, out_ref):
-    out_ref[...] = x_ref[...]
+    for position in range(heads):
+        h = lax.rem(core_index() * (heads // 2) + position, heads)
+        both = dot(qw_ref[h], ga_ref[:, head_columns(position)], NN)
+        to = own_ref if position < heads // 2 else theirs_ref
+        to[pl.ds(position % (heads // 2) * DH, DH), :] = both[:DH] + both[DH:]
+
+
+def gate_kernel(x_ref, *refs):
+    refs[-1][...] = x_ref[...]
 
 
 def core_index():
@@ -249,7 +251,7 @@
         h = core * pair + j
         mine = jnp.exp(one_row(key_ref[heads * DH :, :], h))
         others = jnp.exp(one_row(key_other[heads * DH :, :], h))
-        at = pl.ds(pl.multiple_of(h * DH, DH), DH)
+        at = pl.ds(j * DH, DH)
         grad = jnp.where(first, 1.0, others) * grad_ref[at, :] + jnp.where(first, mine, 1.0) * grad_other[at, :]
         chip_ref[pl.ds(j * DH, DH), :] = grad
         sent_ref[pl.ds(j * DH, DH), :] = grad.astype(jnp.bfloat16)
@@ -267,8 +269,7 @@
     return sum(t * flag((low < p) & (p < high)) for t, p in zip(totals, place))
 
 
-def row_key_kernel(pair, sent_ref, chip_ref, r1, r2, r3, tie_ref, in_ref, whole_ref, table_ref, tail_ref, tied_ref):
-    tied_ref[...] = tie_ref[...]
+def row_key_kernel(pair, sent_ref, chip_ref, r1, r3, r2, in_ref, whole_ref, table_ref, tail_ref):
     x = x_index()
     n = pair * DH
     refs = (sent_ref, r1, r2, r3)
@@ -352,7 +353,7 @@
         grad = enter_ref[pl.ds((pair + i) * DH, DH), :]
         decay = jnp.exp(one_row(key_other[heads * DH :, :], h))
         si = jnp.where(core == 0, key, decay * key + key_other[cols, :])
-        so = jnp.where(core == 0, decay * grad + grad_other[cols, :], grad)
+        so = jnp.where(core == 0, decay * grad + grad_other[pl.ds(i * DH, DH), :], grad)
         hi, lo = pieces(so, 2)
         states[i] = jnp.concatenate(pieces(si, 2), axis=0), jnp.concatenate([hi, lo], axis=0), jnp.concatenate([hi, lo], axis=1)
     si, so, so_wide = states[i]
@@ -455,48 +456,49 @@
     b2 = along_z(b1)
     b2_here = other(b2)
     b1_here = other(call(gate_kernel, (bf16(*grad_out.shape),), b1, b2)[0])
-    key_in, key_row, table, tail, b2 = call(
+    key_in, key_row, table, tail = call(
         functools.partial(row_key_kernel, pair),
-        (f32(pair * DH, DH), f32(pair * DH, DH), f32(16 * pair, DH), bf16(16, DH), bf16(*grad_out.shape)),
-        sent, chip, *from_x, b2, specs=[VMEM] * 6,
+        (f32(pair * DH, DH), f32(pair * DH, DH), f32(16 * pair, DH), bf16(16, DH)),
+        sent, chip, from_x[0], from_x[2], from_x[1], specs=[VMEM] * 5,
     )
     a3 = along_z(a2)
-    b3 = along_z(b2)
+    b3 = along_z(call(gate_kernel, (bf16(*grad_out.shape),), b2, from_x[0], from_x[2], from_x[1])[0])
     a4 = along_z(a3)
 
     qd = grad_out.shape[1]
     acc, w, qw, row, col = call(
         first_kernel,
         (f32(rows, width), bf16(2, width, qd), bf16(heads, 2 * DH, rows), f32(heads, rows), f32(rows, heads)),
-        in_hbm(out_weight), in_hbm(grad_out), in_hbm(queries), in_hbm(log_decay), a1, b1_here, a2, b2_here, a3,
-        specs=[ANY] * 4 + [VMEM] * 5,
+        in_hbm(out_weight), in_hbm(grad_out), in_hbm(queries), in_hbm(log_decay), a1, b1_here, a2, b2_here, a3, tail,
+        specs=[ANY] * 4 + [VMEM] * 6,
         scratch=[
             pltpu.VMEM((6, width, qd), jnp.bfloat16), pltpu.VMEM((rows, qd), jnp.bfloat16),
             pltpu.VMEM((rows, width), jnp.bfloat16), pltpu.VMEM((heads, rows), jnp.float32), pltpu.SemaphoreType.DMA((11,)),
         ],
     )
     b3_here = other(call(gate_kernel, (bf16(*grad_out.shape),), b3, acc)[0])
-    ga, grad_own = call(
-        functools.partial(late_kernel, heads), (bf16(rows, width), f32(heads * DH, DH)), acc, a4, b3_here, w, qw
-    )
-
-    grad_other = other(grad_own)
+    ga, grad_own, grad_theirs = call(
+        functools.partial(late_kernel, heads), (bf16(rows, width), f32(pair * DH, DH), f32(pair * DH, DH)), acc, a4, b3_here, w, qw
+    )
+
+    grad_other = other(grad_theirs)
+    grad_rest = other(grad_own)
     sent, chip = call(
         functools.partial(chip_grad_kernel, heads), (bf16(pair * DH, DH), f32(pair * DH, DH)),
         key_own, key_other, grad_own, grad_other, specs=[VMEM] * 4,
     )
     from_x = [along_seq(sent, dx=d) for d in (2, 1, 3)]
     from_x = [from_x[1], from_x[0], from_x[2]]
-    def local_part(first):
+    def local_part(first, after):
         *parts, tie = call(
             functools.partial(local_kernel, pair, first), (f32(rows, pair * DH),) * 5 + (f32(8, DH),),
-            queries, keys, values, ga, row, col,
+            after, queries, keys, values, ga, row, col,
         )
         dq, dk, dv, start_w, end_w = parts
         return (start_w, end_w, dq, dk, dv), tie
 
-    low, tie = local_part(0)
-    high, tie_high = local_part(pair)
+    low, tie = local_part(0, row)
+    high, tie_high = local_part(pair, grad_rest)
     grad_in, *sent = call(
         functools.partial(row_grad_kernel, pair),
         (f32(pair * DH, DH),) + (bf16(pair * DH + 16, DH),) * 3,
@@ -520,7 +522,7 @@
         out_specs=(ANY,) * 3,
         scratch_shapes=[pltpu.VMEM((3, pair, rows, DH), jnp.float32), pltpu.SemaphoreType.DMA((3, 3 * pair))],
         compiler_params=pltpu.CompilerParams(vmem_limit_bytes=24 * 2**20),
-    )(enter_other, key_other, grad_other, ga, keys, values, *high, own)
+    )(enter_other, key_other, grad_rest, ga, keys, values, *high, own)
 
 
 def solution(mesh):

time: 66.2 us -> 65.9 us (level)
  waiting for transfers between devices: 12.3 us -> 11.1 us
  starting transfers between devices: 38.5 us -> 39.4 us
    ppermute x16 -> x17, waiting for transfers between devices: 5.68 us -> 4.25 us  [along_seq(): return lax.ppermute(array, 'seq', pairs)]
    ppermute x16 -> x17, starting transfers between devices: 22.6 us -> 23.9 us  [along_seq(): return lax.ppermute(array, 'seq', pairs)]
    pallas_call x13 -> x14, Pallas kernels: 12.4 us -> 12.4 us  [call(): pl.pallas_call(kernel, out_shape=outs, in_specs=specs or [VMEM] * len(arg...]
  transfers between devices with their start and end apart: 23 -> 24, of which waited for: 11 -> 10; matrix products, arithmetic and copies ran while one was open for 0% -> 0% of each run, Pallas kernels for 17% -> 17%
where the time goes in v4:
time: 65.9 us; the launch traced here: 65.7 us
  starting transfers between devices  39.4 us (60%)
  Pallas kernels  14.3 us (22%)
  waiting for transfers between devices  11.1 us (17%)
  between operations  0.94 us (1%)
    ppermute x17, starting transfers between devices, along_seq(): return lax.ppermute(array, 'seq', pairs)  23.9 us
    ppermute x7, starting transfers between devices, along_z(): return lax.ppermute(array, ('seq', 'head'), pairs)  15.5 us
    pallas_call x14, Pallas kernels, call(): pl.pallas_call(kernel, out_shape=outs, in_specs=specs or [VMEM] * len(arg...  12.4 us
    ppermute x7, waiting for transfers between devices, along_z(): return lax.ppermute(array, ('seq', 'head'), pairs)  6.85 us
    ppermute x17, waiting for transfers between devices, along_seq(): return lax.ppermute(array, 'seq', pairs)  4.25 us
    pallas_call x1, Pallas kernels, local(): pl.pallas_call(functools.partial(rest_kernel, pair), out_shape=(f32(rows,...  1.85 us
  transfers between devices with their start and end apart: 24, of which 10 were waited for; matrix products, arithmetic and copies ran while one was open for 0% of the time, Pallas kernels for 17%

profile of v4, /device:TPU:1, one launch (start us, length us, event | category | flops | bytes accessed | tf_op | source)
XLA Modules:
  0.0 65.7 jit_solution(6260463034238364513)
XLA Ops:
  0.6 3.3 %collective-permute-start.1 = (bf16[512,384]{1,0:T(8,128)(2,1)}, bf16[512,384]{1,0:T(8,128)(2,1)S(1)}, u32[]{:S(2)}, u32[]{:S(2)}) collective-permute-start(bf16[512,384]{1,0:T(8,128)(2,1)} %c_hbm.1), channel_id=1, source_target_pairs={{0,8},{8,0},{16,24},{24,16},{32,40},{40,32},{48,56},{56,48},{64,72... | collective-permute-start | bytes 1179656 | tf_op jit(solution)/shard_map/ppermute | solution.py:429
  4.0 3.8 %collective-permute-start.6 = (bf16[512,384]{1,0:T(8,128)(2,1)}, bf16[512,384]{1,0:T(8,128)(2,1)S(1)}, u32[]{:S(2)}, u32[]{:S(2)}) collective-permute-start(bf16[512,384]{1,0:T(8,128)(2,1)} %c_hbm.1), channel_id=1, source_target_pairs={{0,1},{1,2},{2,3},{3,4},{4,5},{5,6},{6,7},{7,0},{8,15},{9,8},{10,9... | collective-permute-start | bytes 1179656 | tf_op jit(solution)/shard_map/ppermute | solution.py:422
  7.8 1.6 %collective-permute-start.2 = (bf16[512,384]{1,0:T(8,128)(2,1)S(1)}, bf16[512,384]{1,0:T(8,128)(2,1)S(1)}, u32[]{:S(2)}, u32[]{:S(2)}) collective-permute-start(bf16[512,384]{1,0:T(8,128)(2,1)S(1)} %collective-permute-done.1), channel_id=1, source_target_pairs={{0,1},{1,2},{2,3},{3,4},{4,5},{5,6},{6,7},{7,0},{8,15},{9,8},{10,9... | collective-permute-start | bytes 1179656 | tf_op jit(solution)/shard_map/ppermute | solution.py:422
  9.4 1.8 %shard_map.85 = (f32[520,128]{1,0:T(8,128)S(1)}, f32[8,128]{1,0:T(8,128)}) custom-call(bf16[512,512]{1,0:T(8,128)(2,1)} %refs_4_.3, bf16[512,512]{1,0:T(8,128)(2,1)} %refs_5_.3, f32[4,512]{1,0:T(4,128)} %ld_hbm.3, f32[8,128]{1,0:T(8,128)S(1)} %broadcast_in_dim.3.tie_ref), custom_call_target="tpu_custom_call" | custom-call | tf_op jit(solution)/shard_map/pallas_call | solution.py:32
  11.3 1.5 %collective-permute-done.6.a1 = bf16[512,384]{1,0:T(8,128)(2,1)S(1)} collective-permute-done((bf16[512,384]{1,0:T(8,128)(2,1)}, bf16[512,384]{1,0:T(8,128)(2,1)S(1)}, u32[]{:S(2)}, u32[]{:S(2)}) %collective-permute-start.6) | collective-permute-done | bytes 393248 | tf_op jit(solution)/shard_map/ppermute | solution.py:422
  12.8 3.0 %collective-permute-start.9 = (bf16[512,384]{1,0:T(8,128)(2,1)S(1)}, bf16[512,384]{1,0:T(8,128)(2,1)S(1)}, u32[]{:S(2)}, u32[]{:S(2)}) collective-permute-start(bf16[512,384]{1,0:T(8,128)(2,1)S(1)} %collective-permute-done.6.a1), channel_id=1, source_target_pairs={{0,1},{1,2},{2,3},{3,4},{4,5},{5,6},{6,7},{7,0},{8,15},{9,8},{10,9... | collective-permute-start | bytes 1179656 | tf_op jit(solution)/shard_map/ppermute | solution.py:422
  15.8 1.1 %collective-permute-done.2.tie_ref = bf16[512,384]{1,0:T(8,128)(2,1)S(1)} collective-permute-done((bf16[512,384]{1,0:T(8,128)(2,1)S(1)}, bf16[512,384]{1,0:T(8,128)(2,1)S(1)}, u32[]{:S(2)}, u32[]{:S(2)}) %collective-permute-start.2) | collective-permute-done | bytes 393248 | tf_op jit(solution)/shard_map/ppermute | solution.py:422
  17.0 3.2 %collective-permute-start.7 = (bf16[512,384]{1,0:T(8,128)(2,1)S(1)}, bf16[512,384]{1,0:T(8,128)(2,1)S(1)}, u32[]{:S(2)}, u32[]{:S(2)}) collective-permute-start(bf16[512,384]{1,0:T(8,128)(2,1)S(1)} %get-tuple-element.41.x_ref), channel_id=1, source_target_pairs={{0,1},{1,2},{2,3},{3,4},{4,5},{5,6},{6,7},{7,0},{8,15},{9,8},{10,9... | collective-permute-start | bytes 1179656 | tf_op jit(solution)/shard_map/ppermute | solution.py:422
  20.2 2.7 %collective-permute-start.5 = (bf16[272,128]{1,0:T(8,128)(2,1)S(1)}, bf16[272,128]{1,0:T(8,128)(2,1)S(1)}, u32[]{:S(2)}, u32[]{:S(2)}) collective-permute-start(bf16[272,128]{1,0:T(8,128)(2,1)S(1)} %get-tuple-element.38.sent_ref), channel_id=1, source_target_pairs={{0,32},{8,40},{16,48},{24,56},{32,0},{40,8},{48,16},{56,24},{64,96... | collective-permute-start | bytes 208904 | tf_op jit(solution)/shard_map/ppermute | solution.py:429
  23.0 0.9 %collective-permute-start.4 = (bf16[272,128]{1,0:T(8,128)(2,1)S(1)}, bf16[272,128]{1,0:T(8,128)(2,1)S(1)}, u32[]{:S(2)}, u32[]{:S(2)}) collective-permute-start(bf16[272,128]{1,0:T(8,128)(2,1)S(1)} %get-tuple-element.38.sent_ref), channel_id=1, source_target_pairs={{0,48},{8,56},{16,32},{24,40},{32,16},{40,24},{48,0},{56,8},{64,11... | collective-permute-start | bytes 208904 | tf_op jit(solution)/shard_map/ppermute | solution.py:429
  24.3 1.1 %collective-permute-done.7.refs_0_.x_ref = bf16[512,384]{1,0:T(8,128)(2,1)S(1)} collective-permute-done((bf16[512,384]{1,0:T(8,128)(2,1)S(1)}, bf16[512,384]{1,0:T(8,128)(2,1)S(1)}, u32[]{:S(2)}, u32[]{:S(2)}) %collective-permute-start.7) | collective-permute-done | bytes 393248 | tf_op jit(solution)/shard_map/ppermute | solution.py:422
  25.4 2.2 %collective-permute-start.8 = (bf16[512,384]{1,0:T(8,128)(2,1)S(1)}, bf16[512,384]{1,0:T(8,128)(2,1)S(1)}, u32[]{:S(2)}, u32[]{:S(2)}) collective-permute-start(bf16[512,384]{1,0:T(8,128)(2,1)S(1)} %shard_map.88), channel_id=1, source_target_pairs={{0,8},{8,0},{16,24},{24,16},{32,40},{40,32},{48,56},{56,48},{64,72... | collective-permute-start | bytes 1179656 | tf_op jit(solution)/shard_map/ppermute | solution.py:429
  27.8 1.5 %collective-permute-start.13 = (bf16[512,384]{1,0:T(8,128)(2,1)S(1)}, bf16[512,384]{1,0:T(8,128)(2,1)S(1)}, u32[]{:S(2)}, u32[]{:S(2)}) collective-permute-start(bf16[512,384]{1,0:T(8,128)(2,1)S(1)} %shard_map.90), channel_id=1, source_target_pairs={{0,1},{1,2},{2,3},{3,4},{4,5},{5,6},{6,7},{7,0},{8,15},{9,8},{10,9... | collective-permute-start | bytes 1179656 | tf_op jit(solution)/shard_map/ppermute | solution.py:422
  29.4 1.3 %collective-permute-done.11.a3 = bf16[512,384]{1,0:T(8,128)(2,1)S(1)} collective-permute-done((bf16[512,384]{1,0:T(8,128)(2,1)S(1)}, bf16[512,384]{1,0:T(8,128)(2,1)S(1)}, u32[]{:S(2)}, u32[]{:S(2)}) %collective-permute-start.11) | collective-permute-done | bytes 393248 | tf_op jit(solution)/shard_map/ppermute | solution.py:422
  30.7 2.0 %collective-permute-start.12 = (bf16[512,384]{1,0:T(8,128)(2,1)S(1)}, bf16[512,384]{1,0:T(8,128)(2,1)S(1)}, u32[]{:S(2)}, u32[]{:S(2)}) collective-permute-start(bf16[512,384]{1,0:T(8,128)(2,1)S(1)} %collective-permute-done.11.a3), channel_id=1, source_target_pairs={{0,1},{1,2},{2,3},{3,4},{4,5},{5,6},{6,7},{7,0},{8,15},{9,8},{10,9... | collective-permute-start | bytes 1179656 | tf_op jit(solution)/shard_map/ppermute | solution.py:422
  32.7 4.1 %shard_map.89 = (f32[512,512]{1,0:T(8,128)S(1)}, bf16[2,512,384]{2,1,0:T(8,128)(2,1)S(1)}, bf16[4,256,512]{2,1,0:T(8,128)(2,1)S(1)}, f32[4,512]{1,0:T(4,128)S(1)}, f32[512,4]{1,0:T(8,128)S(1)}) custom-call(bf16[512,3072]{1,0:T(8,128)(2,1)} %w_hbm.1, bf16[512,384]{1,0:T(8,128)(2,1)} %c_hbm.1, bf16[512,512]{1,0:T(8,128)(2,1)} %q_ref.3, f32[4,512]{1,0:T(4,128)} %ld_hbm.3, ...), custom_call_target="tpu_custom_call" | custom-call | tf_op jit(solution)/shard_map/pallas_call | solution.py:32
  36.9 0.5 collective-permute-start.14
  37.4 1.8 %collective-permute-done.12.a4 = bf16[512,384]{1,0:T(8,128)(2,1)S(1)} collective-permute-done((bf16[512,384]{1,0:T(8,128)(2,1)S(1)}, bf16[512,384]{1,0:T(8,128)(2,1)S(1)}, u32[]{:S(2)}, u32[]{:S(2)}) %collective-permute-start.12) | collective-permute-done | bytes 393248 | tf_op jit(solution)/shard_map/ppermute | solution.py:422
  39.2 1.2 %shard_map.92 = (bf16[512,512]{1,0:T(8,128)(2,1)S(1)}, f32[256,128]{1,0:T(8,128)S(1)}, f32[256,128]{1,0:T(8,128)S(1)}) custom-call(f32[512,512]{1,0:T(8,128)S(1)} %get-tuple-element.43.refs_0_.acc_ref, bf16[512,384]{1,0:T(8,128)(2,1)S(1)} %collective-permute-done.12.a4, bf16[512,384]{1,0:T(8,128)(2,1)S(1)} %collective-permute-done.14.b3, ...), custom_call_target="tpu_custom_call" | custom-call | tf_op jit(solution)/shard_map/pallas_call | solution.py:32
  40.4 2.4 %collective-permute-start.15 = (f32[256,128]{1,0:T(8,128)S(1)}, f32[256,128]{1,0:T(8,128)S(1)}, u32[]{:S(2)}, u32[]{:S(2)}) collective-permute-start(f32[256,128]{1,0:T(8,128)S(1)} %get-tuple-element.47), channel_id=1, source_target_pairs={{0,8},{8,0},{16,24},{24,16},{32,40},{40,32},{48,56},{56,48},{64,72... | collective-permute-start | bytes 393224 | tf_op jit(solution)/shard_map/ppermute | solution.py:429
  42.7 1.0 %collective-permute-done.15.grad_other.refs_2_ = f32[256,128]{1,0:T(8,128)S(1)} collective-permute-done((f32[256,128]{1,0:T(8,128)S(1)}, f32[256,128]{1,0:T(8,128)S(1)}, u32[]{:S(2)}, u32[]{:S(2)}) %collective-permute-start.15) | collective-permute-done | bytes 131104 | tf_op jit(solution)/shard_map/ppermute | solution.py:429
  43.8 2.8 %collective-permute-start.18 = (bf16[256,128]{1,0:T(8,128)(2,1)S(1)}, bf16[256,128]{1,0:T(8,128)(2,1)S(1)}, u32[]{:S(2)}, u32[]{:S(2)}) collective-permute-start(bf16[256,128]{1,0:T(8,128)(2,1)S(1)} %get-tuple-element.49), channel_id=1, source_target_pairs={{0,32},{8,40},{16,48},{24,56},{32,0},{40,8},{48,16},{56,24},{64,96... | collective-permute-start | bytes 196616 | tf_op jit(solution)/shard_map/ppermute | solution.py:429
  46.6 0.9 %collective-permute-start.17 = (bf16[256,128]{1,0:T(8,128)(2,1)S(1)}, bf16[256,128]{1,0:T(8,128)(2,1)S(1)}, u32[]{:S(2)}, u32[]{:S(2)}) collective-permute-start(bf16[256,128]{1,0:T(8,128)(2,1)S(1)} %get-tuple-element.49), channel_id=1, source_target_pairs={{0,48},{8,56},{16,32},{24,40},{32,16},{40,24},{48,0},{56,8},{64,11... | collective-permute-start | bytes 196616 | tf_op jit(solution)/shard_map/ppermute | solution.py:429
  47.5 0.9 %collective-permute-start.22 = (f32[256,128]{1,0:T(8,128)S(1)}, f32[256,128]{1,0:T(8,128)S(1)}, u32[]{:S(2)}, u32[]{:S(2)}) collective-permute-start(f32[256,128]{1,0:T(8,128)S(1)} %get-tuple-element.46.grad_ref), channel_id=1, source_target_pairs={{0,8},{8,0},{16,24},{24,16},{32,40},{40,32},{48,56},{56,48},{64,72... | collective-permute-start | bytes 393224 | tf_op jit(solution)/shard_map/ppermute | solution.py:429
  48.4 2.1 %shard_map.94 = (f32[512,256]{1,0:T(8,128)S(1)}, f32[512,256]{1,0:T(8,128)S(1)}, f32[512,256]{1,0:T(8,128)S(1)}, f32[512,256]{1,0:T(8,128)S(1)}, f32[512,256]{1,0:T(8,128)S(1)}, /*index=5*/f32[8,128]{1,0:T(8,128)S(1)}) custom-call(f32[4,512]{1,0:T(4,128)S(1)} %get-tuple-element.52._.row_ref, bf16[512,512]{1,0:T(8,128)(2,1)S(1)} %copy-done.2, ...), custom_call_target="tpu_custom_call" | custom-call | tf_op jit(solution)/shard_map/pallas_call | solution.py:32
  51.0 3.0 %collective-permute-start.19 = (bf16[272,128]{1,0:T(8,128)(2,1)S(1)}, bf16[272,128]{1,0:T(8,128)(2,1)S(1)}, u32[]{:S(2)}, u32[]{:S(2)}) collective-permute-start(bf16[272,128]{1,0:T(8,128)(2,1)S(1)} %get-tuple-element.57), channel_id=1, source_target_pairs={{0,128},{8,136},{16,144},{24,152},{32,160},{40,168},{48,176},{56,1... | collective-permute-start | bytes 208904 | tf_op jit(solution)/shard_map/ppermute | solution.py:429
  54.8 2.1 %shard_map.96 = (f32[512,256]{1,0:T(8,128)S(1)}, f32[512,256]{1,0:T(8,128)S(1)}, f32[512,256]{1,0:T(8,128)S(1)}, f32[512,256]{1,0:T(8,128)S(1)}, f32[512,256]{1,0:T(8,128)S(1)}, /*index=5*/f32[8,128]{1,0:T(8,128)S(1)}) custom-call(f32[256,128]{1,0:T(8,128)S(1)} %collective-permute-done.22._.refs_2_, bf16[512,512]{1,0:T(8,128)(2,1)S(1)} %copy-done.2, ...), custom_call_target="tpu_custom_call" | custom-call | tf_op jit(solution)/shard_map/pallas_call | solution.py:32
  57.2 1.9 %collective-permute-done.21.r3 = bf16[272,128]{1,0:T(8,128)(2,1)S(1)} collective-permute-done((bf16[272,128]{1,0:T(8,128)(2,1)S(1)}, bf16[272,128]{1,0:T(8,128)(2,1)S(1)}, u32[]{:S(2)}, u32[]{:S(2)}) %collective-permute-start.21) | collective-permute-done | bytes 69664 | tf_op jit(solution)/shard_map/ppermute | solution.py:429
  59.2 3.3 %collective-permute-start.23 = (f32[512,128]{1,0:T(8,128)S(1)}, f32[512,128]{1,0:T(8,128)S(1)}, u32[]{:S(2)}, u32[]{:S(2)}) collective-permute-start(f32[512,128]{1,0:T(8,128)S(1)} %shard_map.97.refs_0_), channel_id=1, source_target_pairs={{0,8},{8,0},{16,24},{24,16},{32,40},{40,32},{48,56},{56,48},{64,72... | collective-permute-start | bytes 786440 | tf_op jit(solution)/shard_map/ppermute | solution.py:429
  62.5 0.6 shard_map.98.refs_11_
  63.1 0.5 collective-permute-done.23.refs_0_
  63.7 1.9 %shard_map.99 = (f32[512,512]{1,0:T(8,128)}, f32[512,512]{1,0:T(8,128)}, f32[512,512]{1,0:T(8,128)}) custom-call(f32[512,128]{1,0:T(8,128)S(1)} %collective-permute-done.23.refs_0_, f32[520,128]{1,0:T(8,128)S(1)} %collective-permute-done.key_other.refs_1_, f32[256,128]{1,0:T(8,128)S(1)} %collective-permute-done.22._.refs_2_, ...), custom_call_target="tpu_custom_call" | custom-call | tf_op jit(solution)/shard_map/pallas_call | solution.py:518
  (38 shorter events, 2.9 us)
Async XLA Ops:
  0.6 7.2 %collective-permute-start.1 = (bf16[512,384]{1,0:T(8,128)(2,1)}, bf16[512,384]{1,0:T(8,128)(2,1)S(1)}, u32[]{:S(2)}, u32[]{:S(2)}) collective-permute-start(bf16[512,384]{1,0:T(8,128)(2,1)} %c_hbm.1), channel_id=1, source_target_pairs={{0,8},{8,0},{16,24},{24,16},{32,40},{40,32},{48,56},{56,48},{64,72... | collective-permute-start | bytes 1179656 | tf_op jit(solution)/shard_map/ppermute | solution.py:429
  4.0 8.9 %collective-permute-start.6 = (bf16[512,384]{1,0:T(8,128)(2,1)}, bf16[512,384]{1,0:T(8,128)(2,1)S(1)}, u32[]{:S(2)}, u32[]{:S(2)}) collective-permute-start(bf16[512,384]{1,0:T(8,128)(2,1)} %c_hbm.1), channel_id=1, source_target_pairs={{0,1},{1,2},{2,3},{3,4},{4,5},{5,6},{6,7},{7,0},{8,15},{9,8},{10,9... | collective-permute-start | bytes 1179656 | tf_op jit(solution)/shard_map/ppermute | solution.py:422
  7.8 9.1 %collective-permute-start.2 = (bf16[512,384]{1,0:T(8,128)(2,1)S(1)}, bf16[512,384]{1,0:T(8,128)(2,1)S(1)}, u32[]{:S(2)}, u32[]{:S(2)}) collective-permute-start(bf16[512,384]{1,0:T(8,128)(2,1)S(1)} %collective-permute-done.1), channel_id=1, source_target_pairs={{0,1},{1,2},{2,3},{3,4},{4,5},{5,6},{6,7},{7,0},{8,15},{9,8},{10,9... | collective-permute-start | bytes 1179656 | tf_op jit(solution)/shard_map/ppermute | solution.py:422
  11.2 4.6 %collective-permute-start = (f32[520,128]{1,0:T(8,128)S(1)}, f32[520,128]{1,0:T(8,128)S(1)}, u32[]{:S(2)}, u32[]{:S(2)}) collective-permute-start(f32[520,128]{1,0:T(8,128)S(1)} %get-tuple-element.37.key_ref), channel_id=1, source_target_pairs={{0,8},{8,0},{16,24},{24,16},{32,40},{40,32},{48,56},{56,48},{64,72... | collective-permute-start | bytes 798728 | tf_op jit(solution)/shard_map/ppermute | solution.py:429
  12.8 11.0 %collective-permute-start.9 = (bf16[512,384]{1,0:T(8,128)(2,1)S(1)}, bf16[512,384]{1,0:T(8,128)(2,1)S(1)}, u32[]{:S(2)}, u32[]{:S(2)}) collective-permute-start(bf16[512,384]{1,0:T(8,128)(2,1)S(1)} %collective-permute-done.6.a1), channel_id=1, source_target_pairs={{0,1},{1,2},{2,3},{3,4},{4,5},{5,6},{6,7},{7,0},{8,15},{9,8},{10,9... | collective-permute-start | bytes 1179656 | tf_op jit(solution)/shard_map/ppermute | solution.py:422
  17.0 8.3 %collective-permute-start.7 = (bf16[512,384]{1,0:T(8,128)(2,1)S(1)}, bf16[512,384]{1,0:T(8,128)(2,1)S(1)}, u32[]{:S(2)}, u32[]{:S(2)}) collective-permute-start(bf16[512,384]{1,0:T(8,128)(2,1)S(1)} %get-tuple-element.41.x_ref), channel_id=1, source_target_pairs={{0,1},{1,2},{2,3},{3,4},{4,5},{5,6},{6,7},{7,0},{8,15},{9,8},{10,9... | collective-permute-start | bytes 1179656 | tf_op jit(solution)/shard_map/ppermute | solution.py:422
  20.2 7.4 %collective-permute-start.5 = (bf16[272,128]{1,0:T(8,128)(2,1)S(1)}, bf16[272,128]{1,0:T(8,128)(2,1)S(1)}, u32[]{:S(2)}, u32[]{:S(2)}) collective-permute-start(bf16[272,128]{1,0:T(8,128)(2,1)S(1)} %get-tuple-element.38.sent_ref), channel_id=1, source_target_pairs={{0,32},{8,40},{16,48},{24,56},{32,0},{40,8},{48,16},{56,24},{64,96... | collective-permute-start | bytes 208904 | tf_op jit(solution)/shard_map/ppermute | solution.py:429
  23.0 4.8 %collective-permute-start.4 = (bf16[272,128]{1,0:T(8,128)(2,1)S(1)}, bf16[272,128]{1,0:T(8,128)(2,1)S(1)}, u32[]{:S(2)}, u32[]{:S(2)}) collective-permute-start(bf16[272,128]{1,0:T(8,128)(2,1)S(1)} %get-tuple-element.38.sent_ref), channel_id=1, source_target_pairs={{0,48},{8,56},{16,32},{24,40},{32,16},{40,24},{48,0},{56,8},{64,11... | collective-permute-start | bytes 208904 | tf_op jit(solution)/shard_map/ppermute | solution.py:429
  23.8 3.9 %collective-permute-start.3 = (bf16[272,128]{1,0:T(8,128)(2,1)S(1)}, bf16[272,128]{1,0:T(8,128)(2,1)S(1)}, u32[]{:S(2)}, u32[]{:S(2)}) collective-permute-start(bf16[272,128]{1,0:T(8,128)(2,1)S(1)} %get-tuple-element.38.sent_ref), channel_id=1, source_target_pairs={{0,16},{8,24},{16,0},{24,8},{32,48},{40,56},{48,32},{56,40},{64,80... | collective-permute-start | bytes 208904 | tf_op jit(solution)/shard_map/ppermute | solution.py:429
  23.8 6.9 %collective-permute-start.11 = (bf16[512,384]{1,0:T(8,128)(2,1)S(1)}, bf16[512,384]{1,0:T(8,128)(2,1)S(1)}, u32[]{:S(2)}, u32[]{:S(2)}) collective-permute-start(bf16[512,384]{1,0:T(8,128)(2,1)S(1)} %collective-permute-done.9.a2), channel_id=1, source_target_pairs={{0,1},{1,2},{2,3},{3,4},{4,5},{5,6},{6,7},{7,0},{8,15},{9,8},{10,9... | collective-permute-start | bytes 1179656 | tf_op jit(solution)/shard_map/ppermute | solution.py:422
  25.4 7.3 %collective-permute-start.8 = (bf16[512,384]{1,0:T(8,128)(2,1)S(1)}, bf16[512,384]{1,0:T(8,128)(2,1)S(1)}, u32[]{:S(2)}, u32[]{:S(2)}) collective-permute-start(bf16[512,384]{1,0:T(8,128)(2,1)S(1)} %shard_map.88), channel_id=1, source_target_pairs={{0,8},{8,0},{16,24},{24,16},{32,40},{40,32},{48,56},{56,48},{64,72... | collective-permute-start | bytes 1179656 | tf_op jit(solution)/shard_map/ppermute | solution.py:429
  27.6 5.1 %collective-permute-start.10 = (bf16[512,384]{1,0:T(8,128)(2,1)S(1)}, bf16[512,384]{1,0:T(8,128)(2,1)S(1)}, u32[]{:S(2)}, u32[]{:S(2)}) collective-permute-start(bf16[512,384]{1,0:T(8,128)(2,1)S(1)} %collective-permute-done.7.refs_0_.x_ref), channel_id=1, source_target_pairs={{0,8},{8,0},{16,24},{24,16},{32,40},{40,32},{48,56},{56,48},{64,72... | collective-permute-start | bytes 1179656 | tf_op jit(solution)/shard_map/ppermute | solution.py:429
  27.8 9.0 %collective-permute-start.13 = (bf16[512,384]{1,0:T(8,128)(2,1)S(1)}, bf16[512,384]{1,0:T(8,128)(2,1)S(1)}, u32[]{:S(2)}, u32[]{:S(2)}) collective-permute-start(bf16[512,384]{1,0:T(8,128)(2,1)S(1)} %shard_map.90), channel_id=1, source_target_pairs={{0,1},{1,2},{2,3},{3,4},{4,5},{5,6},{6,7},{7,0},{8,15},{9,8},{10,9... | collective-permute-start | bytes 1179656 | tf_op jit(solution)/shard_map/ppermute | solution.py:422
  30.7 8.4 %collective-permute-start.12 = (bf16[512,384]{1,0:T(8,128)(2,1)S(1)}, bf16[512,384]{1,0:T(8,128)(2,1)S(1)}, u32[]{:S(2)}, u32[]{:S(2)}) collective-permute-start(bf16[512,384]{1,0:T(8,128)(2,1)S(1)} %collective-permute-done.11.a3), channel_id=1, source_target_pairs={{0,1},{1,2},{2,3},{3,4},{4,5},{5,6},{6,7},{7,0},{8,15},{9,8},{10,9... | collective-permute-start | bytes 1179656 | tf_op jit(solution)/shard_map/ppermute | solution.py:422
  36.8 11.6 %copy-start = (bf16[512,512]{1,0:T(8,128)(2,1)S(1)}, bf16[512,512]{1,0:T(8,128)(2,1)}, u32[]{:S(2)}) copy-start(bf16[512,512]{1,0:T(8,128)(2,1)} %refs_4_.3) | copy-start | bytes 1572868
  36.8 11.6 %copy-start.1 = (bf16[512,512]{1,0:T(8,128)(2,1)S(1)}, bf16[512,512]{1,0:T(8,128)(2,1)}, u32[]{:S(2)}) copy-start(bf16[512,512]{1,0:T(8,128)(2,1)} %refs_5_.3) | copy-start | bytes 1572868
  36.8 11.6 %copy-start.2 = (bf16[512,512]{1,0:T(8,128)(2,1)S(1)}, bf16[512,512]{1,0:T(8,128)(2,1)}, u32[]{:S(2)}) copy-start(bf16[512,512]{1,0:T(8,128)(2,1)} %q_ref.3) | copy-start | bytes 1572868
  36.9 2.3 %collective-permute-start.14 = (bf16[512,384]{1,0:T(8,128)(2,1)S(1)}, bf16[512,384]{1,0:T(8,128)(2,1)S(1)}, u32[]{:S(2)}, u32[]{:S(2)}) collective-permute-start(bf16[512,384]{1,0:T(8,128)(2,1)S(1)} %shard_map.91), channel_id=1, source_target_pairs={{0,8},{8,0},{16,24},{24,16},{32,40},{40,32},{48,56},{56,48},{64,72... | collective-permute-start | bytes 1179656 | tf_op jit(solution)/shard_map/ppermute | solution.py:429
  40.4 3.4 %collective-permute-start.15 = (f32[256,128]{1,0:T(8,128)S(1)}, f32[256,128]{1,0:T(8,128)S(1)}, u32[]{:S(2)}, u32[]{:S(2)}) collective-permute-start(f32[256,128]{1,0:T(8,128)S(1)} %get-tuple-element.47), channel_id=1, source_target_pairs={{0,8},{8,0},{16,24},{24,16},{32,40},{40,32},{48,56},{56,48},{64,72... | collective-permute-start | bytes 393224 | tf_op jit(solution)/shard_map/ppermute | solution.py:429
  43.8 6.7 %collective-permute-start.18 = (bf16[256,128]{1,0:T(8,128)(2,1)S(1)}, bf16[256,128]{1,0:T(8,128)(2,1)S(1)}, u32[]{:S(2)}, u32[]{:S(2)}) collective-permute-start(bf16[256,128]{1,0:T(8,128)(2,1)S(1)} %get-tuple-element.49), channel_id=1, source_target_pairs={{0,32},{8,40},{16,48},{24,56},{32,0},{40,8},{48,16},{56,24},{64,96... | collective-permute-start | bytes 196616 | tf_op jit(solution)/shard_map/ppermute | solution.py:429
  46.6 4.3 %collective-permute-start.17 = (bf16[256,128]{1,0:T(8,128)(2,1)S(1)}, bf16[256,128]{1,0:T(8,128)(2,1)S(1)}, u32[]{:S(2)}, u32[]{:S(2)}) collective-permute-start(bf16[256,128]{1,0:T(8,128)(2,1)S(1)} %get-tuple-element.49), channel_id=1, source_target_pairs={{0,48},{8,56},{16,32},{24,40},{32,16},{40,24},{48,0},{56,8},{64,11... | collective-permute-start | bytes 196616 | tf_op jit(solution)/shard_map/ppermute | solution.py:429
  47.5 3.5 %collective-permute-start.16 = (bf16[256,128]{1,0:T(8,128)(2,1)S(1)}, bf16[256,128]{1,0:T(8,128)(2,1)S(1)}, u32[]{:S(2)}, u32[]{:S(2)}) collective-permute-start(bf16[256,128]{1,0:T(8,128)(2,1)S(1)} %get-tuple-element.49), channel_id=1, source_target_pairs={{0,16},{8,24},{16,0},{24,8},{32,48},{40,56},{48,32},{56,40},{64,80... | collective-permute-start | bytes 196616 | tf_op jit(solution)/shard_map/ppermute | solution.py:429
  47.5 7.3 %collective-permute-start.22 = (f32[256,128]{1,0:T(8,128)S(1)}, f32[256,128]{1,0:T(8,128)S(1)}, u32[]{:S(2)}, u32[]{:S(2)}) collective-permute-start(f32[256,128]{1,0:T(8,128)S(1)} %get-tuple-element.46.grad_ref), channel_id=1, source_target_pairs={{0,8},{8,0},{16,24},{24,16},{32,40},{40,32},{48,56},{56,48},{64,72... | collective-permute-start | bytes 393224 | tf_op jit(solution)/shard_map/ppermute | solution.py:429
  51.0 5.8 %collective-permute-start.19 = (bf16[272,128]{1,0:T(8,128)(2,1)S(1)}, bf16[272,128]{1,0:T(8,128)(2,1)S(1)}, u32[]{:S(2)}, u32[]{:S(2)}) collective-permute-start(bf16[272,128]{1,0:T(8,128)(2,1)S(1)} %get-tuple-element.57), channel_id=1, source_target_pairs={{0,128},{8,136},{16,144},{24,152},{32,160},{40,168},{48,176},{56,1... | collective-permute-start | bytes 208904 | tf_op jit(solution)/shard_map/ppermute | solution.py:429
  54.0 3.2 %collective-permute-start.20 = (bf16[272,128]{1,0:T(8,128)(2,1)S(1)}, bf16[272,128]{1,0:T(8,128)(2,1)S(1)}, u32[]{:S(2)}, u32[]{:S(2)}) collective-permute-start(bf16[272,128]{1,0:T(8,128)(2,1)S(1)} %get-tuple-element.58), channel_id=1, source_target_pairs={{0,64},{8,72},{16,80},{24,88},{32,96},{40,104},{48,112},{56,120},{... | collective-permute-start | bytes 208904 | tf_op jit(solution)/shard_map/ppermute | solution.py:429
  54.4 4.7 %collective-permute-start.21 = (bf16[272,128]{1,0:T(8,128)(2,1)S(1)}, bf16[272,128]{1,0:T(8,128)(2,1)S(1)}, u32[]{:S(2)}, u32[]{:S(2)}) collective-permute-start(bf16[272,128]{1,0:T(8,128)(2,1)S(1)} %get-tuple-element.59), channel_id=1, source_target_pairs={{0,192},{8,200},{16,208},{24,216},{32,224},{40,232},{48,240},{56,2... | collective-permute-start | bytes 208904 | tf_op jit(solution)/shard_map/ppermute | solution.py:429
  59.2 4.4 %collective-permute-start.23 = (f32[512,128]{1,0:T(8,128)S(1)}, f32[512,128]{1,0:T(8,128)S(1)}, u32[]{:S(2)}, u32[]{:S(2)}) collective-permute-start(f32[512,128]{1,0:T(8,128)S(1)} %shard_map.97.refs_0_), channel_id=1, source_target_pairs={{0,8},{8,0},{16,24},{24,16},{32,40},{40,32},{48,56},{56,48},{64,72... | collective-permute-start | bytes 786440 | tf_op jit(solution)/shard_map/ppermute | solution.py:429

commit v5 on v4

--- a/solution.py
+++ b/solution.py
@@ -372,19 +372,34 @@
 
 
 def own_kernel(first, *refs):
-    *inputs, out_ref = refs
-    step = out_ref.shape[2] // 4
+    *inputs, gq_ref, gk_ref, gv_ref, out_ref, room, sems = refs
+    outs = (gq_ref, gk_ref, gv_ref)
+    n = out_ref.shape[2]
+    step = n // 4
     states = {}
-    for i in range(out_ref.shape[1]):
+    copies = []
+    for i in range(1 + out_ref.shape[1]):
         for part in range(4):
+            at = pl.ds(part * step, step)
             for j, value in enumerate(closed(first, i, part, *inputs, states)):
-                out_ref[j, i, pl.ds(part * step, step)] = value
+                if i:
+                    out_ref[j, i - 1, at] = value
+                else:
+                    room[j, at] = value
+        if i == 0:
+            for j in range(3):
+                copy = pltpu.make_async_copy(room.at[j], outs[j].at[:, head_columns(first)], sems.at[j])
+                copy.start()
+                copies.append(copy)
+    for copy in copies:
+        copy.wait()
 
 
 def rest_kernel(first, *refs):
-    *inputs, own_ref, gq_ref, gk_ref, gv_ref, room, sems = refs
+    inputs, own_ref, (gq_ref, gk_ref, gv_ref, room, sems) = refs[:11], refs[11], refs[-5:]
     outs = (gq_ref, gk_ref, gv_ref)
-    pair, n = own_ref.shape[1:3]
+    n = own_ref.shape[2]
+    pair = room.shape[1]
     step = n // 4
     copies = []
 
@@ -393,9 +408,8 @@
         copy.start()
         copies.append(copy)
 
-    for i in range(pair):
-        for j in range(3):
-            send(own_ref.at[j, i], j, i, pl.ds(0, n), sems.at[j, i])
+    for j in range(3):
+        send(own_ref.at[j, 0], j, 1, pl.ds(0, n), sems.at[j, 0])
     states = {}
     for i in range(pair):
         for part in range(4):
@@ -512,17 +526,25 @@
     )
     enter_other = other(enter)
 
-    (own,) = call(
-        functools.partial(own_kernel, 0), (f32(3, pair, rows, DH),), enter, key_other, grad_other, ga, keys, values, *low
-    )
-    return pl.pallas_call(
-        functools.partial(rest_kernel, pair),
-        out_shape=(f32(rows, width),) * 3,
-        in_specs=[VMEM] * 12,
-        out_specs=(ANY,) * 3,
-        scratch_shapes=[pltpu.VMEM((3, pair, rows, DH), jnp.float32), pltpu.SemaphoreType.DMA((3, 3 * pair))],
+    *done, own = pl.pallas_call(
+        functools.partial(own_kernel, 0),
+        out_shape=(f32(rows, width),) * 3 + (f32(3, 1, rows, DH),),
+        in_specs=[VMEM] * 11,
+        out_specs=(ANY,) * 3 + (VMEM,),
+        scratch_shapes=[pltpu.VMEM((3, rows, DH), jnp.float32), pltpu.SemaphoreType.DMA((3,))],
         compiler_params=pltpu.CompilerParams(vmem_limit_bytes=24 * 2**20),
-    )(enter_other, key_other, grad_rest, ga, keys, values, *high, own)
+    )(enter, key_other, grad_other, ga, keys, values, *low)
+    return tuple(
+        pl.pallas_call(
+            functools.partial(rest_kernel, pair),
+            out_shape=(f32(rows, width),) * 3,
+            in_specs=[VMEM] * 12 + [ANY] * 3,
+            out_specs=(ANY,) * 3,
+            scratch_shapes=[pltpu.VMEM((3, pair, rows, DH), jnp.float32), pltpu.SemaphoreType.DMA((3, 3 * pair))],
+            input_output_aliases={12 + j: j for j in range(3)},
+            compiler_params=pltpu.CompilerParams(vmem_limit_bytes=24 * 2**20),
+        )(enter_other, key_other, grad_rest, ga, keys, values, *high, own, *done)
+    )
 
 
 def solution(mesh):

time: 65.9 us -> 65.9 us (level)
    pallas_call x0 -> x1, Pallas kernels: none -> 1.31 us  [local(): pl.pallas_call(functools.partial(own_kernel, 0), out_shape=(f32(rows, wid...]
    pallas_call x14 -> x13, Pallas kernels: 12.4 us -> 11.8 us  [call(): pl.pallas_call(kernel, out_shape=outs, in_specs=specs or [VMEM] * len(arg...]
  transfers between devices with their start and end apart: 24 -> 24, of which waited for: 10 -> 9; matrix products, arithmetic and copies ran while one was open for 0% -> 0% of each run, Pallas kernels for 17% -> 18%
where the time goes in v5:
time: 65.9 us; the launch traced here: 65.7 us
  starting transfers between devices  39.4 us (60%)
  Pallas kernels  14.8 us (22%)
  waiting for transfers between devices  10.6 us (16%)
  between operations  0.95 us (1%)
    ppermute x17, starting transfers between devices, along_seq(): return lax.ppermute(array, 'seq', pairs)  23.9 us
    ppermute x7, starting transfers between devices, along_z(): return lax.ppermute(array, ('seq', 'head'), pairs)  15.5 us
    pallas_call x13, Pallas kernels, call(): pl.pallas_call(kernel, out_shape=outs, in_specs=specs or [VMEM] * len(arg...  11.8 us
    ppermute x7, waiting for transfers between devices, along_z(): return lax.ppermute(array, ('seq', 'head'), pairs)  6.85 us
    ppermute x17, waiting for transfers between devices, along_seq(): return lax.ppermute(array, 'seq', pairs)  3.71 us
    pallas_call x1, Pallas kernels, local(): pl.pallas_call(functools.partial(rest_kernel, pair), out_shape=(f32(rows,...  1.72 us
  transfers between devices with their start and end apart: 24, of which 9 were waited for; matrix products, arithmetic and copies ran while one was open for 0% of the time, Pallas kernels for 18%

profile of v5, /device:TPU:1, one launch (start us, length us, event | category | flops | bytes accessed | tf_op | source)
XLA Modules:
  0.0 65.7 jit_solution(1605254401630634636)
XLA Ops:
  0.6 3.3 %collective-permute-start.1 = (bf16[512,384]{1,0:T(8,128)(2,1)}, bf16[512,384]{1,0:T(8,128)(2,1)S(1)}, u32[]{:S(2)}, u32[]{:S(2)}) collective-permute-start(bf16[512,384]{1,0:T(8,128)(2,1)} %c_hbm.1), channel_id=1, source_target_pairs={{0,8},{8,0},{16,24},{24,16},{32,40},{40,32},{48,56},{56,48},{64,72... | collective-permute-start | bytes 1179656 | tf_op jit(solution)/shard_map/ppermute | solution.py:443
  4.0 3.8 %collective-permute-start.6 = (bf16[512,384]{1,0:T(8,128)(2,1)}, bf16[512,384]{1,0:T(8,128)(2,1)S(1)}, u32[]{:S(2)}, u32[]{:S(2)}) collective-permute-start(bf16[512,384]{1,0:T(8,128)(2,1)} %c_hbm.1), channel_id=1, source_target_pairs={{0,1},{1,2},{2,3},{3,4},{4,5},{5,6},{6,7},{7,0},{8,15},{9,8},{10,9... | collective-permute-start | bytes 1179656 | tf_op jit(solution)/shard_map/ppermute | solution.py:436
  7.8 1.6 %collective-permute-start.2 = (bf16[512,384]{1,0:T(8,128)(2,1)S(1)}, bf16[512,384]{1,0:T(8,128)(2,1)S(1)}, u32[]{:S(2)}, u32[]{:S(2)}) collective-permute-start(bf16[512,384]{1,0:T(8,128)(2,1)S(1)} %collective-permute-done.1), channel_id=1, source_target_pairs={{0,1},{1,2},{2,3},{3,4},{4,5},{5,6},{6,7},{7,0},{8,15},{9,8},{10,9... | collective-permute-start | bytes 1179656 | tf_op jit(solution)/shard_map/ppermute | solution.py:436
  9.4 1.8 %shard_map.85 = (f32[520,128]{1,0:T(8,128)S(1)}, f32[8,128]{1,0:T(8,128)}) custom-call(bf16[512,512]{1,0:T(8,128)(2,1)} %refs_4_.3, bf16[512,512]{1,0:T(8,128)(2,1)} %refs_5_.3, f32[4,512]{1,0:T(4,128)} %ld_hbm.3, f32[8,128]{1,0:T(8,128)S(1)} %broadcast_in_dim.3.tie_ref), custom_call_target="tpu_custom_call" | custom-call | tf_op jit(solution)/shard_map/pallas_call | solution.py:32
  11.3 1.5 %collective-permute-done.6.a1 = bf16[512,384]{1,0:T(8,128)(2,1)S(1)} collective-permute-done((bf16[512,384]{1,0:T(8,128)(2,1)}, bf16[512,384]{1,0:T(8,128)(2,1)S(1)}, u32[]{:S(2)}, u32[]{:S(2)}) %collective-permute-start.6) | collective-permute-done | bytes 393248 | tf_op jit(solution)/shard_map/ppermute | solution.py:436
  12.8 3.0 %collective-permute-start.9 = (bf16[512,384]{1,0:T(8,128)(2,1)S(1)}, bf16[512,384]{1,0:T(8,128)(2,1)S(1)}, u32[]{:S(2)}, u32[]{:S(2)}) collective-permute-start(bf16[512,384]{1,0:T(8,128)(2,1)S(1)} %collective-permute-done.6.a1), channel_id=1, source_target_pairs={{0,1},{1,2},{2,3},{3,4},{4,5},{5,6},{6,7},{7,0},{8,15},{9,8},{10,9... | collective-permute-start | bytes 1179656 | tf_op jit(solution)/shard_map/ppermute | solution.py:436
  15.8 1.1 %collective-permute-done.2.tie_ref = bf16[512,384]{1,0:T(8,128)(2,1)S(1)} collective-permute-done((bf16[512,384]{1,0:T(8,128)(2,1)S(1)}, bf16[512,384]{1,0:T(8,128)(2,1)S(1)}, u32[]{:S(2)}, u32[]{:S(2)}) %collective-permute-start.2) | collective-permute-done | bytes 393248 | tf_op jit(solution)/shard_map/ppermute | solution.py:436
  17.0 3.2 %collective-permute-start.7 = (bf16[512,384]{1,0:T(8,128)(2,1)S(1)}, bf16[512,384]{1,0:T(8,128)(2,1)S(1)}, u32[]{:S(2)}, u32[]{:S(2)}) collective-permute-start(bf16[512,384]{1,0:T(8,128)(2,1)S(1)} %get-tuple-element.45.x_ref), channel_id=1, source_target_pairs={{0,1},{1,2},{2,3},{3,4},{4,5},{5,6},{6,7},{7,0},{8,15},{9,8},{10,9... | collective-permute-start | bytes 1179656 | tf_op jit(solution)/shard_map/ppermute | solution.py:436
  20.2 2.7 %collective-permute-start.5 = (bf16[272,128]{1,0:T(8,128)(2,1)S(1)}, bf16[272,128]{1,0:T(8,128)(2,1)S(1)}, u32[]{:S(2)}, u32[]{:S(2)}) collective-permute-start(bf16[272,128]{1,0:T(8,128)(2,1)S(1)} %get-tuple-element.42.sent_ref), channel_id=1, source_target_pairs={{0,32},{8,40},{16,48},{24,56},{32,0},{40,8},{48,16},{56,24},{64,96... | collective-permute-start | bytes 208904 | tf_op jit(solution)/shard_map/ppermute | solution.py:443
  23.0 0.9 %collective-permute-start.4 = (bf16[272,128]{1,0:T(8,128)(2,1)S(1)}, bf16[272,128]{1,0:T(8,128)(2,1)S(1)}, u32[]{:S(2)}, u32[]{:S(2)}) collective-permute-start(bf16[272,128]{1,0:T(8,128)(2,1)S(1)} %get-tuple-element.42.sent_ref), channel_id=1, source_target_pairs={{0,48},{8,56},{16,32},{24,40},{32,16},{40,24},{48,0},{56,8},{64,11... | collective-permute-start | bytes 208904 | tf_op jit(solution)/shard_map/ppermute | solution.py:443
  24.3 1.1 %collective-permute-done.7.refs_0_.x_ref = bf16[512,384]{1,0:T(8,128)(2,1)S(1)} collective-permute-done((bf16[512,384]{1,0:T(8,128)(2,1)S(1)}, bf16[512,384]{1,0:T(8,128)(2,1)S(1)}, u32[]{:S(2)}, u32[]{:S(2)}) %collective-permute-start.7) | collective-permute-done | bytes 393248 | tf_op jit(solution)/shard_map/ppermute | solution.py:436
  25.4 2.2 %collective-permute-start.8 = (bf16[512,384]{1,0:T(8,128)(2,1)S(1)}, bf16[512,384]{1,0:T(8,128)(2,1)S(1)}, u32[]{:S(2)}, u32[]{:S(2)}) collective-permute-start(bf16[512,384]{1,0:T(8,128)(2,1)S(1)} %shard_map.88), channel_id=1, source_target_pairs={{0,8},{8,0},{16,24},{24,16},{32,40},{40,32},{48,56},{56,48},{64,72... | collective-permute-start | bytes 1179656 | tf_op jit(solution)/shard_map/ppermute | solution.py:443
  27.8 1.5 %collective-permute-start.13 = (bf16[512,384]{1,0:T(8,128)(2,1)S(1)}, bf16[512,384]{1,0:T(8,128)(2,1)S(1)}, u32[]{:S(2)}, u32[]{:S(2)}) collective-permute-start(bf16[512,384]{1,0:T(8,128)(2,1)S(1)} %shard_map.90), channel_id=1, source_target_pairs={{0,1},{1,2},{2,3},{3,4},{4,5},{5,6},{6,7},{7,0},{8,15},{9,8},{10,9... | collective-permute-start | bytes 1179656 | tf_op jit(solution)/shard_map/ppermute | solution.py:436
  29.4 1.3 %collective-permute-done.11.a3 = bf16[512,384]{1,0:T(8,128)(2,1)S(1)} collective-permute-done((bf16[512,384]{1,0:T(8,128)(2,1)S(1)}, bf16[512,384]{1,0:T(8,128)(2,1)S(1)}, u32[]{:S(2)}, u32[]{:S(2)}) %collective-permute-start.11) | collective-permute-done | bytes 393248 | tf_op jit(solution)/shard_map/ppermute | solution.py:436
  30.7 2.0 %collective-permute-start.12 = (bf16[512,384]{1,0:T(8,128)(2,1)S(1)}, bf16[512,384]{1,0:T(8,128)(2,1)S(1)}, u32[]{:S(2)}, u32[]{:S(2)}) collective-permute-start(bf16[512,384]{1,0:T(8,128)(2,1)S(1)} %collective-permute-done.11.a3), channel_id=1, source_target_pairs={{0,1},{1,2},{2,3},{3,4},{4,5},{5,6},{6,7},{7,0},{8,15},{9,8},{10,9... | collective-permute-start | bytes 1179656 | tf_op jit(solution)/shard_map/ppermute | solution.py:436
  32.7 4.1 %shard_map.89 = (f32[512,512]{1,0:T(8,128)S(1)}, bf16[2,512,384]{2,1,0:T(8,128)(2,1)S(1)}, bf16[4,256,512]{2,1,0:T(8,128)(2,1)S(1)}, f32[4,512]{1,0:T(4,128)S(1)}, f32[512,4]{1,0:T(8,128)S(1)}) custom-call(bf16[512,3072]{1,0:T(8,128)(2,1)} %w_hbm.1, bf16[512,384]{1,0:T(8,128)(2,1)} %c_hbm.1, bf16[512,512]{1,0:T(8,128)(2,1)} %q_ref.3, f32[4,512]{1,0:T(4,128)} %ld_hbm.3, ...), custom_call_target="tpu_custom_call" | custom-call | tf_op jit(solution)/shard_map/pallas_call | solution.py:32
  36.9 0.5 collective-permute-start.14
  37.4 1.8 %collective-permute-done.12.a4 = bf16[512,384]{1,0:T(8,128)(2,1)S(1)} collective-permute-done((bf16[512,384]{1,0:T(8,128)(2,1)S(1)}, bf16[512,384]{1,0:T(8,128)(2,1)S(1)}, u32[]{:S(2)}, u32[]{:S(2)}) %collective-permute-start.12) | collective-permute-done | bytes 393248 | tf_op jit(solution)/shard_map/ppermute | solution.py:436
  39.2 1.2 %shard_map.92 = (bf16[512,512]{1,0:T(8,128)(2,1)S(1)}, f32[256,128]{1,0:T(8,128)S(1)}, f32[256,128]{1,0:T(8,128)S(1)}) custom-call(f32[512,512]{1,0:T(8,128)S(1)} %get-tuple-element.47.refs_0_.acc_ref, bf16[512,384]{1,0:T(8,128)(2,1)S(1)} %collective-permute-done.12.a4, bf16[512,384]{1,0:T(8,128)(2,1)S(1)} %collective-permute-done.14.b3, ...), custom_call_target="tpu_custom_call" | custom-call | tf_op jit(solution)/shard_map/pallas_call | solution.py:32
  40.4 2.4 %collective-permute-start.15 = (f32[256,128]{1,0:T(8,128)S(1)}, f32[256,128]{1,0:T(8,128)S(1)}, u32[]{:S(2)}, u32[]{:S(2)}) collective-permute-start(f32[256,128]{1,0:T(8,128)S(1)} %get-tuple-element.51), channel_id=1, source_target_pairs={{0,8},{8,0},{16,24},{24,16},{32,40},{40,32},{48,56},{56,48},{64,72... | collective-permute-start | bytes 393224 | tf_op jit(solution)/shard_map/ppermute | solution.py:443
  42.7 1.0 %collective-permute-done.15.grad_other.refs_2_ = f32[256,128]{1,0:T(8,128)S(1)} collective-permute-done((f32[256,128]{1,0:T(8,128)S(1)}, f32[256,128]{1,0:T(8,128)S(1)}, u32[]{:S(2)}, u32[]{:S(2)}) %collective-permute-start.15) | collective-permute-done | bytes 131104 | tf_op jit(solution)/shard_map/ppermute | solution.py:443
  43.8 2.8 %collective-permute-start.18 = (bf16[256,128]{1,0:T(8,128)(2,1)S(1)}, bf16[256,128]{1,0:T(8,128)(2,1)S(1)}, u32[]{:S(2)}, u32[]{:S(2)}) collective-permute-start(bf16[256,128]{1,0:T(8,128)(2,1)S(1)} %get-tuple-element.53), channel_id=1, source_target_pairs={{0,32},{8,40},{16,48},{24,56},{32,0},{40,8},{48,16},{56,24},{64,96... | collective-permute-start | bytes 196616 | tf_op jit(solution)/shard_map/ppermute | solution.py:443
  46.6 0.9 %collective-permute-start.17 = (bf16[256,128]{1,0:T(8,128)(2,1)S(1)}, bf16[256,128]{1,0:T(8,128)(2,1)S(1)}, u32[]{:S(2)}, u32[]{:S(2)}) collective-permute-start(bf16[256,128]{1,0:T(8,128)(2,1)S(1)} %get-tuple-element.53), channel_id=1, source_target_pairs={{0,48},{8,56},{16,32},{24,40},{32,16},{40,24},{48,0},{56,8},{64,11... | collective-permute-start | bytes 196616 | tf_op jit(solution)/shard_map/ppermute | solution.py:443
  47.5 0.9 %collective-permute-start.22 = (f32[256,128]{1,0:T(8,128)S(1)}, f32[256,128]{1,0:T(8,128)S(1)}, u32[]{:S(2)}, u32[]{:S(2)}) collective-permute-start(f32[256,128]{1,0:T(8,128)S(1)} %get-tuple-element.50.grad_ref), channel_id=1, source_target_pairs={{0,8},{8,0},{16,24},{24,16},{32,40},{40,32},{48,56},{56,48},{64,72... | collective-permute-start | bytes 393224 | tf_op jit(solution)/shard_map/ppermute | solution.py:443
  48.4 2.1 %shard_map.94 = (f32[512,256]{1,0:T(8,128)S(1)}, f32[512,256]{1,0:T(8,128)S(1)}, f32[512,256]{1,0:T(8,128)S(1)}, f32[512,256]{1,0:T(8,128)S(1)}, f32[512,256]{1,0:T(8,128)S(1)}, /*index=5*/f32[8,128]{1,0:T(8,128)S(1)}) custom-call(f32[4,512]{1,0:T(4,128)S(1)} %get-tuple-element.56._.row_ref, bf16[512,512]{1,0:T(8,128)(2,1)S(1)} %copy-done.2, ...), custom_call_target="tpu_custom_call" | custom-call | tf_op jit(solution)/shard_map/pallas_call | solution.py:32
  50.5 0.5 collective-permute-done.17.r3
  51.0 3.0 %collective-permute-start.19 = (bf16[272,128]{1,0:T(8,128)(2,1)S(1)}, bf16[272,128]{1,0:T(8,128)(2,1)S(1)}, u32[]{:S(2)}, u32[]{:S(2)}) collective-permute-start(bf16[272,128]{1,0:T(8,128)(2,1)S(1)} %get-tuple-element.61), channel_id=1, source_target_pairs={{0,128},{8,136},{16,144},{24,152},{32,160},{40,168},{48,176},{56,1... | collective-permute-start | bytes 208904 | tf_op jit(solution)/shard_map/ppermute | solution.py:443
  54.8 2.1 %shard_map.96 = (f32[512,256]{1,0:T(8,128)S(1)}, f32[512,256]{1,0:T(8,128)S(1)}, f32[512,256]{1,0:T(8,128)S(1)}, f32[512,256]{1,0:T(8,128)S(1)}, f32[512,256]{1,0:T(8,128)S(1)}, /*index=5*/f32[8,128]{1,0:T(8,128)S(1)}) custom-call(f32[256,128]{1,0:T(8,128)S(1)} %collective-permute-done.22._.refs_2_, bf16[512,512]{1,0:T(8,128)(2,1)S(1)} %copy-done.2, ...), custom_call_target="tpu_custom_call" | custom-call | tf_op jit(solution)/shard_map/pallas_call | solution.py:32
  57.2 1.9 %collective-permute-done.21.r3 = bf16[272,128]{1,0:T(8,128)(2,1)S(1)} collective-permute-done((bf16[272,128]{1,0:T(8,128)(2,1)S(1)}, bf16[272,128]{1,0:T(8,128)(2,1)S(1)}, u32[]{:S(2)}, u32[]{:S(2)}) %collective-permute-start.21) | collective-permute-done | bytes 69664 | tf_op jit(solution)/shard_map/ppermute | solution.py:443
  59.2 3.3 %collective-permute-start.23 = (f32[512,128]{1,0:T(8,128)S(1)}, f32[512,128]{1,0:T(8,128)S(1)}, u32[]{:S(2)}, u32[]{:S(2)}) collective-permute-start(f32[512,128]{1,0:T(8,128)S(1)} %shard_map.97.refs_0_), channel_id=1, source_target_pairs={{0,8},{8,0},{16,24},{24,16},{32,40},{40,32},{48,56},{56,48},{64,72... | collective-permute-start | bytes 786440 | tf_op jit(solution)/shard_map/ppermute | solution.py:443
  62.5 1.3 %shard_map.98 = (f32[512,512]{1,0:T(8,128)}, f32[512,512]{1,0:T(8,128)}, f32[512,512]{1,0:T(8,128)}, f32[3,1,512,128]{3,2,1,0:T(8,128)S(1)}) custom-call(f32[512,128]{1,0:T(8,128)S(1)} %shard_map.97.refs_0_, f32[520,128]{1,0:T(8,128)S(1)} %collective-permute-done.key_other.refs_1_, f32[256,128]{1,0:T(8,128)S(1)} %collective-permute-done.15.grad_other.refs_2_, ...), custom_call_target="tpu_custom_call" | custom-call | tf_op jit(solution)/shard_map/pallas_call | solution.py:529
  63.8 1.7 %shard_map.99 = (f32[512,512]{1,0:T(8,128)}, f32[512,512]{1,0:T(8,128)}, f32[512,512]{1,0:T(8,128)}) custom-call(f32[512,128]{1,0:T(8,128)S(1)} %collective-permute-done.23.refs_0_, f32[520,128]{1,0:T(8,128)S(1)} %collective-permute-done.key_other.refs_1_, ...), custom_call_target="tpu_custom_call", output_to_operand_aliasing={{0}: (12, {}), {1}: (13, {}), {2}: (14, {})} | custom-call | tf_op jit(solution)/shard_map/pallas_call | solution.py:538
  (38 shorter events, 2.4 us)
Async XLA Ops:
  0.6 7.2 %collective-permute-start.1 = (bf16[512,384]{1,0:T(8,128)(2,1)}, bf16[512,384]{1,0:T(8,128)(2,1)S(1)}, u32[]{:S(2)}, u32[]{:S(2)}) collective-permute-start(bf16[512,384]{1,0:T(8,128)(2,1)} %c_hbm.1), channel_id=1, source_target_pairs={{0,8},{8,0},{16,24},{24,16},{32,40},{40,32},{48,56},{56,48},{64,72... | collective-permute-start | bytes 1179656 | tf_op jit(solution)/shard_map/ppermute | solution.py:443
  4.0 8.9 %collective-permute-start.6 = (bf16[512,384]{1,0:T(8,128)(2,1)}, bf16[512,384]{1,0:T(8,128)(2,1)S(1)}, u32[]{:S(2)}, u32[]{:S(2)}) collective-permute-start(bf16[512,384]{1,0:T(8,128)(2,1)} %c_hbm.1), channel_id=1, source_target_pairs={{0,1},{1,2},{2,3},{3,4},{4,5},{5,6},{6,7},{7,0},{8,15},{9,8},{10,9... | collective-permute-start | bytes 1179656 | tf_op jit(solution)/shard_map/ppermute | solution.py:436
  7.8 9.1 %collective-permute-start.2 = (bf16[512,384]{1,0:T(8,128)(2,1)S(1)}, bf16[512,384]{1,0:T(8,128)(2,1)S(1)}, u32[]{:S(2)}, u32[]{:S(2)}) collective-permute-start(bf16[512,384]{1,0:T(8,128)(2,1)S(1)} %collective-permute-done.1), channel_id=1, source_target_pairs={{0,1},{1,2},{2,3},{3,4},{4,5},{5,6},{6,7},{7,0},{8,15},{9,8},{10,9... | collective-permute-start | bytes 1179656 | tf_op jit(solution)/shard_map/ppermute | solution.py:436
  11.2 4.6 %collective-permute-start = (f32[520,128]{1,0:T(8,128)S(1)}, f32[520,128]{1,0:T(8,128)S(1)}, u32[]{:S(2)}, u32[]{:S(2)}) collective-permute-start(f32[520,128]{1,0:T(8,128)S(1)} %get-tuple-element.41.key_ref), channel_id=1, source_target_pairs={{0,8},{8,0},{16,24},{24,16},{32,40},{40,32},{48,56},{56,48},{64,72... | collective-permute-start | bytes 798728 | tf_op jit(solution)/shard_map/ppermute | solution.py:443
  12.8 11.0 %collective-permute-start.9 = (bf16[512,384]{1,0:T(8,128)(2,1)S(1)}, bf16[512,384]{1,0:T(8,128)(2,1)S(1)}, u32[]{:S(2)}, u32[]{:S(2)}) collective-permute-start(bf16[512,384]{1,0:T(8,128)(2,1)S(1)} %collective-permute-done.6.a1), channel_id=1, source_target_pairs={{0,1},{1,2},{2,3},{3,4},{4,5},{5,6},{6,7},{7,0},{8,15},{9,8},{10,9... | collective-permute-start | bytes 1179656 | tf_op jit(solution)/shard_map/ppermute | solution.py:436
  17.0 8.3 %collective-permute-start.7 = (bf16[512,384]{1,0:T(8,128)(2,1)S(1)}, bf16[512,384]{1,0:T(8,128)(2,1)S(1)}, u32[]{:S(2)}, u32[]{:S(2)}) collective-permute-start(bf16[512,384]{1,0:T(8,128)(2,1)S(1)} %get-tuple-element.45.x_ref), channel_id=1, source_target_pairs={{0,1},{1,2},{2,3},{3,4},{4,5},{5,6},{6,7},{7,0},{8,15},{9,8},{10,9... | collective-permute-start | bytes 1179656 | tf_op jit(solution)/shard_map/ppermute | solution.py:436
  20.2 7.4 %collective-permute-start.5 = (bf16[272,128]{1,0:T(8,128)(2,1)S(1)}, bf16[272,128]{1,0:T(8,128)(2,1)S(1)}, u32[]{:S(2)}, u32[]{:S(2)}) collective-permute-start(bf16[272,128]{1,0:T(8,128)(2,1)S(1)} %get-tuple-element.42.sent_ref), channel_id=1, source_target_pairs={{0,32},{8,40},{16,48},{24,56},{32,0},{40,8},{48,16},{56,24},{64,96... | collective-permute-start | bytes 208904 | tf_op jit(solution)/shard_map/ppermute | solution.py:443
  23.0 4.8 %collective-permute-start.4 = (bf16[272,128]{1,0:T(8,128)(2,1)S(1)}, bf16[272,128]{1,0:T(8,128)(2,1)S(1)}, u32[]{:S(2)}, u32[]{:S(2)}) collective-permute-start(bf16[272,128]{1,0:T(8,128)(2,1)S(1)} %get-tuple-element.42.sent_ref), channel_id=1, source_target_pairs={{0,48},{8,56},{16,32},{24,40},{32,16},{40,24},{48,0},{56,8},{64,11... | collective-permute-start | bytes 208904 | tf_op jit(solution)/shard_map/ppermute | solution.py:443
  23.8 3.9 %collective-permute-start.3 = (bf16[272,128]{1,0:T(8,128)(2,1)S(1)}, bf16[272,128]{1,0:T(8,128)(2,1)S(1)}, u32[]{:S(2)}, u32[]{:S(2)}) collective-permute-start(bf16[272,128]{1,0:T(8,128)(2,1)S(1)} %get-tuple-element.42.sent_ref), channel_id=1, source_target_pairs={{0,16},{8,24},{16,0},{24,8},{32,48},{40,56},{48,32},{56,40},{64,80... | collective-permute-start | bytes 208904 | tf_op jit(solution)/shard_map/ppermute | solution.py:443
  23.8 6.9 %collective-permute-start.11 = (bf16[512,384]{1,0:T(8,128)(2,1)S(1)}, bf16[512,384]{1,0:T(8,128)(2,1)S(1)}, u32[]{:S(2)}, u32[]{:S(2)}) collective-permute-start(bf16[512,384]{1,0:T(8,128)(2,1)S(1)} %collective-permute-done.9.a2), channel_id=1, source_target_pairs={{0,1},{1,2},{2,3},{3,4},{4,5},{5,6},{6,7},{7,0},{8,15},{9,8},{10,9... | collective-permute-start | bytes 1179656 | tf_op jit(solution)/shard_map/ppermute | solution.py:436
  25.4 7.3 %collective-permute-start.8 = (bf16[512,384]{1,0:T(8,128)(2,1)S(1)}, bf16[512,384]{1,0:T(8,128)(2,1)S(1)}, u32[]{:S(2)}, u32[]{:S(2)}) collective-permute-start(bf16[512,384]{1,0:T(8,128)(2,1)S(1)} %shard_map.88), channel_id=1, source_target_pairs={{0,8},{8,0},{16,24},{24,16},{32,40},{40,32},{48,56},{56,48},{64,72... | collective-permute-start | bytes 1179656 | tf_op jit(solution)/shard_map/ppermute | solution.py:443
  27.6 5.1 %collective-permute-start.10 = (bf16[512,384]{1,0:T(8,128)(2,1)S(1)}, bf16[512,384]{1,0:T(8,128)(2,1)S(1)}, u32[]{:S(2)}, u32[]{:S(2)}) collective-permute-start(bf16[512,384]{1,0:T(8,128)(2,1)S(1)} %collective-permute-done.7.refs_0_.x_ref), channel_id=1, source_target_pairs={{0,8},{8,0},{16,24},{24,16},{32,40},{40,32},{48,56},{56,48},{64,72... | collective-permute-start | bytes 1179656 | tf_op jit(solution)/shard_map/ppermute | solution.py:443
  27.8 9.0 %collective-permute-start.13 = (bf16[512,384]{1,0:T(8,128)(2,1)S(1)}, bf16[512,384]{1,0:T(8,128)(2,1)S(1)}, u32[]{:S(2)}, u32[]{:S(2)}) collective-permute-start(bf16[512,384]{1,0:T(8,128)(2,1)S(1)} %shard_map.90), channel_id=1, source_target_pairs={{0,1},{1,2},{2,3},{3,4},{4,5},{5,6},{6,7},{7,0},{8,15},{9,8},{10,9... | collective-permute-start | bytes 1179656 | tf_op jit(solution)/shard_map/ppermute | solution.py:436
  30.7 8.4 %collective-permute-start.12 = (bf16[512,384]{1,0:T(8,128)(2,1)S(1)}, bf16[512,384]{1,0:T(8,128)(2,1)S(1)}, u32[]{:S(2)}, u32[]{:S(2)}) collective-permute-start(bf16[512,384]{1,0:T(8,128)(2,1)S(1)} %collective-permute-done.11.a3), channel_id=1, source_target_pairs={{0,1},{1,2},{2,3},{3,4},{4,5},{5,6},{6,7},{7,0},{8,15},{9,8},{10,9... | collective-permute-start | bytes 1179656 | tf_op jit(solution)/shard_map/ppermute | solution.py:436
  36.8 11.6 %copy-start = (bf16[512,512]{1,0:T(8,128)(2,1)S(1)}, bf16[512,512]{1,0:T(8,128)(2,1)}, u32[]{:S(2)}) copy-start(bf16[512,512]{1,0:T(8,128)(2,1)} %refs_4_.3) | copy-start | bytes 1572868
  36.8 11.6 %copy-start.1 = (bf16[512,512]{1,0:T(8,128)(2,1)S(1)}, bf16[512,512]{1,0:T(8,128)(2,1)}, u32[]{:S(2)}) copy-start(bf16[512,512]{1,0:T(8,128)(2,1)} %refs_5_.3) | copy-start | bytes 1572868
  36.8 11.6 %copy-start.2 = (bf16[512,512]{1,0:T(8,128)(2,1)S(1)}, bf16[512,512]{1,0:T(8,128)(2,1)}, u32[]{:S(2)}) copy-start(bf16[512,512]{1,0:T(8,128)(2,1)} %q_ref.3) | copy-start | bytes 1572868
  36.9 2.3 %collective-permute-start.14 = (bf16[512,384]{1,0:T(8,128)(2,1)S(1)}, bf16[512,384]{1,0:T(8,128)(2,1)S(1)}, u32[]{:S(2)}, u32[]{:S(2)}) collective-permute-start(bf16[512,384]{1,0:T(8,128)(2,1)S(1)} %shard_map.91), channel_id=1, source_target_pairs={{0,8},{8,0},{16,24},{24,16},{32,40},{40,32},{48,56},{56,48},{64,72... | collective-permute-start | bytes 1179656 | tf_op jit(solution)/shard_map/ppermute | solution.py:443
  40.4 3.4 %collective-permute-start.15 = (f32[256,128]{1,0:T(8,128)S(1)}, f32[256,128]{1,0:T(8,128)S(1)}, u32[]{:S(2)}, u32[]{:S(2)}) collective-permute-start(f32[256,128]{1,0:T(8,128)S(1)} %get-tuple-element.51), channel_id=1, source_target_pairs={{0,8},{8,0},{16,24},{24,16},{32,40},{40,32},{48,56},{56,48},{64,72... | collective-permute-start | bytes 393224 | tf_op jit(solution)/shard_map/ppermute | solution.py:443
  43.8 6.7 %collective-permute-start.18 = (bf16[256,128]{1,0:T(8,128)(2,1)S(1)}, bf16[256,128]{1,0:T(8,128)(2,1)S(1)}, u32[]{:S(2)}, u32[]{:S(2)}) collective-permute-start(bf16[256,128]{1,0:T(8,128)(2,1)S(1)} %get-tuple-element.53), channel_id=1, source_target_pairs={{0,32},{8,40},{16,48},{24,56},{32,0},{40,8},{48,16},{56,24},{64,96... | collective-permute-start | bytes 196616 | tf_op jit(solution)/shard_map/ppermute | solution.py:443
  46.6 4.3 %collective-permute-start.17 = (bf16[256,128]{1,0:T(8,128)(2,1)S(1)}, bf16[256,128]{1,0:T(8,128)(2,1)S(1)}, u32[]{:S(2)}, u32[]{:S(2)}) collective-permute-start(bf16[256,128]{1,0:T(8,128)(2,1)S(1)} %get-tuple-element.53), channel_id=1, source_target_pairs={{0,48},{8,56},{16,32},{24,40},{32,16},{40,24},{48,0},{56,8},{64,11... | collective-permute-start | bytes 196616 | tf_op jit(solution)/shard_map/ppermute | solution.py:443
  47.5 3.5 %collective-permute-start.16 = (bf16[256,128]{1,0:T(8,128)(2,1)S(1)}, bf16[256,128]{1,0:T(8,128)(2,1)S(1)}, u32[]{:S(2)}, u32[]{:S(2)}) collective-permute-start(bf16[256,128]{1,0:T(8,128)(2,1)S(1)} %get-tuple-element.53), channel_id=1, source_target_pairs={{0,16},{8,24},{16,0},{24,8},{32,48},{40,56},{48,32},{56,40},{64,80... | collective-permute-start | bytes 196616 | tf_op jit(solution)/shard_map/ppermute | solution.py:443
  47.5 7.3 %collective-permute-start.22 = (f32[256,128]{1,0:T(8,128)S(1)}, f32[256,128]{1,0:T(8,128)S(1)}, u32[]{:S(2)}, u32[]{:S(2)}) collective-permute-start(f32[256,128]{1,0:T(8,128)S(1)} %get-tuple-element.50.grad_ref), channel_id=1, source_target_pairs={{0,8},{8,0},{16,24},{24,16},{32,40},{40,32},{48,56},{56,48},{64,72... | collective-permute-start | bytes 393224 | tf_op jit(solution)/shard_map/ppermute | solution.py:443
  51.0 5.8 %collective-permute-start.19 = (bf16[272,128]{1,0:T(8,128)(2,1)S(1)}, bf16[272,128]{1,0:T(8,128)(2,1)S(1)}, u32[]{:S(2)}, u32[]{:S(2)}) collective-permute-start(bf16[272,128]{1,0:T(8,128)(2,1)S(1)} %get-tuple-element.61), channel_id=1, source_target_pairs={{0,128},{8,136},{16,144},{24,152},{32,160},{40,168},{48,176},{56,1... | collective-permute-start | bytes 208904 | tf_op jit(solution)/shard_map/ppermute | solution.py:443
  54.0 3.2 %collective-permute-start.20 = (bf16[272,128]{1,0:T(8,128)(2,1)S(1)}, bf16[272,128]{1,0:T(8,128)(2,1)S(1)}, u32[]{:S(2)}, u32[]{:S(2)}) collective-permute-start(bf16[272,128]{1,0:T(8,128)(2,1)S(1)} %get-tuple-element.62), channel_id=1, source_target_pairs={{0,64},{8,72},{16,80},{24,88},{32,96},{40,104},{48,112},{56,120},{... | collective-permute-start | bytes 208904 | tf_op jit(solution)/shard_map/ppermute | solution.py:443
  54.4 4.7 %collective-permute-start.21 = (bf16[272,128]{1,0:T(8,128)(2,1)S(1)}, bf16[272,128]{1,0:T(8,128)(2,1)S(1)}, u32[]{:S(2)}, u32[]{:S(2)}) collective-permute-start(bf16[272,128]{1,0:T(8,128)(2,1)S(1)} %get-tuple-element.63), channel_id=1, source_target_pairs={{0,192},{8,200},{16,208},{24,216},{32,224},{40,232},{48,240},{56,2... | collective-permute-start | bytes 208904 | tf_op jit(solution)/shard_map/ppermute | solution.py:443
  59.2 4.6 %collective-permute-start.23 = (f32[512,128]{1,0:T(8,128)S(1)}, f32[512,128]{1,0:T(8,128)S(1)}, u32[]{:S(2)}, u32[]{:S(2)}) collective-permute-start(f32[512,128]{1,0:T(8,128)S(1)} %shard_map.97.refs_0_), channel_id=1, source_target_pairs={{0,8},{8,0},{16,24},{24,16},{32,40},{40,32},{48,56},{56,48},{64,72... | collective-permute-start | bytes 786440 | tf_op jit(solution)/shard_map/ppermute | solution.py:443

commit v6 on v4

--- a/solution.py
+++ b/solution.py
@@ -177,8 +177,8 @@
 
 
 def late_kernel(heads, acc_ref, a4, b3, w_ref, qw_ref, ga_ref, own_ref, theirs_ref):
-    half = acc_ref.shape[0] // 2
-    for part in range(2):
+    half = acc_ref.shape[0]
+    for part in range(1):
         at = pl.ds(part * half, half)
         ga_ref[at, :] = (
             acc_ref[at, :] + dot(a4[at, :], w_ref[0], NT) + dot(b3[at, :], w_ref[1], NT)

time: 65.9 us -> 65.9 us (level)
  no operation moved by 1% of the time
where the time goes in v6:
time: 65.9 us; the launch traced here: 65.7 us
  starting transfers between devices  39.4 us (60%)
  Pallas kernels  14.3 us (22%)
  waiting for transfers between devices  11.1 us (17%)
  between operations  0.94 us (1%)
    ppermute x17, starting transfers between devices, along_seq(): return lax.ppermute(array, 'seq', pairs)  23.9 us
    ppermute x7, starting transfers between devices, along_z(): return lax.ppermute(array, ('seq', 'head'), pairs)  15.5 us
    pallas_call x14, Pallas kernels, call(): pl.pallas_call(kernel, out_shape=outs, in_specs=specs or [VMEM] * len(arg...  12.4 us
    ppermute x7, waiting for transfers between devices, along_z(): return lax.ppermute(array, ('seq', 'head'), pairs)  6.85 us
    ppermute x17, waiting for transfers between devices, along_seq(): return lax.ppermute(array, 'seq', pairs)  4.25 us
    pallas_call x1, Pallas kernels, local(): pl.pallas_call(functools.partial(rest_kernel, pair), out_shape=(f32(rows,...  1.85 us
  transfers between devices with their start and end apart: 24, of which 10 were waited for; matrix products, arithmetic and copies ran while one was open for 0% of the time, Pallas kernels for 17%

profile of v6, /device:TPU:1, one launch (start us, length us, event | category | flops | bytes accessed | tf_op | source)
XLA Modules:
  0.0 65.7 jit_solution(3695367904640398925)
XLA Ops:
  0.6 3.3 %collective-permute-start.1 = (bf16[512,384]{1,0:T(8,128)(2,1)}, bf16[512,384]{1,0:T(8,128)(2,1)S(1)}, u32[]{:S(2)}, u32[]{:S(2)}) collective-permute-start(bf16[512,384]{1,0:T(8,128)(2,1)} %c_hbm.1), channel_id=1, source_target_pairs={{0,8},{8,0},{16,24},{24,16},{32,40},{40,32},{48,56},{56,48},{64,72... | collective-permute-start | bytes 1179656 | tf_op jit(solution)/shard_map/ppermute | solution.py:429
  4.0 3.8 %collective-permute-start.6 = (bf16[512,384]{1,0:T(8,128)(2,1)}, bf16[512,384]{1,0:T(8,128)(2,1)S(1)}, u32[]{:S(2)}, u32[]{:S(2)}) collective-permute-start(bf16[512,384]{1,0:T(8,128)(2,1)} %c_hbm.1), channel_id=1, source_target_pairs={{0,1},{1,2},{2,3},{3,4},{4,5},{5,6},{6,7},{7,0},{8,15},{9,8},{10,9... | collective-permute-start | bytes 1179656 | tf_op jit(solution)/shard_map/ppermute | solution.py:422
  7.8 1.6 %collective-permute-start.2 = (bf16[512,384]{1,0:T(8,128)(2,1)S(1)}, bf16[512,384]{1,0:T(8,128)(2,1)S(1)}, u32[]{:S(2)}, u32[]{:S(2)}) collective-permute-start(bf16[512,384]{1,0:T(8,128)(2,1)S(1)} %collective-permute-done.1), channel_id=1, source_target_pairs={{0,1},{1,2},{2,3},{3,4},{4,5},{5,6},{6,7},{7,0},{8,15},{9,8},{10,9... | collective-permute-start | bytes 1179656 | tf_op jit(solution)/shard_map/ppermute | solution.py:422
  9.4 1.8 %shard_map.85 = (f32[520,128]{1,0:T(8,128)S(1)}, f32[8,128]{1,0:T(8,128)}) custom-call(bf16[512,512]{1,0:T(8,128)(2,1)} %refs_4_.3, bf16[512,512]{1,0:T(8,128)(2,1)} %refs_5_.3, f32[4,512]{1,0:T(4,128)} %ld_hbm.3, f32[8,128]{1,0:T(8,128)S(1)} %broadcast_in_dim.3.tie_ref), custom_call_target="tpu_custom_call" | custom-call | tf_op jit(solution)/shard_map/pallas_call | solution.py:32
  11.3 1.5 %collective-permute-done.6.a1 = bf16[512,384]{1,0:T(8,128)(2,1)S(1)} collective-permute-done((bf16[512,384]{1,0:T(8,128)(2,1)}, bf16[512,384]{1,0:T(8,128)(2,1)S(1)}, u32[]{:S(2)}, u32[]{:S(2)}) %collective-permute-start.6) | collective-permute-done | bytes 393248 | tf_op jit(solution)/shard_map/ppermute | solution.py:422
  12.8 3.0 %collective-permute-start.9 = (bf16[512,384]{1,0:T(8,128)(2,1)S(1)}, bf16[512,384]{1,0:T(8,128)(2,1)S(1)}, u32[]{:S(2)}, u32[]{:S(2)}) collective-permute-start(bf16[512,384]{1,0:T(8,128)(2,1)S(1)} %collective-permute-done.6.a1), channel_id=1, source_target_pairs={{0,1},{1,2},{2,3},{3,4},{4,5},{5,6},{6,7},{7,0},{8,15},{9,8},{10,9... | collective-permute-start | bytes 1179656 | tf_op jit(solution)/shard_map/ppermute | solution.py:422
  15.8 1.1 %collective-permute-done.2.tie_ref = bf16[512,384]{1,0:T(8,128)(2,1)S(1)} collective-permute-done((bf16[512,384]{1,0:T(8,128)(2,1)S(1)}, bf16[512,384]{1,0:T(8,128)(2,1)S(1)}, u32[]{:S(2)}, u32[]{:S(2)}) %collective-permute-start.2) | collective-permute-done | bytes 393248 | tf_op jit(solution)/shard_map/ppermute | solution.py:422
  17.0 3.2 %collective-permute-start.7 = (bf16[512,384]{1,0:T(8,128)(2,1)S(1)}, bf16[512,384]{1,0:T(8,128)(2,1)S(1)}, u32[]{:S(2)}, u32[]{:S(2)}) collective-permute-start(bf16[512,384]{1,0:T(8,128)(2,1)S(1)} %get-tuple-element.41.x_ref), channel_id=1, source_target_pairs={{0,1},{1,2},{2,3},{3,4},{4,5},{5,6},{6,7},{7,0},{8,15},{9,8},{10,9... | collective-permute-start | bytes 1179656 | tf_op jit(solution)/shard_map/ppermute | solution.py:422
  20.2 2.7 %collective-permute-start.5 = (bf16[272,128]{1,0:T(8,128)(2,1)S(1)}, bf16[272,128]{1,0:T(8,128)(2,1)S(1)}, u32[]{:S(2)}, u32[]{:S(2)}) collective-permute-start(bf16[272,128]{1,0:T(8,128)(2,1)S(1)} %get-tuple-element.38.sent_ref), channel_id=1, source_target_pairs={{0,32},{8,40},{16,48},{24,56},{32,0},{40,8},{48,16},{56,24},{64,96... | collective-permute-start | bytes 208904 | tf_op jit(solution)/shard_map/ppermute | solution.py:429
  23.0 0.9 %collective-permute-start.4 = (bf16[272,128]{1,0:T(8,128)(2,1)S(1)}, bf16[272,128]{1,0:T(8,128)(2,1)S(1)}, u32[]{:S(2)}, u32[]{:S(2)}) collective-permute-start(bf16[272,128]{1,0:T(8,128)(2,1)S(1)} %get-tuple-element.38.sent_ref), channel_id=1, source_target_pairs={{0,48},{8,56},{16,32},{24,40},{32,16},{40,24},{48,0},{56,8},{64,11... | collective-permute-start | bytes 208904 | tf_op jit(solution)/shard_map/ppermute | solution.py:429
  24.3 1.1 %collective-permute-done.7.refs_0_.x_ref = bf16[512,384]{1,0:T(8,128)(2,1)S(1)} collective-permute-done((bf16[512,384]{1,0:T(8,128)(2,1)S(1)}, bf16[512,384]{1,0:T(8,128)(2,1)S(1)}, u32[]{:S(2)}, u32[]{:S(2)}) %collective-permute-start.7) | collective-permute-done | bytes 393248 | tf_op jit(solution)/shard_map/ppermute | solution.py:422
  25.4 2.2 %collective-permute-start.8 = (bf16[512,384]{1,0:T(8,128)(2,1)S(1)}, bf16[512,384]{1,0:T(8,128)(2,1)S(1)}, u32[]{:S(2)}, u32[]{:S(2)}) collective-permute-start(bf16[512,384]{1,0:T(8,128)(2,1)S(1)} %shard_map.88), channel_id=1, source_target_pairs={{0,8},{8,0},{16,24},{24,16},{32,40},{40,32},{48,56},{56,48},{64,72... | collective-permute-start | bytes 1179656 | tf_op jit(solution)/shard_map/ppermute | solution.py:429
  27.8 1.5 %collective-permute-start.13 = (bf16[512,384]{1,0:T(8,128)(2,1)S(1)}, bf16[512,384]{1,0:T(8,128)(2,1)S(1)}, u32[]{:S(2)}, u32[]{:S(2)}) collective-permute-start(bf16[512,384]{1,0:T(8,128)(2,1)S(1)} %shard_map.90), channel_id=1, source_target_pairs={{0,1},{1,2},{2,3},{3,4},{4,5},{5,6},{6,7},{7,0},{8,15},{9,8},{10,9... | collective-permute-start | bytes 1179656 | tf_op jit(solution)/shard_map/ppermute | solution.py:422
  29.4 1.3 %collective-permute-done.11.a3 = bf16[512,384]{1,0:T(8,128)(2,1)S(1)} collective-permute-done((bf16[512,384]{1,0:T(8,128)(2,1)S(1)}, bf16[512,384]{1,0:T(8,128)(2,1)S(1)}, u32[]{:S(2)}, u32[]{:S(2)}) %collective-permute-start.11) | collective-permute-done | bytes 393248 | tf_op jit(solution)/shard_map/ppermute | solution.py:422
  30.7 2.0 %collective-permute-start.12 = (bf16[512,384]{1,0:T(8,128)(2,1)S(1)}, bf16[512,384]{1,0:T(8,128)(2,1)S(1)}, u32[]{:S(2)}, u32[]{:S(2)}) collective-permute-start(bf16[512,384]{1,0:T(8,128)(2,1)S(1)} %collective-permute-done.11.a3), channel_id=1, source_target_pairs={{0,1},{1,2},{2,3},{3,4},{4,5},{5,6},{6,7},{7,0},{8,15},{9,8},{10,9... | collective-permute-start | bytes 1179656 | tf_op jit(solution)/shard_map/ppermute | solution.py:422
  32.7 4.1 %shard_map.89 = (f32[512,512]{1,0:T(8,128)S(1)}, bf16[2,512,384]{2,1,0:T(8,128)(2,1)S(1)}, bf16[4,256,512]{2,1,0:T(8,128)(2,1)S(1)}, f32[4,512]{1,0:T(4,128)S(1)}, f32[512,4]{1,0:T(8,128)S(1)}) custom-call(bf16[512,3072]{1,0:T(8,128)(2,1)} %w_hbm.1, bf16[512,384]{1,0:T(8,128)(2,1)} %c_hbm.1, bf16[512,512]{1,0:T(8,128)(2,1)} %q_ref.3, f32[4,512]{1,0:T(4,128)} %ld_hbm.3, ...), custom_call_target="tpu_custom_call" | custom-call | tf_op jit(solution)/shard_map/pallas_call | solution.py:32
  36.9 0.5 collective-permute-start.14
  37.4 1.8 %collective-permute-done.12.a4 = bf16[512,384]{1,0:T(8,128)(2,1)S(1)} collective-permute-done((bf16[512,384]{1,0:T(8,128)(2,1)S(1)}, bf16[512,384]{1,0:T(8,128)(2,1)S(1)}, u32[]{:S(2)}, u32[]{:S(2)}) %collective-permute-start.12) | collective-permute-done | bytes 393248 | tf_op jit(solution)/shard_map/ppermute | solution.py:422
  39.2 1.2 %shard_map.92 = (bf16[512,512]{1,0:T(8,128)(2,1)S(1)}, f32[256,128]{1,0:T(8,128)S(1)}, f32[256,128]{1,0:T(8,128)S(1)}) custom-call(f32[512,512]{1,0:T(8,128)S(1)} %get-tuple-element.43.refs_0_.acc_ref, bf16[512,384]{1,0:T(8,128)(2,1)S(1)} %collective-permute-done.12.a4, bf16[512,384]{1,0:T(8,128)(2,1)S(1)} %collective-permute-done.14.b3, ...), custom_call_target="tpu_custom_call" | custom-call | tf_op jit(solution)/shard_map/pallas_call | solution.py:32
  40.4 2.4 %collective-permute-start.15 = (f32[256,128]{1,0:T(8,128)S(1)}, f32[256,128]{1,0:T(8,128)S(1)}, u32[]{:S(2)}, u32[]{:S(2)}) collective-permute-start(f32[256,128]{1,0:T(8,128)S(1)} %get-tuple-element.47), channel_id=1, source_target_pairs={{0,8},{8,0},{16,24},{24,16},{32,40},{40,32},{48,56},{56,48},{64,72... | collective-permute-start | bytes 393224 | tf_op jit(solution)/shard_map/ppermute | solution.py:429
  42.7 1.0 %collective-permute-done.15.grad_other.refs_2_ = f32[256,128]{1,0:T(8,128)S(1)} collective-permute-done((f32[256,128]{1,0:T(8,128)S(1)}, f32[256,128]{1,0:T(8,128)S(1)}, u32[]{:S(2)}, u32[]{:S(2)}) %collective-permute-start.15) | collective-permute-done | bytes 131104 | tf_op jit(solution)/shard_map/ppermute | solution.py:429
  43.8 2.8 %collective-permute-start.18 = (bf16[256,128]{1,0:T(8,128)(2,1)S(1)}, bf16[256,128]{1,0:T(8,128)(2,1)S(1)}, u32[]{:S(2)}, u32[]{:S(2)}) collective-permute-start(bf16[256,128]{1,0:T(8,128)(2,1)S(1)} %get-tuple-element.49), channel_id=1, source_target_pairs={{0,32},{8,40},{16,48},{24,56},{32,0},{40,8},{48,16},{56,24},{64,96... | collective-permute-start | bytes 196616 | tf_op jit(solution)/shard_map/ppermute | solution.py:429
  46.6 0.9 %collective-permute-start.17 = (bf16[256,128]{1,0:T(8,128)(2,1)S(1)}, bf16[256,128]{1,0:T(8,128)(2,1)S(1)}, u32[]{:S(2)}, u32[]{:S(2)}) collective-permute-start(bf16[256,128]{1,0:T(8,128)(2,1)S(1)} %get-tuple-element.49), channel_id=1, source_target_pairs={{0,48},{8,56},{16,32},{24,40},{32,16},{40,24},{48,0},{56,8},{64,11... | collective-permute-start | bytes 196616 | tf_op jit(solution)/shard_map/ppermute | solution.py:429
  47.5 0.9 %collective-permute-start.22 = (f32[256,128]{1,0:T(8,128)S(1)}, f32[256,128]{1,0:T(8,128)S(1)}, u32[]{:S(2)}, u32[]{:S(2)}) collective-permute-start(f32[256,128]{1,0:T(8,128)S(1)} %get-tuple-element.46.grad_ref), channel_id=1, source_target_pairs={{0,8},{8,0},{16,24},{24,16},{32,40},{40,32},{48,56},{56,48},{64,72... | collective-permute-start | bytes 393224 | tf_op jit(solution)/shard_map/ppermute | solution.py:429
  48.4 2.0 %shard_map.94 = (f32[512,256]{1,0:T(8,128)S(1)}, f32[512,256]{1,0:T(8,128)S(1)}, f32[512,256]{1,0:T(8,128)S(1)}, f32[512,256]{1,0:T(8,128)S(1)}, f32[512,256]{1,0:T(8,128)S(1)}, /*index=5*/f32[8,128]{1,0:T(8,128)S(1)}) custom-call(f32[4,512]{1,0:T(4,128)S(1)} %get-tuple-element.52._.row_ref, bf16[512,512]{1,0:T(8,128)(2,1)S(1)} %copy-done.2, ...), custom_call_target="tpu_custom_call" | custom-call | tf_op jit(solution)/shard_map/pallas_call | solution.py:32
  51.0 3.0 %collective-permute-start.19 = (bf16[272,128]{1,0:T(8,128)(2,1)S(1)}, bf16[272,128]{1,0:T(8,128)(2,1)S(1)}, u32[]{:S(2)}, u32[]{:S(2)}) collective-permute-start(bf16[272,128]{1,0:T(8,128)(2,1)S(1)} %get-tuple-element.57), channel_id=1, source_target_pairs={{0,128},{8,136},{16,144},{24,152},{32,160},{40,168},{48,176},{56,1... | collective-permute-start | bytes 208904 | tf_op jit(solution)/shard_map/ppermute | solution.py:429
  54.8 2.1 %shard_map.96 = (f32[512,256]{1,0:T(8,128)S(1)}, f32[512,256]{1,0:T(8,128)S(1)}, f32[512,256]{1,0:T(8,128)S(1)}, f32[512,256]{1,0:T(8,128)S(1)}, f32[512,256]{1,0:T(8,128)S(1)}, /*index=5*/f32[8,128]{1,0:T(8,128)S(1)}) custom-call(f32[256,128]{1,0:T(8,128)S(1)} %collective-permute-done.22._.refs_2_, bf16[512,512]{1,0:T(8,128)(2,1)S(1)} %copy-done.2, ...), custom_call_target="tpu_custom_call" | custom-call | tf_op jit(solution)/shard_map/pallas_call | solution.py:32
  57.2 1.9 %collective-permute-done.21.r3 = bf16[272,128]{1,0:T(8,128)(2,1)S(1)} collective-permute-done((bf16[272,128]{1,0:T(8,128)(2,1)S(1)}, bf16[272,128]{1,0:T(8,128)(2,1)S(1)}, u32[]{:S(2)}, u32[]{:S(2)}) %collective-permute-start.21) | collective-permute-done | bytes 69664 | tf_op jit(solution)/shard_map/ppermute | solution.py:429
  59.2 3.3 %collective-permute-start.23 = (f32[512,128]{1,0:T(8,128)S(1)}, f32[512,128]{1,0:T(8,128)S(1)}, u32[]{:S(2)}, u32[]{:S(2)}) collective-permute-start(f32[512,128]{1,0:T(8,128)S(1)} %shard_map.97.refs_0_), channel_id=1, source_target_pairs={{0,8},{8,0},{16,24},{24,16},{32,40},{40,32},{48,56},{56,48},{64,72... | collective-permute-start | bytes 786440 | tf_op jit(solution)/shard_map/ppermute | solution.py:429
  62.5 0.6 shard_map.98.refs_11_
  63.1 0.5 collective-permute-done.23.refs_0_
  63.7 1.9 %shard_map.99 = (f32[512,512]{1,0:T(8,128)}, f32[512,512]{1,0:T(8,128)}, f32[512,512]{1,0:T(8,128)}) custom-call(f32[512,128]{1,0:T(8,128)S(1)} %collective-permute-done.23.refs_0_, f32[520,128]{1,0:T(8,128)S(1)} %collective-permute-done.key_other.refs_1_, f32[256,128]{1,0:T(8,128)S(1)} %collective-permute-done.22._.refs_2_, ...), custom_call_target="tpu_custom_call" | custom-call | tf_op jit(solution)/shard_map/pallas_call | solution.py:518
  (38 shorter events, 2.9 us)
Async XLA Ops:
  0.6 7.2 %collective-permute-start.1 = (bf16[512,384]{1,0:T(8,128)(2,1)}, bf16[512,384]{1,0:T(8,128)(2,1)S(1)}, u32[]{:S(2)}, u32[]{:S(2)}) collective-permute-start(bf16[512,384]{1,0:T(8,128)(2,1)} %c_hbm.1), channel_id=1, source_target_pairs={{0,8},{8,0},{16,24},{24,16},{32,40},{40,32},{48,56},{56,48},{64,72... | collective-permute-start | bytes 1179656 | tf_op jit(solution)/shard_map/ppermute | solution.py:429
  4.0 8.9 %collective-permute-start.6 = (bf16[512,384]{1,0:T(8,128)(2,1)}, bf16[512,384]{1,0:T(8,128)(2,1)S(1)}, u32[]{:S(2)}, u32[]{:S(2)}) collective-permute-start(bf16[512,384]{1,0:T(8,128)(2,1)} %c_hbm.1), channel_id=1, source_target_pairs={{0,1},{1,2},{2,3},{3,4},{4,5},{5,6},{6,7},{7,0},{8,15},{9,8},{10,9... | collective-permute-start | bytes 1179656 | tf_op jit(solution)/shard_map/ppermute | solution.py:422
  7.8 9.1 %collective-permute-start.2 = (bf16[512,384]{1,0:T(8,128)(2,1)S(1)}, bf16[512,384]{1,0:T(8,128)(2,1)S(1)}, u32[]{:S(2)}, u32[]{:S(2)}) collective-permute-start(bf16[512,384]{1,0:T(8,128)(2,1)S(1)} %collective-permute-done.1), channel_id=1, source_target_pairs={{0,1},{1,2},{2,3},{3,4},{4,5},{5,6},{6,7},{7,0},{8,15},{9,8},{10,9... | collective-permute-start | bytes 1179656 | tf_op jit(solution)/shard_map/ppermute | solution.py:422
  11.2 4.6 %collective-permute-start = (f32[520,128]{1,0:T(8,128)S(1)}, f32[520,128]{1,0:T(8,128)S(1)}, u32[]{:S(2)}, u32[]{:S(2)}) collective-permute-start(f32[520,128]{1,0:T(8,128)S(1)} %get-tuple-element.37.key_ref), channel_id=1, source_target_pairs={{0,8},{8,0},{16,24},{24,16},{32,40},{40,32},{48,56},{56,48},{64,72... | collective-permute-start | bytes 798728 | tf_op jit(solution)/shard_map/ppermute | solution.py:429
  12.8 11.0 %collective-permute-start.9 = (bf16[512,384]{1,0:T(8,128)(2,1)S(1)}, bf16[512,384]{1,0:T(8,128)(2,1)S(1)}, u32[]{:S(2)}, u32[]{:S(2)}) collective-permute-start(bf16[512,384]{1,0:T(8,128)(2,1)S(1)} %collective-permute-done.6.a1), channel_id=1, source_target_pairs={{0,1},{1,2},{2,3},{3,4},{4,5},{5,6},{6,7},{7,0},{8,15},{9,8},{10,9... | collective-permute-start | bytes 1179656 | tf_op jit(solution)/shard_map/ppermute | solution.py:422
  17.0 8.3 %collective-permute-start.7 = (bf16[512,384]{1,0:T(8,128)(2,1)S(1)}, bf16[512,384]{1,0:T(8,128)(2,1)S(1)}, u32[]{:S(2)}, u32[]{:S(2)}) collective-permute-start(bf16[512,384]{1,0:T(8,128)(2,1)S(1)} %get-tuple-element.41.x_ref), channel_id=1, source_target_pairs={{0,1},{1,2},{2,3},{3,4},{4,5},{5,6},{6,7},{7,0},{8,15},{9,8},{10,9... | collective-permute-start | bytes 1179656 | tf_op jit(solution)/shard_map/ppermute | solution.py:422
  20.2 7.4 %collective-permute-start.5 = (bf16[272,128]{1,0:T(8,128)(2,1)S(1)}, bf16[272,128]{1,0:T(8,128)(2,1)S(1)}, u32[]{:S(2)}, u32[]{:S(2)}) collective-permute-start(bf16[272,128]{1,0:T(8,128)(2,1)S(1)} %get-tuple-element.38.sent_ref), channel_id=1, source_target_pairs={{0,32},{8,40},{16,48},{24,56},{32,0},{40,8},{48,16},{56,24},{64,96... | collective-permute-start | bytes 208904 | tf_op jit(solution)/shard_map/ppermute | solution.py:429
  23.0 4.8 %collective-permute-start.4 = (bf16[272,128]{1,0:T(8,128)(2,1)S(1)}, bf16[272,128]{1,0:T(8,128)(2,1)S(1)}, u32[]{:S(2)}, u32[]{:S(2)}) collective-permute-start(bf16[272,128]{1,0:T(8,128)(2,1)S(1)} %get-tuple-element.38.sent_ref), channel_id=1, source_target_pairs={{0,48},{8,56},{16,32},{24,40},{32,16},{40,24},{48,0},{56,8},{64,11... | collective-permute-start | bytes 208904 | tf_op jit(solution)/shard_map/ppermute | solution.py:429
  23.8 3.9 %collective-permute-start.3 = (bf16[272,128]{1,0:T(8,128)(2,1)S(1)}, bf16[272,128]{1,0:T(8,128)(2,1)S(1)}, u32[]{:S(2)}, u32[]{:S(2)}) collective-permute-start(bf16[272,128]{1,0:T(8,128)(2,1)S(1)} %get-tuple-element.38.sent_ref), channel_id=1, source_target_pairs={{0,16},{8,24},{16,0},{24,8},{32,48},{40,56},{48,32},{56,40},{64,80... | collective-permute-start | bytes 208904 | tf_op jit(solution)/shard_map/ppermute | solution.py:429
  23.8 6.9 %collective-permute-start.11 = (bf16[512,384]{1,0:T(8,128)(2,1)S(1)}, bf16[512,384]{1,0:T(8,128)(2,1)S(1)}, u32[]{:S(2)}, u32[]{:S(2)}) collective-permute-start(bf16[512,384]{1,0:T(8,128)(2,1)S(1)} %collective-permute-done.9.a2), channel_id=1, source_target_pairs={{0,1},{1,2},{2,3},{3,4},{4,5},{5,6},{6,7},{7,0},{8,15},{9,8},{10,9... | collective-permute-start | bytes 1179656 | tf_op jit(solution)/shard_map/ppermute | solution.py:422
  25.4 7.3 %collective-permute-start.8 = (bf16[512,384]{1,0:T(8,128)(2,1)S(1)}, bf16[512,384]{1,0:T(8,128)(2,1)S(1)}, u32[]{:S(2)}, u32[]{:S(2)}) collective-permute-start(bf16[512,384]{1,0:T(8,128)(2,1)S(1)} %shard_map.88), channel_id=1, source_target_pairs={{0,8},{8,0},{16,24},{24,16},{32,40},{40,32},{48,56},{56,48},{64,72... | collective-permute-start | bytes 1179656 | tf_op jit(solution)/shard_map/ppermute | solution.py:429
  27.6 5.1 %collective-permute-start.10 = (bf16[512,384]{1,0:T(8,128)(2,1)S(1)}, bf16[512,384]{1,0:T(8,128)(2,1)S(1)}, u32[]{:S(2)}, u32[]{:S(2)}) collective-permute-start(bf16[512,384]{1,0:T(8,128)(2,1)S(1)} %collective-permute-done.7.refs_0_.x_ref), channel_id=1, source_target_pairs={{0,8},{8,0},{16,24},{24,16},{32,40},{40,32},{48,56},{56,48},{64,72... | collective-permute-start | bytes 1179656 | tf_op jit(solution)/shard_map/ppermute | solution.py:429
  27.8 9.0 %collective-permute-start.13 = (bf16[512,384]{1,0:T(8,128)(2,1)S(1)}, bf16[512,384]{1,0:T(8,128)(2,1)S(1)}, u32[]{:S(2)}, u32[]{:S(2)}) collective-permute-start(bf16[512,384]{1,0:T(8,128)(2,1)S(1)} %shard_map.90), channel_id=1, source_target_pairs={{0,1},{1,2},{2,3},{3,4},{4,5},{5,6},{6,7},{7,0},{8,15},{9,8},{10,9... | collective-permute-start | bytes 1179656 | tf_op jit(solution)/shard_map/ppermute | solution.py:422
  30.7 8.4 %collective-permute-start.12 = (bf16[512,384]{1,0:T(8,128)(2,1)S(1)}, bf16[512,384]{1,0:T(8,128)(2,1)S(1)}, u32[]{:S(2)}, u32[]{:S(2)}) collective-permute-start(bf16[512,384]{1,0:T(8,128)(2,1)S(1)} %collective-permute-done.11.a3), channel_id=1, source_target_pairs={{0,1},{1,2},{2,3},{3,4},{4,5},{5,6},{6,7},{7,0},{8,15},{9,8},{10,9... | collective-permute-start | bytes 1179656 | tf_op jit(solution)/shard_map/ppermute | solution.py:422
  36.8 11.6 %copy-start = (bf16[512,512]{1,0:T(8,128)(2,1)S(1)}, bf16[512,512]{1,0:T(8,128)(2,1)}, u32[]{:S(2)}) copy-start(bf16[512,512]{1,0:T(8,128)(2,1)} %refs_4_.3) | copy-start | bytes 1572868
  36.8 11.6 %copy-start.1 = (bf16[512,512]{1,0:T(8,128)(2,1)S(1)}, bf16[512,512]{1,0:T(8,128)(2,1)}, u32[]{:S(2)}) copy-start(bf16[512,512]{1,0:T(8,128)(2,1)} %refs_5_.3) | copy-start | bytes 1572868
  36.8 11.6 %copy-start.2 = (bf16[512,512]{1,0:T(8,128)(2,1)S(1)}, bf16[512,512]{1,0:T(8,128)(2,1)}, u32[]{:S(2)}) copy-start(bf16[512,512]{1,0:T(8,128)(2,1)} %q_ref.3) | copy-start | bytes 1572868
  36.9 2.3 %collective-permute-start.14 = (bf16[512,384]{1,0:T(8,128)(2,1)S(1)}, bf16[512,384]{1,0:T(8,128)(2,1)S(1)}, u32[]{:S(2)}, u32[]{:S(2)}) collective-permute-start(bf16[512,384]{1,0:T(8,128)(2,1)S(1)} %shard_map.91), channel_id=1, source_target_pairs={{0,8},{8,0},{16,24},{24,16},{32,40},{40,32},{48,56},{56,48},{64,72... | collective-permute-start | bytes 1179656 | tf_op jit(solution)/shard_map/ppermute | solution.py:429
  40.4 3.4 %collective-permute-start.15 = (f32[256,128]{1,0:T(8,128)S(1)}, f32[256,128]{1,0:T(8,128)S(1)}, u32[]{:S(2)}, u32[]{:S(2)}) collective-permute-start(f32[256,128]{1,0:T(8,128)S(1)} %get-tuple-element.47), channel_id=1, source_target_pairs={{0,8},{8,0},{16,24},{24,16},{32,40},{40,32},{48,56},{56,48},{64,72... | collective-permute-start | bytes 393224 | tf_op jit(solution)/shard_map/ppermute | solution.py:429
  43.8 6.7 %collective-permute-start.18 = (bf16[256,128]{1,0:T(8,128)(2,1)S(1)}, bf16[256,128]{1,0:T(8,128)(2,1)S(1)}, u32[]{:S(2)}, u32[]{:S(2)}) collective-permute-start(bf16[256,128]{1,0:T(8,128)(2,1)S(1)} %get-tuple-element.49), channel_id=1, source_target_pairs={{0,32},{8,40},{16,48},{24,56},{32,0},{40,8},{48,16},{56,24},{64,96... | collective-permute-start | bytes 196616 | tf_op jit(solution)/shard_map/ppermute | solution.py:429
  46.6 4.3 %collective-permute-start.17 = (bf16[256,128]{1,0:T(8,128)(2,1)S(1)}, bf16[256,128]{1,0:T(8,128)(2,1)S(1)}, u32[]{:S(2)}, u32[]{:S(2)}) collective-permute-start(bf16[256,128]{1,0:T(8,128)(2,1)S(1)} %get-tuple-element.49), channel_id=1, source_target_pairs={{0,48},{8,56},{16,32},{24,40},{32,16},{40,24},{48,0},{56,8},{64,11... | collective-permute-start | bytes 196616 | tf_op jit(solution)/shard_map/ppermute | solution.py:429
  47.5 3.5 %collective-permute-start.16 = (bf16[256,128]{1,0:T(8,128)(2,1)S(1)}, bf16[256,128]{1,0:T(8,128)(2,1)S(1)}, u32[]{:S(2)}, u32[]{:S(2)}) collective-permute-start(bf16[256,128]{1,0:T(8,128)(2,1)S(1)} %get-tuple-element.49), channel_id=1, source_target_pairs={{0,16},{8,24},{16,0},{24,8},{32,48},{40,56},{48,32},{56,40},{64,80... | collective-permute-start | bytes 196616 | tf_op jit(solution)/shard_map/ppermute | solution.py:429
  47.5 7.3 %collective-permute-start.22 = (f32[256,128]{1,0:T(8,128)S(1)}, f32[256,128]{1,0:T(8,128)S(1)}, u32[]{:S(2)}, u32[]{:S(2)}) collective-permute-start(f32[256,128]{1,0:T(8,128)S(1)} %get-tuple-element.46.grad_ref), channel_id=1, source_target_pairs={{0,8},{8,0},{16,24},{24,16},{32,40},{40,32},{48,56},{56,48},{64,72... | collective-permute-start | bytes 393224 | tf_op jit(solution)/shard_map/ppermute | solution.py:429
  51.0 5.8 %collective-permute-start.19 = (bf16[272,128]{1,0:T(8,128)(2,1)S(1)}, bf16[272,128]{1,0:T(8,128)(2,1)S(1)}, u32[]{:S(2)}, u32[]{:S(2)}) collective-permute-start(bf16[272,128]{1,0:T(8,128)(2,1)S(1)} %get-tuple-element.57), channel_id=1, source_target_pairs={{0,128},{8,136},{16,144},{24,152},{32,160},{40,168},{48,176},{56,1... | collective-permute-start | bytes 208904 | tf_op jit(solution)/shard_map/ppermute | solution.py:429
  54.0 3.2 %collective-permute-start.20 = (bf16[272,128]{1,0:T(8,128)(2,1)S(1)}, bf16[272,128]{1,0:T(8,128)(2,1)S(1)}, u32[]{:S(2)}, u32[]{:S(2)}) collective-permute-start(bf16[272,128]{1,0:T(8,128)(2,1)S(1)} %get-tuple-element.58), channel_id=1, source_target_pairs={{0,64},{8,72},{16,80},{24,88},{32,96},{40,104},{48,112},{56,120},{... | collective-permute-start | bytes 208904 | tf_op jit(solution)/shard_map/ppermute | solution.py:429
  54.4 4.7 %collective-permute-start.21 = (bf16[272,128]{1,0:T(8,128)(2,1)S(1)}, bf16[272,128]{1,0:T(8,128)(2,1)S(1)}, u32[]{:S(2)}, u32[]{:S(2)}) collective-permute-start(bf16[272,128]{1,0:T(8,128)(2,1)S(1)} %get-tuple-element.59), channel_id=1, source_target_pairs={{0,192},{8,200},{16,208},{24,216},{32,224},{40,232},{48,240},{56,2... | collective-permute-start | bytes 208904 | tf_op jit(solution)/shard_map/ppermute | solution.py:429
  59.2 4.4 %collective-permute-start.23 = (f32[512,128]{1,0:T(8,128)S(1)}, f32[512,128]{1,0:T(8,128)S(1)}, u32[]{:S(2)}, u32[]{:S(2)}) collective-permute-start(f32[512,128]{1,0:T(8,128)S(1)} %shard_map.97.refs_0_), channel_id=1, source_target_pairs={{0,8},{8,0},{16,24},{24,16},{32,40},{40,32},{48,56},{56,48},{64,72... | collective-permute-start | bytes 786440 | tf_op jit(solution)/shard_map/ppermute | solution.py:429
